TPU v7x, 256 devices: a whole 4x4x8 slice. The times are simulated.
256 devices in a mesh: img: 64 (over z, y, core), tok: 4 (over x).
Axes of the slice: x: 4, y: 4, z: 8, core: 2. Of those that a mesh axis runs over, the one named last changes fastest.
Arguments:
- tokens: bfloat16 [2048, 128, 1024], P('img', 'tok'), may hold values from -6 to 6
- embed: bfloat16 [1024, 768], replicated, may hold values from -0.1875 to 0.1875
- norm_gain: float32 [768], replicated, may hold values from 0.1 to 1.9
- pairs: int32 [2048, 2], P('img'), may hold values from 0 to 2047, as said below
- wq_first: bfloat16 [768, 768], replicated, may hold values from -0.21875 to 0.21875
- wkv_first: bfloat16 [768, 1536], replicated, may hold values from -0.21875 to 0.21875
- wq_second: bfloat16 [768, 768], replicated, may hold values from -0.21875 to 0.21875
- wkv_second: bfloat16 [768, 1536], replicated, may hold values from -0.21875 to 0.21875
Outputs:
- joined: bfloat16 [2048, 128, 768], P('img', 'tok')
Inputs may be any that keep to these rules, and one draw needn't show every extreme that they name: `pairs`: the first image of every row lies among the 32 images owned by the img index that holds the row (images are owned in contiguous runs of 32); the two images of a row differ; among the rows of one img index at most 2 second images share an owner, and exactly 2 do for one owner on every index.
All inputs are finite; a program needn't handle non-finite values.
Results may differ from a plain program's by a relative error of at most 0.0051.
Values may be sent and summed in bfloat16 or wider, within the bound.
No kernel may reach another device: no remote copies, remote signals or barrier semaphores. Data moves between devices by JAX's collectives and lax.ppermute only.
A program may use at most 128 MiB of HBM per device.

v0:
```python
import jax
import jax.numpy as jnp
from jax import lax
from jax.sharding import PartitionSpec as P

HEADS = 12


def layer_norm(values, norm_gain):
    centred = values - jnp.mean(values, axis=-1, keepdims=True)
    spread = jnp.mean(centred * centred, axis=-1, keepdims=True)
    return centred * lax.rsqrt(spread + 1e-06) * norm_gain


def project(inputs, weight):
    flat = inputs.reshape(-1, inputs.shape[-1])
    result = jnp.dot(flat, weight, preferred_element_type=jnp.float32).astype(jnp.bfloat16)
    return result.reshape(inputs.shape[0], inputs.shape[1], weight.shape[1])


def attend(queries, keyvals, head_count):
    batch, rows, width = queries.shape
    head_size = width // head_count
    keys = keyvals[:, :, :width].reshape(batch, -1, head_count, head_size)
    values = keyvals[:, :, width:].reshape(batch, -1, head_count, head_size)
    query_heads = queries.reshape(batch, rows, head_count, head_size)
    scores = jnp.einsum("pqhe,pkhe->phqk", query_heads, keys, preferred_element_type=jnp.float32)
    scores = scores * (1.0 / float(head_size) ** 0.5)
    scores = scores - jnp.max(scores, axis=-1, keepdims=True)
    expd = jnp.exp(scores)
    weights = (expd / jnp.sum(expd, axis=-1, keepdims=True)).astype(jnp.bfloat16)
    output = jnp.einsum("phqk,pkhe->pqhe", weights, values, preferred_element_type=jnp.float32)
    return output.reshape(batch, rows, width).astype(jnp.bfloat16)


def body(tokens, embed, norm_gain, pairs, wq_first, wkv_first, wq_second, wkv_second):
    img_count, tok_rows, enc_width = tokens.shape
    width = embed.shape[1]
    owner_count = lax.axis_size("img")
    group_size = lax.axis_size("tok")
    pair_count = pairs.shape[0]
    capacity = pair_count // owner_count + 2
    slot_count = owner_count * capacity
    device_index = lax.axis_index("img")
    row_width = tok_rows * width
    embedded = jnp.dot(tokens.reshape(-1, enc_width), embed, preferred_element_type=jnp.float32)
    normed = layer_norm(embedded, norm_gain).astype(jnp.bfloat16)
    normed_flat = normed.reshape(img_count, row_width)
    first_local = pairs[:, 0] - device_index * img_count
    second_owner = pairs[:, 1] // img_count
    second_local = pairs[:, 1] - second_owner * img_count
    positions = jnp.arange(pair_count)
    same_owner = second_owner[:, None] == second_owner[None, :]
    earlier = positions[None, :] < positions[:, None]
    rank_of = jnp.sum((same_owner & earlier).astype(jnp.int32), axis=1)
    slot_of = second_owner * capacity + rank_of
    slot_ids = jnp.arange(slot_count)
    slot_hot = slot_of[:, None] == slot_ids[None, :]
    asked_here = jnp.sum(jnp.where(slot_hot, second_local[:, None] + 1, 0), axis=0) - 1
    asked = lax.all_to_all(
        asked_here.reshape(owner_count, capacity), "img", split_axis=0, concat_axis=0, tiled=True
    )
    image_ids = jnp.arange(img_count)
    choose_hot = asked.reshape(slot_count)[:, None] == image_ids[None, :]
    outgoing = jnp.dot(
        choose_hot.astype(jnp.bfloat16), normed_flat, preferred_element_type=jnp.float32
    )
    outgoing = outgoing.astype(jnp.bfloat16).reshape(owner_count, capacity, tok_rows, width)
    fetched = lax.all_to_all(outgoing, "img", split_axis=0, concat_axis=0, tiled=True)
    first_hot = (first_local[:, None] == image_ids[None, :]).astype(jnp.bfloat16)
    first_rows = jnp.dot(first_hot, normed_flat, preferred_element_type=jnp.float32)
    first_rows = first_rows.astype(jnp.bfloat16).reshape(pair_count, tok_rows, width)
    second_rows = jnp.dot(
        slot_hot.astype(jnp.bfloat16),
        fetched.reshape(slot_count, row_width),
        preferred_element_type=jnp.float32,
    )
    second_rows = second_rows.astype(jnp.bfloat16).reshape(pair_count, tok_rows, width)
    per_group = pair_count // group_size
    grouped_first = first_rows.reshape(group_size, per_group, tok_rows, width)
    grouped_second = second_rows.reshape(group_size, per_group, tok_rows, width)
    first_whole = lax.all_to_all(grouped_first, "tok", split_axis=0, concat_axis=2, tiled=True)
    second_whole = lax.all_to_all(grouped_second, "tok", split_axis=0, concat_axis=2, tiled=True)
    items = first_whole.shape[1]
    first_whole = first_whole.reshape(items, -1, width)
    second_whole = second_whole.reshape(items, -1, width)
    out_first = attend(project(first_whole, wq_first), project(second_whole, wkv_first), HEADS)
    out_second = attend(project(second_whole, wq_second), project(first_whole, wkv_second), HEADS)
    out_first = out_first.reshape(1, items, -1, width)
    out_second = out_second.reshape(1, items, -1, width)
    cross_first = lax.all_to_all(out_first, "tok", split_axis=2, concat_axis=0, tiled=True)
    cross_second = lax.all_to_all(out_second, "tok", split_axis=2, concat_axis=0, tiled=True)
    cross_first = cross_first.reshape(pair_count, tok_rows, width)
    cross_second = cross_second.reshape(pair_count, tok_rows, width)
    slot_hot_back = (slot_ids[:, None] == slot_of[None, :]).astype(jnp.bfloat16)
    back_rows = jnp.dot(
        slot_hot_back,
        cross_second.reshape(pair_count, row_width),
        preferred_element_type=jnp.float32,
    )
    back_rows = back_rows.astype(jnp.bfloat16).reshape(owner_count, capacity, tok_rows, width)
    returned = lax.all_to_all(back_rows, "img", split_axis=0, concat_axis=0, tiled=True)
    local_hot = image_ids[:, None] == first_local[None, :]
    owner_hot = image_ids[:, None] == asked.reshape(slot_count)[None, :]
    update = jnp.dot(
        local_hot.astype(jnp.bfloat16),
        cross_first.reshape(pair_count, row_width),
        preferred_element_type=jnp.float32,
    )
    update = update + jnp.dot(
        owner_hot.astype(jnp.bfloat16),
        returned.reshape(slot_count, row_width),
        preferred_element_type=jnp.float32,
    )
    count = jnp.sum(local_hot.astype(jnp.float32), axis=1) + jnp.sum(
        owner_hot.astype(jnp.float32), axis=1
    )
    joined = update / jnp.maximum(count, 1.0)[:, None] + normed_flat.astype(jnp.float32)
    return joined.reshape(img_count, tok_rows, width).astype(jnp.bfloat16)


def solution(mesh):
    in_specs = (P("img", "tok", None), P(), P(), P("img", None), P(), P(), P(), P())
    out_specs = P("img", "tok", None)
    return jax.shard_map(body, mesh=mesh, in_specs=in_specs, out_specs=out_specs, check_vma=False)
```

profile of v0, /device:TPU:1, one launch (start us, length us, event | category | flops | bytes accessed | tf_op | source)
XLA Modules:
  0.0 480.7 jit_solution(14416216609481865962)
XLA Ops:
  2.6 13.2 %all-to-all-start = ((s32[64,1,2]{2,1,0:T(1,128)}), s32[64,1,2]{2,1,0:T(1,128)S(1)}, u32[]{:S(2)}, u32[]{:S(2)}) async-start(s32[64,1,2]{2,1,0:T(1,128)} %bitcast.6), calls=%async_computation | async-start | bytes 65536 | tf_op jit(solution)/shard_map/all_to_all | solution.py:60
  15.8 3.9 fusion.34
  22.0 2.6 copy.57
  24.6 2.7 reshape.162
  30.8 4.3 all-to-all-start.3
  36.7 3.2 convolution_convert_fusion.1
  39.9 4.5 copy.80
  44.4 11.2 %all-to-all-done.3 = bf16[4,8,32,768]{3,2,1,0:T(8,128)(2,1)} async-done(((bf16[4,8,32,768]{3,2,1,0:T(8,128)(2,1)}), bf16[4,8,32,768]{3,2,1,0:T(8,128)(2,1)}, u32[]{:S(2)}, u32[]{:S(2)}) %all-to-all-start.3) | async-done | bytes 1572896 | tf_op jit(solution)/shard_map/all_to_all | solution.py:82
  55.6 11.9 %all-to-all-start.1 = ((bf16[64,2,32,768]{3,2,1,0:T(8,128)(2,1)}), bf16[64,2,32,768]{3,2,1,0:T(8,128)(2,1)}, u32[]{:S(2)}, u32[]{:S(2)}) async-start(bf16[64,2,32,768]{3,2,1,0:T(8,128)(2,1)} %bitcast.110), calls=%async_computation.1 | async-start | bytes 12582912 | tf_op jit(solution)/shard_map/all_to_all | solution.py:69
  67.5 2.7 copy.62
  70.2 135.8 %all-to-all-done.1 = bf16[64,2,32,768]{3,2,1,0:T(8,128)(2,1)} async-done(((bf16[64,2,32,768]{3,2,1,0:T(8,128)(2,1)}), bf16[64,2,32,768]{3,2,1,0:T(8,128)(2,1)}, u32[]{:S(2)}, u32[]{:S(2)}) %all-to-all-start.1) | async-done | bytes 6291488 | tf_op jit(solution)/shard_map/all_to_all | solution.py:69
  206.0 7.0 %copy.81 = bf16[16,8,32,768]{3,1,2,0:T(8,128)(2,1)S(1)} copy(bf16[16,8,32,768]{3,2,1,0:T(8,128)(2,1)} %bitcast.42) | data formatting | bytes 12582912
  215.5 4.9 %all-to-all-start.2 = ((bf16[4,8,32,768]{3,2,1,0:T(8,128)(2,1)}), bf16[4,8,32,768]{3,2,1,0:T(8,128)(2,1)}, u32[]{:S(2)}, u32[]{:S(2)}) async-start(bf16[4,8,32,768]{3,2,1,0:T(8,128)(2,1)} %copy.58), calls=%async_computation.2 | async-start | bytes 3145728 | tf_op jit(solution)/shard_map/all_to_all | solution.py:83
  220.4 4.3 convolution_convert_fusion.7
  227.3 3.1 copy.82
  230.4 2.8 convolution_convert_fusion.4
  240.4 2.8 convolution_convert_fusion.5
  245.3 2.6 copy.60
  247.9 2.6 copy.64
  250.5 4.4 convolution_convert_fusion.6
  260.4 5.9 %fusion.36 = (f32[8,12,128]{2,1,0:T(8,128)S(1)}, f32[8,12,128,128]{2,3,1,0:T(8,128)S(1)}) fusion(f32[8,12,128,128]{2,3,1,0:T(8,128)S(1)} %fusion.17), kind=kOutput, calls=%fused_computation.79 | output fusion | flops 6291583 | bytes 12632064 | tf_op jit(solution)/shard_map/sub | solution.py:29
  268.5 2.9 copy.75
  271.4 4.7 all-to-all-start.5
  278.6 5.9 %fusion.35 = (f32[8,12,128]{2,1,0:T(8,128)S(1)}, f32[8,12,128,128]{2,3,1,0:T(8,128)S(1)}) fusion(f32[8,12,128,128]{2,3,1,0:T(8,128)S(1)} %fusion.19), kind=kOutput, calls=%fused_computation.78 | output fusion | flops 6291583 | bytes 12632064 | tf_op jit(solution)/shard_map/sub | solution.py:29
  286.7 3.0 copy.67
  289.7 3.0 all-to-all-done.5
  292.7 3.6 all-to-all-start.4
  300.8 4.5 copy.86
  305.3 6.3 %all-to-all-done.4 = bf16[1,8,128,768]{3,1,0,2:T(8,128)(2,1)S(1)} async-done(((bf16[1,8,128,768]{3,1,0,2:T(8,128)(2,1)}), bf16[1,8,128,768]{3,1,0,2:T(8,128)(2,1)S(1)}, u32[]{:S(2)}, u32[]{:S(2)}) %all-to-all-start.4) | async-done | bytes 1572896 | tf_op jit(solution)/shard_map/all_to_all | solution.py:91
  311.6 19.8 %all-to-all-start.6 = ((bf16[64,2,32,768]{3,2,1,0:T(8,128)(2,1)}), bf16[64,2,32,768]{3,2,1,0:T(8,128)(2,1)}, u32[]{:S(2)}, u32[]{:S(2)}) async-start(bf16[64,2,32,768]{3,2,1,0:T(8,128)(2,1)} %bitcast.109), calls=%async_computation.6 | async-start | bytes 12582912 | tf_op jit(solution)/shard_map/all_to_all | solution.py:102
  335.1 134.7 %all-to-all-done.6 = bf16[64,2,32,768]{3,2,1,0:T(8,128)(2,1)} async-done(((bf16[64,2,32,768]{3,2,1,0:T(8,128)(2,1)}), bf16[64,2,32,768]{3,2,1,0:T(8,128)(2,1)}, u32[]{:S(2)}, u32[]{:S(2)}) %all-to-all-start.6) | async-done | bytes 6291488 | tf_op jit(solution)/shard_map/all_to_all | solution.py:102
  469.9 7.2 %copy.87 = bf16[16,8,32,768]{3,1,2,0:T(8,128)(2,1)S(1)} copy(bf16[16,8,32,768]{3,2,1,0:T(8,128)(2,1)} %bitcast.66) | data formatting | bytes 12582912
  (70 shorter events, 48.1 us)
Async XLA Ops:
  0.0 230.4 %copy-start = (bf16[768,1536]{1,0:T(8,128)(2,1)S(1)}, bf16[768,1536]{1,0:T(8,128)(2,1)}, u32[]{:S(2)}) copy-start(bf16[768,1536]{1,0:T(8,128)(2,1)} %param.15) | copy-start | bytes 7077892
  2.6 28.2 %all-to-all-start = ((s32[64,1,2]{2,1,0:T(1,128)}), s32[64,1,2]{2,1,0:T(1,128)S(1)}, u32[]{:S(2)}, u32[]{:S(2)}) async-start(s32[64,1,2]{2,1,0:T(1,128)} %bitcast.6), calls=%async_computation | async-start | bytes 65536 | tf_op jit(solution)/shard_map/all_to_all | solution.py:60
  19.7 0.7 copy-start.9
  30.8 24.8 %all-to-all-start.3 = ((bf16[4,8,32,768]{3,2,1,0:T(8,128)(2,1)}), bf16[4,8,32,768]{3,2,1,0:T(8,128)(2,1)}, u32[]{:S(2)}, u32[]{:S(2)}) async-start(bf16[4,8,32,768]{3,2,1,0:T(8,128)(2,1)} %copy.61), calls=%async_computation.3 | async-start | bytes 3145728 | tf_op jit(solution)/shard_map/all_to_all | solution.py:82
  55.6 150.4 %all-to-all-start.1 = ((bf16[64,2,32,768]{3,2,1,0:T(8,128)(2,1)}), bf16[64,2,32,768]{3,2,1,0:T(8,128)(2,1)}, u32[]{:S(2)}, u32[]{:S(2)}) async-start(bf16[64,2,32,768]{3,2,1,0:T(8,128)(2,1)} %bitcast.110), calls=%async_computation.1 | async-start | bytes 12582912 | tf_op jit(solution)/shard_map/all_to_all | solution.py:69
  215.5 22.7 %all-to-all-start.2 = ((bf16[4,8,32,768]{3,2,1,0:T(8,128)(2,1)}), bf16[4,8,32,768]{3,2,1,0:T(8,128)(2,1)}, u32[]{:S(2)}, u32[]{:S(2)}) async-start(bf16[4,8,32,768]{3,2,1,0:T(8,128)(2,1)} %copy.58), calls=%async_computation.2 | async-start | bytes 3145728 | tf_op jit(solution)/shard_map/all_to_all | solution.py:83
  227.3 3.1 copy-start.7
  238.2 2.1 copy-start.11
  239.9 3.3 copy-start.8
  260.4 5.9 %copy-start.6 = (bf16[8,128,768]{1,2,0:T(8,128)(2,1)S(1)}, bf16[8,128,768]{1,2,0:T(8,128)(2,1)}, u32[]{:S(2)}) copy-start(bf16[8,128,768]{1,2,0:T(8,128)(2,1)} %copy.70) | copy-start | bytes 4718596
  271.4 4.7 copy-start.3
  271.4 21.3 %all-to-all-start.5 = ((bf16[1,8,128,768]{3,1,0,2:T(8,128)(2,1)}), bf16[1,8,128,768]{3,1,0,2:T(8,128)(2,1)}, u32[]{:S(2)}, u32[]{:S(2)}) async-start(bf16[1,8,128,768]{3,1,0,2:T(8,128)(2,1)} %copy.75), calls=%async_computation.5 | async-start | bytes 3145728 | tf_op jit(solution)/shard_map/all_to_all | solution.py:92
  278.6 5.9 %copy-start.5 = (bf16[8,128,768]{1,2,0:T(8,128)(2,1)S(1)}, bf16[8,128,768]{1,2,0:T(8,128)(2,1)}, u32[]{:S(2)}) copy-start(bf16[8,128,768]{1,2,0:T(8,128)(2,1)} %copy.60) | copy-start | bytes 4718596
  289.7 6.6 %copy-start.10 = (s32[32,2]{0,1:T(2,128)S(1)}, s32[32,2]{0,1:T(2,128)}, u32[]{:S(2)}) copy-start(s32[32,2]{0,1:T(2,128)} %param.11) | copy-start | bytes 772
  292.7 18.9 %all-to-all-start.4 = ((bf16[1,8,128,768]{3,1,0,2:T(8,128)(2,1)}), bf16[1,8,128,768]{3,1,0,2:T(8,128)(2,1)S(1)}, u32[]{:S(2)}, u32[]{:S(2)}) async-start(bf16[1,8,128,768]{3,1,0,2:T(8,128)(2,1)} %copy.67), calls=%async_computation.4 | async-start | bytes 3145728 | tf_op jit(solution)/shard_map/all_to_all | solution.py:91
  311.6 158.3 %all-to-all-start.6 = ((bf16[64,2,32,768]{3,2,1,0:T(8,128)(2,1)}), bf16[64,2,32,768]{3,2,1,0:T(8,128)(2,1)}, u32[]{:S(2)}, u32[]{:S(2)}) async-start(bf16[64,2,32,768]{3,2,1,0:T(8,128)(2,1)} %bitcast.109), calls=%async_computation.6 | async-start | bytes 12582912 | tf_op jit(solution)/shard_map/all_to_all | solution.py:102
  469.9 7.2 %copy-start.2 = (bf16[32,24576]{1,0:T(8,128)(2,1)S(1)}, bf16[32,24576]{1,0:T(8,128)(2,1)}, u32[]{:S(2)}) copy-start(bf16[32,24576]{1,0:T(8,128)(2,1)} %reshape.162) | copy-start | bytes 4718596
  469.9 7.2 %copy-start.4 = (f32[32,24576]{1,0:T(8,128)S(1)}, f32[32,24576]{1,0:T(8,128)}, u32[]{:S(2)}) copy-start(f32[32,24576]{1,0:T(8,128)} %fusion.23) | copy-start | bytes 9437188
  478.2 2.2 copy-start.1
where the time goes:
time: 490 us; the launch traced here: 481 us
  waiting for transfers between devices  291 us (59%)
  local copies, waits for them, and re-layouts  72.7 us (15%)
  starting transfers between devices  62.2 us (13%)
  matrix products  37.5 us (8%)
  other arithmetic  16.7 us (3%)
    all_to_all x1, waiting for transfers between devices, body(): lax.all_to_all(outgoing, 'img', split_axis=0, concat_axis=0, tiled=True)  136 us
    all_to_all x1, waiting for transfers between devices, body(): lax.all_to_all(back_rows, 'img', split_axis=0, concat_axis=0, tiled=True)  135 us
    unnamed x33, local copies, waits for them, and re-layouts  32.9 us
    all_to_all x1, starting transfers between devices, body(): lax.all_to_all(back_rows, 'img', split_axis=0, concat_axis=0, tiled=True)  19.8 us
    dot_general x4, matrix products, project(): jnp.dot(flat, weight, preferred_element_type=jnp.float32)  14.3 us
    all_to_all x1, starting transfers between devices, body(): lax.all_to_all(asked_here.reshape(owner_count, capacity), 'img', split_ax...  13.2 us
    all_to_all x1, starting transfers between devices, body(): lax.all_to_all(outgoing, 'img', split_axis=0, concat_axis=0, tiled=True)  11.9 us
    sub x2, other arithmetic, attend(): scores = scores - jnp.max(scores, axis=-1, keepdims=True)  11.8 us
  transfers between devices with their start and end apart: 7, of which 5 were waited for; matrix products, arithmetic and copies ran while one was open for 15% of the time, Pallas kernels for 0%

commit v1 on v0

v1 whole, which is shorter than its diff:
```python
import functools

import jax
import jax.numpy as jnp
from jax import lax
from jax.experimental import pallas as pl
from jax.experimental.pallas import tpu as pltpu
from jax.sharding import PartitionSpec as P

HEAD = 64
VMEM_LIMIT = 56 * 1024 * 1024
F32 = jnp.float32
BF16 = jnp.bfloat16


def call(kernel, out_shape, flops, nbytes, **kwargs):
    return pl.pallas_call(
        kernel,
        out_shape=out_shape,
        compiler_params=pltpu.CompilerParams(vmem_limit_bytes=VMEM_LIMIT),
        cost_estimate=pl.CostEstimate(flops=flops, bytes_accessed=nbytes, transcendentals=0),
        **kwargs,
    )


def whole(*shape):
    return pl.BlockSpec(shape, lambda *_: (0,) * len(shape))


def embed_kernel(first_ref, tok_ref, x_ref, w_ref, gain_ref, normed_ref, pieces_ref, f0, f1, f2, f3, scratch):
    step = pl.program_id(0)
    rows = x_ref.shape[0]
    width = w_ref.shape[1]
    half = width // 2
    e = jnp.dot(x_ref[...], w_ref[...], preferred_element_type=F32)
    c = e - jnp.mean(e, axis=-1, keepdims=True)
    spread = jnp.mean(c * c, axis=-1, keepdims=True)
    n = c * lax.rsqrt(spread + 1e-06) * gain_ref[...]
    normed_ref[...] = n.astype(BF16)
    lane_blocks = width // 128
    start = pl.multiple_of(step * rows, rows)
    for b in range(lane_blocks):
        scratch[b, pl.ds(start, rows), :] = n[:, b * 128:(b + 1) * 128]

    @pl.when(step == pl.num_programs(0) - 1)
    def _():
        images = pieces_ref.shape[1]
        toks = scratch.shape[1] // images
        for r in range(toks):
            for b in range(lane_blocks):
                v = scratch[b, pl.ds(r, images, stride=toks), :].astype(BF16)
                h, at = divmod(b * 128, half)
                pieces_ref[h * toks + r, :, at:at + 128] = v
        group = tok_ref[0]
        for k, f in enumerate((f0, f1, f2, f3)):
            items = f.shape[0]
            for j in range(items):
                p = first_ref[lax.rem(group + k, 4) * items + j]
                at = pl.multiple_of(p * toks, toks)
                for b in range(lane_blocks):
                    f[j, :, b * 128:(b + 1) * 128] = scratch[b, pl.ds(at, toks), :].astype(BF16)


def pick_kernel(ids_ref, table_ref, out_ref):
    rows = ids_ref.shape[0]
    count = table_ref.shape[0]
    ids = ids_ref[...]
    lane = lax.broadcasted_iota(jnp.int32, (rows, 128), 1)
    hot = [(ids - b * 128 == lane).astype(F32).astype(BF16) for b in range(count // 128)]
    hot = jnp.concatenate(hot, axis=1)
    out_ref[...] = jnp.dot(hot, table_ref[...], preferred_element_type=F32).astype(BF16)


def sum_kernel(ids_ref, rows_ref, out_ref):
    step = pl.program_id(0)
    images = out_ref.shape[0]
    image = lax.broadcasted_iota(jnp.int32, (images, ids_ref.shape[1]), 0) + step * images
    hot = (ids_ref[...] == image).astype(F32).astype(BF16)
    out_ref[...] = jnp.dot(hot, rows_ref[...], preferred_element_type=F32).astype(BF16)


def first_kernel(f0, f1, f2, f3, wq_ref, wkv_ref, q_ref, kv_ref):
    for k, f in enumerate((f0, f1, f2, f3)):
        items, toks, width = f.shape
        x = f[...].reshape(items * toks, width)
        q = jnp.dot(x, wq_ref[...], preferred_element_type=F32).astype(BF16)
        q_ref[:, k * toks:(k + 1) * toks, :] = q.reshape(items, toks, -1)
        kv = jnp.dot(x, wkv_ref[...], preferred_element_type=F32).astype(BF16)
        kv_ref[:, k * toks:(k + 1) * toks, :] = kv.reshape(items, toks, -1)


def masks(rows):
    lane = lax.broadcasted_iota(jnp.int32, (rows, 128), 1)
    low = lane < HEAD
    one_low = jnp.where(low, 1.0, 0.0).astype(BF16)
    one_high = jnp.where(low, 0.0, 1.0).astype(BF16)
    return low, one_low, one_high


def attend(q, k, v, low, one_low, one_high):
    rows = k.shape[0]
    zero = jnp.zeros((rows, 128), BF16)
    kk = jnp.concatenate([jnp.where(low, k, zero), jnp.where(low, zero, k)], axis=0)
    top = jnp.concatenate([jnp.where(low, v, zero), one_low], axis=1)
    bottom = jnp.concatenate([jnp.where(low, zero, v), one_high], axis=1)
    vv = jnp.concatenate([top, bottom], axis=0)
    s = lax.dot_general(q, kk, (((1,), (1,)), ((), ())), preferred_element_type=F32)
    s = s * (1.0 / HEAD ** 0.5)
    parts = []
    for part in (s[:, :rows], s[:, rows:]):
        parts.append(jnp.exp(part - jnp.max(part, axis=-1, keepdims=True)).astype(BF16))
    o = jnp.dot(jnp.concatenate(parts, axis=1), vv, preferred_element_type=F32)
    return o[:, :128] / o[:, 128:]


def decode_kernel(x_ref, q_ref, kv_ref, wq_ref, wkv_ref, g0, g1, g2, g3, back_ref, scratch, o_scr, x_scr, q_scr, kv_scr):
    step = pl.program_id(0)
    steps = pl.num_programs(0)
    lane_blocks = scratch.shape[0]
    per_half = lane_blocks // 2
    rows = scratch.shape[1]
    toks = q_ref.shape[1]

    @pl.when(step == 0)
    def _():
        for b in range(lane_blocks):
            h, at = divmod(b, per_half)
            scratch[b] = x_ref[h, :, at * 128:(at + 1) * 128].astype(F32)
        items = rows // toks
        for j in range(items):
            for b in range(lane_blocks):
                x_scr[j * toks:(j + 1) * toks, b * 128:(b + 1) * 128] = scratch[
                    b, pl.ds(j, toks, stride=items), :
                ].astype(BF16)

        @pl.loop(0, rows // 256)
        def _(i):
            at = pl.ds(pl.multiple_of(i * 256, 256), 256)
            x = x_scr[at, :]
            q_scr[at, :] = jnp.dot(x, wq_ref[...], preferred_element_type=F32).astype(BF16)
            kv_scr[at, :] = jnp.dot(x, wkv_ref[...], preferred_element_type=F32).astype(BF16)

    mine = pl.ds(pl.multiple_of(step * toks, toks), toks)

    width = lane_blocks * 128
    part = toks // 4
    masked = masks(toks)

    @pl.loop(0, lane_blocks // 2)
    def _(i):
        for u in range(2):
            h = i * 2 + u
            lo = pl.multiple_of(h * 128, 128)
            keys = pl.ds(lo, 128)
            values = pl.ds(pl.multiple_of(lo + width, 128), 128)
            o = attend(q_ref[0, :, keys], kv_scr[mine, keys], kv_scr[mine, values], *masked).astype(BF16)
            for k, g in enumerate((g0, g1, g2, g3)):
                g[0, :, keys] = o[k * part:(k + 1) * part]
            o_scr[h, mine, :] = attend(q_scr[mine, keys], kv_ref[0, :, keys], kv_ref[0, :, values], *masked)

    @pl.when(step == steps - 1)
    def _():
        for b in range(lane_blocks):
            h, at = divmod(b, per_half)
            for j in range(rows // toks):
                scratch[b, pl.ds(j, toks, stride=rows // toks), :] = o_scr[b, j * toks:(j + 1) * toks, :]
            back_ref[h, :, at * 128:(at + 1) * 128] = scratch[b].astype(BF16)


def near_kernel(first_ref, tok_ref, r0, r1, r2, r3, acc_ref):
    acc_ref[...] = jnp.zeros_like(acc_ref)
    group = tok_ref[0]
    for k, r in enumerate((r0, r1, r2, r3)):
        items = r.shape[0]

        @pl.loop(0, items)
        def _(j, r=r, k=k, items=items):
            p = first_ref[lax.rem(group + k, 4) * items + j]
            acc_ref[p] = acc_ref[p] + r[j].astype(F32)


def join_kernel(recip_ref, far_ref, acc_ref, normed_ref, out_ref, scratch):
    images, toks, width = acc_ref.shape
    half = width // 2
    lane_blocks = width // 128
    for r in range(toks):
        for b in range(lane_blocks):
            h, at = divmod(b * 128, half)
            scratch[b, pl.ds(r, images, stride=toks), :] = far_ref[h * toks + r, :, at:at + 128].astype(F32)

    @pl.loop(0, images)
    def _(i):
        recip = recip_ref[i]
        at = pl.ds(pl.multiple_of(i * toks, toks), toks)
        for b in range(lane_blocks):
            lanes = slice(b * 128, (b + 1) * 128)
            total = scratch[b, at, :] + acc_ref[i, :, lanes]
            out_ref[i, :, lanes] = (total * recip + normed_ref[at, lanes].astype(F32)).astype(BF16)


def body(tokens, embed, norm_gain, pairs, wq_first, wkv_first, wq_second, wkv_second):
    images, toks, enc = tokens.shape
    width = embed.shape[1]
    half = width // 2
    owners = lax.axis_size("img")
    groups = lax.axis_size("tok")
    count = pairs.shape[0]
    items = count // groups
    total = owners * count
    all_images = owners * images
    rows = images * toks
    img = lax.axis_index("img")
    tok = lax.axis_index("tok").astype(jnp.int32).reshape(1)
    smem = pl.BlockSpec(memory_space=pltpu.SMEM)
    vmem = pl.BlockSpec(memory_space=pltpu.VMEM)

    first_local = pairs[:, 0] - img * images
    all_pairs = lax.all_gather(pairs, "img", axis=0, tiled=True)
    second = all_pairs[:, 1]
    own_ids = img * images + jnp.arange(images)
    seen = jnp.sum((all_pairs.reshape(1, -1) == own_ids[:, None]).astype(F32), axis=1)
    recip = 1.0 / jnp.maximum(seen, 1.0)

    part = jax.ShapeDtypeStruct((items, toks, width), BF16)
    block = 256
    normed, pieces, f0, f1, f2, f3 = call(
        embed_kernel,
        [
            jax.ShapeDtypeStruct((rows, width), BF16),
            jax.ShapeDtypeStruct((owners, images, half), BF16),
            part, part, part, part,
        ],
        2 * rows * enc * width,
        2 * rows * (enc + 3 * width) + 2 * enc * width,
        grid=(rows // block,),
        in_specs=[
            smem, smem,
            pl.BlockSpec((block, enc), lambda i: (i, 0)),
            whole(enc, width),
            whole(1, width),
        ],
        out_specs=[
            pl.BlockSpec((block, width), lambda i: (i, 0)),
            whole(owners, images, half),
        ] + [whole(items, toks, width)] * 4,
        scratch_shapes=[pltpu.VMEM((width // 128, rows, 128), F32)],
        name="embed",
    )(first_local, tok, tokens.reshape(rows, enc), embed, norm_gain.reshape(1, width))

    table = lax.all_to_all(pieces, "img", split_axis=0, concat_axis=0, tiled=True)
    firsts = [f0]
    for k, f in enumerate((f1, f2, f3)):
        perm = [(t, (t + k + 1) % groups) for t in range(groups)]
        firsts.append(lax.ppermute(f, "tok", perm))

    step_rows = 256
    ids = jnp.broadcast_to(second[:, None], (total, 128))
    asked = call(
        pick_kernel,
        jax.ShapeDtypeStruct((total, half), BF16),
        2 * total * all_images * half,
        2 * (total + all_images) * half,
        grid=(total // step_rows,),
        in_specs=[
            pl.BlockSpec((step_rows, 128), lambda i: (i, 0)),
            whole(all_images, half),
        ],
        out_specs=pl.BlockSpec((step_rows, half), lambda i: (i, 0)),
        name="pick",
    )(ids, table.reshape(all_images, half))
    seconds = lax.all_to_all(
        asked.reshape(owners * groups, items, half), ("img", "tok"), split_axis=0, concat_axis=0, tiled=True
    )

    whole_toks = toks * groups
    q_first, kv_second = call(
        first_kernel,
        [
            jax.ShapeDtypeStruct((items, whole_toks, width), BF16),
            jax.ShapeDtypeStruct((items, whole_toks, 2 * width), BF16),
        ],
        2 * items * whole_toks * width * 3 * width,
        2 * items * whole_toks * width * 4 + 6 * width * width,
        in_specs=[vmem] * 6,
        out_specs=[vmem] * 2,
        name="first",
    )(*firsts, wq_first, wkv_second)

    pair_rows = items * whole_toks
    g0, g1, g2, g3, back = call(
        decode_kernel,
        [part, part, part, part, jax.ShapeDtypeStruct((2, pair_rows, half), BF16)],
        2 * pair_rows * width * 3 * width + 16 * pair_rows * whole_toks * width,
        2 * pair_rows * width * 6 + 6 * width * width,
        grid=(items,),
        in_specs=[
            whole(2, pair_rows, half),
            pl.BlockSpec((1, whole_toks, width), lambda j: (j, 0, 0)),
            pl.BlockSpec((1, whole_toks, 2 * width), lambda j: (j, 0, 0)),
            whole(width, width),
            whole(width, 2 * width),
        ],
        out_specs=[pl.BlockSpec((1, toks, width), lambda j: (j, 0, 0))] * 4 + [whole(2, pair_rows, half)],
        scratch_shapes=[
            pltpu.VMEM((width // 128, pair_rows, 128), F32),
            pltpu.VMEM((width // 128, pair_rows, 128), F32),
            pltpu.VMEM((pair_rows, width), BF16),
            pltpu.VMEM((pair_rows, width), BF16),
            pltpu.VMEM((pair_rows, 2 * width), BF16),
        ],
        name="decode",
    )(seconds.reshape(2, pair_rows, half), q_first, kv_second, wq_second, wkv_first)

    returned = lax.all_to_all(
        back.reshape(owners * groups, items, half), ("img", "tok"), split_axis=0, concat_axis=0, tiled=True
    )
    near = [g0]
    for k, g in enumerate((g1, g2, g3)):
        perm = [(t, (t - k - 1) % groups) for t in range(groups)]
        near.append(lax.ppermute(g, "tok", perm))
    acc = call(
        near_kernel,
        jax.ShapeDtypeStruct((images, toks, width), F32),
        rows * width,
        6 * rows * width,
        in_specs=[smem, smem] + [vmem] * 4,
        out_specs=vmem,
        name="near",
    )(first_local, tok, *near)
    sums = call(
        sum_kernel,
        jax.ShapeDtypeStruct((all_images, half), BF16),
        2 * total * all_images * half,
        2 * (total + all_images) * half,
        grid=(all_images // step_rows,),
        in_specs=[whole(1, total), whole(total, half)],
        out_specs=pl.BlockSpec((step_rows, half), lambda i: (i, 0)),
        name="sum",
    )(second.reshape(1, total), returned.reshape(total, half))
    far = lax.all_to_all(
        sums.reshape(owners, images, half), "img", split_axis=0, concat_axis=0, tiled=True
    )
    return call(
        join_kernel,
        jax.ShapeDtypeStruct((images, toks, width), BF16),
        rows * width * 4,
        rows * width * 10,
        in_specs=[smem] + [vmem] * 3,
        out_specs=vmem,
        scratch_shapes=[pltpu.VMEM((width // 128, rows, 128), F32)],
        name="join",
    )(recip, far, acc, normed)


def solution(mesh):
    in_specs = (P("img", "tok", None), P(), P(), P("img", None), P(), P(), P(), P())
    out_specs = P("img", "tok", None)
    return jax.shard_map(body, mesh=mesh, in_specs=in_specs, out_specs=out_specs, check_vma=False)
```

time: 490 us -> 305 us (0.62); the launches traced: 481 us -> 304 us
  waiting for transfers between devices: 291 us -> 59.2 us
  blocking collectives: 0 us -> 129 us
  Pallas kernels: 0 us -> 69 us
  local copies, waits for them, and re-layouts: 72.7 us -> 7.75 us
  matrix products: 37.5 us -> 0 us
  starting transfers between devices: 62.2 us -> 36.9 us
  other arithmetic: 16.7 us -> 1.99 us
    all_to_all x7 -> x3, waiting for transfers between devices: 291 us -> 12.5 us  [the longest x1 12.5 us: body(): lax.all_to_all(sums.reshape(owners, images, half), 'img', split_axis=0, c...]
    all_gather x0 -> x1, blocking collectives: none -> 72.4 us  [body(): all_pairs = lax.all_gather(pairs, 'img', axis=0, tiled=True)]
    pallas_call x0 -> x7, Pallas kernels: none -> 69 us  [the longest x1 22.8 us: body(): call(decode_kernel, [part, part, part, part, jax.ShapeDtypeStruct((2, pai...]
    all_to_all x0 -> x1, blocking collectives: none -> 56.8 us  [body(): lax.all_to_all(back.reshape(owners * groups, items, half), ('img', 'tok')...]
    ppermute x0 -> x6, waiting for transfers between devices: none -> 46.7 us  [the longest x3 28 us: body(): firsts.append(lax.ppermute(f, 'tok', perm))]
    dot_general x15 -> x0, matrix products: 37.5 us -> none  [the longest x4 14.3 us: project(): jnp.dot(flat, weight, preferred_element_type=jnp.float32)]
    all_to_all x7 -> x3, starting transfers between devices: 62.2 us -> 29.5 us  [the longest x1 13.2 us: body(): lax.all_to_all(pieces, 'img', split_axis=0, concat_axis=0, tiled=True)]
    unnamed x33 -> x25, local copies, waits for them, and re-layouts: 32.9 us -> 3.41 us
  transfers between devices with their start and end apart: 7 -> 9, of which waited for: 5 -> 7; matrix products, arithmetic and copies ran while one was open for 15% -> 1% of each run, Pallas kernels for 0% -> 4%
where the time goes in v1:
time: 305 us; the launch traced here: 304 us
  blocking collectives  129 us (42%)
  Pallas kernels  69 us (23%)
  waiting for transfers between devices  59.2 us (19%)
  starting transfers between devices  36.9 us (12%)
  local copies, waits for them, and re-layouts  7.75 us (3%)
    all_gather x1, blocking collectives, body(): all_pairs = lax.all_gather(pairs, 'img', axis=0, tiled=True)  72.4 us
    all_to_all x1, blocking collectives, body(): lax.all_to_all(back.reshape(owners * groups, items, half), ('img', 'tok')...  56.8 us
    ppermute x3, waiting for transfers between devices, body(): firsts.append(lax.ppermute(f, 'tok', perm))  28 us
    pallas_call x1, Pallas kernels, body(): call(decode_kernel, [part, part, part, part, jax.ShapeDtypeStruct((2, pai...  22.8 us
    ppermute x3, waiting for transfers between devices, body(): near.append(lax.ppermute(g, 'tok', perm))  18.7 us
    all_to_all x1, starting transfers between devices, body(): lax.all_to_all(pieces, 'img', split_axis=0, concat_axis=0, tiled=True)  13.2 us
    all_to_all x1, waiting for transfers between devices, body(): lax.all_to_all(sums.reshape(owners, images, half), 'img', split_axis=0, c...  12.5 us
    all_to_all x1, starting transfers between devices, body(): lax.all_to_all(asked.reshape(owners * groups, items, half), ('img', 'tok'...  10.8 us
  transfers between devices with their start and end apart: 9, of which 7 were waited for; matrix products, arithmetic and copies ran while one was open for 1% of the time, Pallas kernels for 4%

profile of v1, /device:TPU:1, one launch (start us, length us, event | category | flops | bytes accessed | tf_op | source)
XLA Modules:
  0.0 304.0 jit_solution(15965895328581518893)
XLA Ops:
  0.0 1.3 reshape.37.gain_ref
  1.3 1.2 subtract_bitcast_fusion.first_ref
  2.5 9.9 %embed.1 = (bf16[1024,768]{1,0:T(8,128)(2,1)}, bf16[64,32,384]{2,1,0:T(8,128)(2,1)}, bf16[8,32,768]{2,1,0:T(8,128)(2,1)}, bf16[8,32,768]{2,1,0:T(8,128)(2,1)}, b...) custom-call(s32[32]{0:T(128)} %subtract_bitcast_fusion.first_ref, s32[1]{0:T(128)} %bitcast.4.tok_ref, ...), custom_call_target="tpu_custom_call" | custom-call | flops 1610612736 | bytes 8388608 | tf_op jit(solution)/shard_map/embed/pallas_call | solution.py:226
  12.4 13.2 %all-to-all-start = ((bf16[64,32,384]{2,1,0:T(8,128)(2,1)}), bf16[64,32,384]{2,1,0:T(8,128)(2,1)S(1)}, u32[]{:S(2)}, u32[]{:S(2)}) async-start(bf16[64,32,384]{2,1,0:T(8,128)(2,1)} %get-tuple-element.18), calls=%async_computation | async-start | bytes 3145728 | tf_op jit(solution)/shard_map/all_to_all | solution.py:250
  25.6 72.4 %all-gather = s32[64,32,2]{1,2,0:T(2,128)S(1)} all-gather(s32[1,32,2]{1,2,0:T(2,128)S(1)} %bitcast.23), channel_id=1, replica_groups=mesh['img'=64,'tok'=4] {'img'}, dimensions={0}, use_global_device_ids=true | all-gather | bytes 16640 | tf_op jit(solution)/shard_map/all_gather | solution.py:218
  98.1 0.6 fusion
  98.7 1.5 broadcast_in_dim.9.ids_ref
  100.2 8.7 %pick.1 = bf16[2048,384]{1,0:T(8,128)(2,1)} custom-call(s32[2048,128]{1,0:T(8,128)} %broadcast_in_dim.9.ids_ref, bf16[2048,384]{1,0:T(8,128)(2,1)} %bitcast.19), custom_call_target="tpu_custom_call" | custom-call | flops 3221225472 | bytes 3145728 | tf_op jit(solution)/shard_map/pick/pallas_call | solution.py:258
  109.0 10.8 %all-to-all-start.1 = ((bf16[256,8,384]{2,1,0:T(8,128)(2,1)}), bf16[256,8,384]{2,1,0:T(8,128)(2,1)S(1)}, u32[]{:S(2)}, u32[]{:S(2)}) async-start(bf16[256,8,384]{2,1,0:T(8,128)(2,1)} %bitcast.18), calls=%async_computation.1 | async-start | bytes 3145728 | tf_op jit(solution)/shard_map/all_to_all | solution.py:271
  119.8 1.5 collective-permute-start
  121.3 2.4 collective-permute-start.1
  123.7 1.2 collective-permute-start.2
  124.9 11.6 %collective-permute-done.f1 = bf16[8,32,768]{2,1,0:T(8,128)(2,1)S(1)} collective-permute-done((bf16[8,32,768]{2,1,0:T(8,128)(2,1)S(1)}, bf16[8,32,768]{2,1,0:T(8,128)(2,1)S(1)}, u32[]{:S(2)}, u32[]{:S(2)}) %collective-permute-start) | collective-permute-done | bytes 393248 | tf_op jit(solution)/shard_map/ppermute | solution.py:254
  136.5 16.4 %collective-permute-done.1.f2 = bf16[8,32,768]{2,1,0:T(8,128)(2,1)S(1)} collective-permute-done((bf16[8,32,768]{2,1,0:T(8,128)(2,1)S(1)}, bf16[8,32,768]{2,1,0:T(8,128)(2,1)S(1)}, u32[]{:S(2)}, u32[]{:S(2)}) %collective-permute-start.1) | collective-permute-done | bytes 393248 | tf_op jit(solution)/shard_map/ppermute | solution.py:254
  152.9 0.8 copy-done.10
  153.8 8.0 %first.1 = (bf16[8,128,768]{2,1,0:T(8,128)(2,1)}, bf16[8,128,1536]{2,1,0:T(8,128)(2,1)}) custom-call(bf16[8,32,768]{2,1,0:T(8,128)(2,1)} %get-tuple-element.19.f0, bf16[8,32,768]{2,1,0:T(8,128)(2,1)} %copy-done.9, bf16[8,32,768]{2,1,0:T(8,128)(2,1)} %copy-done.10, bf16[8,32,768]{2,1,0:T(8,128)(2,1)} %copy-done.11, bf16[768,768]{1,0:T(8,128)(2,1)} %wq_ref.2, ...), custom_call_target="tpu_custom_call" | custom-call | flops 3623878656 | bytes 9830400 | tf_op jit(solution)/shard_map/first/pallas_call | solution.py:276
  161.9 1.1 copy-done.1
  163.0 22.8 %decode.1 = (bf16[8,32,768]{2,1,0:T(8,128)(2,1)}, bf16[8,32,768]{2,1,0:T(8,128)(2,1)}, bf16[8,32,768]{2,1,0:T(8,128)(2,1)}, bf16[8,32,768]{2,1,0:T(8,128)(2,1)}, bf16[2,1024,384]{2,1,0:T(8,128)(2,1)}) custom-call(bf16[2,1024,384]{2,1,0:T(8,128)(2,1)} %bitcast.17, bf16[8,128,768]{2,1,0:T(8,128)(2,1)} %get-tuple-element.23.q_ref, ...), custom_call_target="tpu_custom_call" | custom-call | flops 5234491392 | bytes 12976128 | tf_op jit(solution)/shard_map/decode/pallas_call | solution.py:290
  185.8 56.8 %all_to_all.20 = bf16[256,8,384]{2,1,0:T(8,128)(2,1)} all-to-all(bf16[256,8,384]{2,1,0:T(8,128)(2,1)} %bitcast.20), channel_id=1, replica_groups=mesh['img'=64,'tok'=4] {'img','tok'}, dimensions={0} | all-to-all | bytes 3145728 | tf_op jit(solution)/shard_map/all_to_all | solution.py:314
  242.5 7.9 %sum.1 = bf16[2048,384]{1,0:T(8,128)(2,1)} custom-call(s32[1,2048]{1,0:T(1,128)} %get-tuple-element.32.ids_ref, bf16[2048,384]{1,0:T(8,128)(2,1)} %bitcast.21), custom_call_target="tpu_custom_call" | custom-call | flops 3221225472 | bytes 3145728 | tf_op jit(solution)/shard_map/sum/pallas_call | solution.py:330
  250.4 5.5 %all-to-all-start.3 = ((bf16[64,32,384]{2,1,0:T(8,128)(2,1)}), bf16[64,32,384]{2,1,0:T(8,128)(2,1)S(1)}, u32[]{:S(2)}, u32[]{:S(2)}) async-start(bf16[64,32,384]{2,1,0:T(8,128)(2,1)} %bitcast.16), calls=%async_computation.3 | async-start | bytes 3145728 | tf_op jit(solution)/shard_map/all_to_all | solution.py:340
  255.8 1.5 collective-permute-start.3
  257.4 0.6 collective-permute-start.4
  258.7 0.5 eq.15
  259.4 0.6 maximum_divide_fusion.recip_ref
  259.9 6.4 %collective-permute-done.3.r1 = bf16[8,32,768]{2,1,0:T(8,128)(2,1)S(1)} collective-permute-done((bf16[8,32,768]{2,1,0:T(8,128)(2,1)}, bf16[8,32,768]{2,1,0:T(8,128)(2,1)S(1)}, u32[]{:S(2)}, u32[]{:S(2)}) %collective-permute-start.3) | collective-permute-done | bytes 393248 | tf_op jit(solution)/shard_map/ppermute | solution.py:320
  266.4 2.7 collective-permute-done.4.r2
  269.0 9.6 %collective-permute-done.5.r3 = bf16[8,32,768]{2,1,0:T(8,128)(2,1)} collective-permute-done((bf16[8,32,768]{2,1,0:T(8,128)(2,1)}, bf16[8,32,768]{2,1,0:T(8,128)(2,1)}, u32[]{:S(2)}, u32[]{:S(2)}) %collective-permute-start.5) | collective-permute-done | bytes 393248 | tf_op jit(solution)/shard_map/ppermute | solution.py:320
  278.7 3.7 %near.1.acc_ref = f32[32,32,768]{2,1,0:T(8,128)} custom-call(s32[32]{0:T(128)} %subtract_bitcast_fusion.first_ref, s32[1]{0:T(128)} %bitcast.4.tok_ref, bf16[8,32,768]{2,1,0:T(8,128)(2,1)} %get-tuple-element.26.r0, bf16[8,32,768]{2,1,0:T(8,128)(2,1)} %copy-done.3, bf16[8,32,768]{2,1,0:T(8,128)(2,1)} %copy-done.4, bf16[8,32,768]{2,1,0:T(8,128)(2,1)} %collective-permute-done.5.r3), custom_call_target="tpu_custom_call" | custom-call | flops 786432 | bytes 4718592 | tf_op jit(solution)/shard_map/near/pallas_call | solution.py:321
  282.4 12.5 %all-to-all-done.3.far_ref = bf16[64,32,384]{2,1,0:T(8,128)(2,1)S(1)} async-done(((bf16[64,32,384]{2,1,0:T(8,128)(2,1)}), bf16[64,32,384]{2,1,0:T(8,128)(2,1)S(1)}, u32[]{:S(2)}, u32[]{:S(2)}) %all-to-all-start.3) | async-done | bytes 1572896 | tf_op jit(solution)/shard_map/all_to_all | solution.py:340
  294.8 1.2 copy-done
  296.0 8.0 %join.1 = bf16[32,32,768]{2,1,0:T(8,128)(2,1)} custom-call(f32[32]{0:T(128)} %maximum_divide_fusion.recip_ref, bf16[64,32,384]{2,1,0:T(8,128)(2,1)} %copy-done, f32[32,32,768]{2,1,0:T(8,128)} %near.1.acc_ref, bf16[1024,768]{1,0:T(8,128)(2,1)} %get-tuple-element.30.normed_ref), custom_call_target="tpu_custom_call" | custom-call | flops 3145728 | bytes 7864320 | tf_op jit(solution)/shard_map/join/pallas_call | solution.py:343
  (30 shorter events, 1.3 us)
Async XLA Ops:
  12.4 13.2 %copy-start.5 = (s32[32,2]{0,1:T(2,128)S(1)}, s32[32,2]{0,1:T(2,128)}, u32[]{:S(2)}) copy-start(s32[32,2]{0,1:T(2,128)} %param.11) | copy-start | bytes 772
  12.4 86.3 %all-to-all-start = ((bf16[64,32,384]{2,1,0:T(8,128)(2,1)}), bf16[64,32,384]{2,1,0:T(8,128)(2,1)S(1)}, u32[]{:S(2)}, u32[]{:S(2)}) async-start(bf16[64,32,384]{2,1,0:T(8,128)(2,1)} %get-tuple-element.18), calls=%async_computation | async-start | bytes 3145728 | tf_op jit(solution)/shard_map/all_to_all | solution.py:250
  98.7 1.5 copy-start.2
  109.0 10.9 %copy-start.8 = (bf16[8,32,768]{2,1,0:T(8,128)(2,1)S(1)}, bf16[8,32,768]{2,1,0:T(8,128)(2,1)}, u32[]{:S(2)}) copy-start(bf16[8,32,768]{2,1,0:T(8,128)(2,1)} %get-tuple-element.20) | copy-start | bytes 1179652
  109.0 12.3 %copy-start.7 = (bf16[8,32,768]{2,1,0:T(8,128)(2,1)S(1)}, bf16[8,32,768]{2,1,0:T(8,128)(2,1)}, u32[]{:S(2)}) copy-start(bf16[8,32,768]{2,1,0:T(8,128)(2,1)} %get-tuple-element.21) | copy-start | bytes 1179652
  109.0 14.7 %copy-start.6 = (bf16[8,32,768]{2,1,0:T(8,128)(2,1)S(1)}, bf16[8,32,768]{2,1,0:T(8,128)(2,1)}, u32[]{:S(2)}) copy-start(bf16[8,32,768]{2,1,0:T(8,128)(2,1)} %get-tuple-element.22) | copy-start | bytes 1179652
  109.0 52.9 %all-to-all-start.1 = ((bf16[256,8,384]{2,1,0:T(8,128)(2,1)}), bf16[256,8,384]{2,1,0:T(8,128)(2,1)S(1)}, u32[]{:S(2)}, u32[]{:S(2)}) async-start(bf16[256,8,384]{2,1,0:T(8,128)(2,1)} %bitcast.18), calls=%async_computation.1 | async-start | bytes 3145728 | tf_op jit(solution)/shard_map/all_to_all | solution.py:271
  119.8 16.6 %collective-permute-start = (bf16[8,32,768]{2,1,0:T(8,128)(2,1)S(1)}, bf16[8,32,768]{2,1,0:T(8,128)(2,1)S(1)}, u32[]{:S(2)}, u32[]{:S(2)}) collective-permute-start(bf16[8,32,768]{2,1,0:T(8,128)(2,1)S(1)} %copy-done.8), channel_id=1, source_target_pairs={{0,1},{1,2},{2,3},{3,0},{4,5},{5,6},{6,7},{7,4},{8,9},{9,10},{10,1... | collective-permute-start | bytes 1179656 | tf_op jit(solution)/shard_map/ppermute | solution.py:254
  121.3 31.6 %collective-permute-start.1 = (bf16[8,32,768]{2,1,0:T(8,128)(2,1)S(1)}, bf16[8,32,768]{2,1,0:T(8,128)(2,1)S(1)}, u32[]{:S(2)}, u32[]{:S(2)}) collective-permute-start(bf16[8,32,768]{2,1,0:T(8,128)(2,1)S(1)} %copy-done.7), channel_id=1, source_target_pairs={{0,2},{1,3},{2,0},{3,1},{4,6},{5,7},{6,4},{7,5},{8,10},{9,11},{10,... | collective-permute-start | bytes 1179656 | tf_op jit(solution)/shard_map/ppermute | solution.py:254
  123.7 29.2 %collective-permute-start.2 = (bf16[8,32,768]{2,1,0:T(8,128)(2,1)S(1)}, bf16[8,32,768]{2,1,0:T(8,128)(2,1)S(1)}, u32[]{:S(2)}, u32[]{:S(2)}) collective-permute-start(bf16[8,32,768]{2,1,0:T(8,128)(2,1)S(1)} %copy-done.6), channel_id=1, source_target_pairs={{0,3},{1,0},{2,1},{3,2},{4,7},{5,4},{6,5},{7,6},{8,11},{9,8},{10,9... | collective-permute-start | bytes 1179656 | tf_op jit(solution)/shard_map/ppermute | solution.py:254
  136.5 16.4 %copy-start.9 = (bf16[8,32,768]{2,1,0:T(8,128)(2,1)}, bf16[8,32,768]{2,1,0:T(8,128)(2,1)S(1)}, u32[]{:S(2)}) copy-start(bf16[8,32,768]{2,1,0:T(8,128)(2,1)S(1)} %collective-permute-done.f1) | copy-start | bytes 1179652
  152.8 0.8 copy-start.10
  152.8 1.0 copy-start.11
  161.9 1.1 copy-start.1
  250.4 44.5 %all-to-all-start.3 = ((bf16[64,32,384]{2,1,0:T(8,128)(2,1)}), bf16[64,32,384]{2,1,0:T(8,128)(2,1)S(1)}, u32[]{:S(2)}, u32[]{:S(2)}) async-start(bf16[64,32,384]{2,1,0:T(8,128)(2,1)} %bitcast.16), calls=%async_computation.3 | async-start | bytes 3145728 | tf_op jit(solution)/shard_map/all_to_all | solution.py:340
  255.8 10.5 %collective-permute-start.3 = (bf16[8,32,768]{2,1,0:T(8,128)(2,1)}, bf16[8,32,768]{2,1,0:T(8,128)(2,1)S(1)}, u32[]{:S(2)}, u32[]{:S(2)}) collective-permute-start(bf16[8,32,768]{2,1,0:T(8,128)(2,1)} %get-tuple-element.27), channel_id=1, source_target_pairs={{0,3},{1,0},{2,1},{3,2},{4,7},{5,4},{6,5},{7,6},{8,11},{9,8},{10,9... | collective-permute-start | bytes 1179656 | tf_op jit(solution)/shard_map/ppermute | solution.py:320
  257.4 11.7 %collective-permute-start.4 = (bf16[8,32,768]{2,1,0:T(8,128)(2,1)}, bf16[8,32,768]{2,1,0:T(8,128)(2,1)S(1)}, u32[]{:S(2)}, u32[]{:S(2)}) collective-permute-start(bf16[8,32,768]{2,1,0:T(8,128)(2,1)} %get-tuple-element.28), channel_id=1, source_target_pairs={{0,2},{1,3},{2,0},{3,1},{4,6},{5,7},{6,4},{7,5},{8,10},{9,11},{10,... | collective-permute-start | bytes 1179656 | tf_op jit(solution)/shard_map/ppermute | solution.py:320
  258.0 20.6 %collective-permute-start.5 = (bf16[8,32,768]{2,1,0:T(8,128)(2,1)}, bf16[8,32,768]{2,1,0:T(8,128)(2,1)}, u32[]{:S(2)}, u32[]{:S(2)}) collective-permute-start(bf16[8,32,768]{2,1,0:T(8,128)(2,1)} %get-tuple-element.29), channel_id=1, source_target_pairs={{0,1},{1,2},{2,3},{3,0},{4,5},{5,6},{6,7},{7,4},{8,9},{9,10},{10,1... | collective-permute-start | bytes 1179656 | tf_op jit(solution)/shard_map/ppermute | solution.py:320
  266.4 12.3 %copy-start.3 = (bf16[8,32,768]{2,1,0:T(8,128)(2,1)}, bf16[8,32,768]{2,1,0:T(8,128)(2,1)S(1)}, u32[]{:S(2)}) copy-start(bf16[8,32,768]{2,1,0:T(8,128)(2,1)S(1)} %collective-permute-done.3.r1) | copy-start | bytes 1179652
  269.0 9.6 %copy-start.4 = (bf16[8,32,768]{2,1,0:T(8,128)(2,1)}, bf16[8,32,768]{2,1,0:T(8,128)(2,1)S(1)}, u32[]{:S(2)}) copy-start(bf16[8,32,768]{2,1,0:T(8,128)(2,1)S(1)} %collective-permute-done.4.r2) | copy-start | bytes 1179652
  294.8 1.2 copy-start

commit v2 on v1

v2 whole, which is shorter than its diff:
```python
import jax
import jax.numpy as jnp
from jax import lax
from jax.experimental import pallas as pl
from jax.experimental.pallas import tpu as pltpu
from jax.sharding import PartitionSpec as P

HEAD = 64
MIB = 1024 * 1024
F32 = jnp.float32
BF16 = jnp.bfloat16


def call(kernel, out_shape, flops, nbytes, vmem_mib, **kwargs):
    return pl.pallas_call(
        kernel,
        out_shape=out_shape,
        compiler_params=pltpu.CompilerParams(vmem_limit_bytes=vmem_mib * MIB),
        cost_estimate=pl.CostEstimate(flops=flops, bytes_accessed=nbytes, transcendentals=0),
        **kwargs,
    )


def hbm(x):
    return pltpu.with_memory_space_constraint(x, pltpu.HBM)


def whole(*shape):
    return pl.BlockSpec(shape, lambda *_: (0,) * len(shape))


def embed_kernel(x_ref, w_ref, gain_ref, ids_ref, normed_ref, pieces_ref, scratch):
    step = pl.program_id(0)
    rows = x_ref.shape[0]
    width = w_ref.shape[1]
    e = jnp.dot(x_ref[...], w_ref[...], preferred_element_type=F32)
    c = e - jnp.mean(e, axis=-1, keepdims=True)
    spread = jnp.mean(c * c, axis=-1, keepdims=True)
    n = c * lax.rsqrt(spread + 1e-06) * gain_ref[...]
    normed_ref[...] = n.astype(BF16)
    start = pl.multiple_of(step * rows, rows)
    for b in range(width // 128):
        scratch[b, pl.ds(start, rows), :] = n[:, b * 128:(b + 1) * 128]

    @pl.when(step == pl.num_programs(0) - 1)
    def _():
        per_half = width // 256
        toks = pieces_ref.shape[0] // 2
        images = scratch.shape[1] // toks
        for r in range(toks):
            for b in range(width // 128):
                h, at = divmod(b, per_half)
                v = scratch[b, pl.ds(r, images, stride=toks), :]
                pieces_ref[h * toks + r, at * images:(at + 1) * images, :] = v.astype(BF16)
        for m in range(2 * toks):
            pieces_ref[m, per_half * images:, :] = ids_ref[...]


def gather_kernel(first_ref, tok_ref, normed_ref, f0, f1, f2, f3):
    group = tok_ref[0]
    for k, f in enumerate((f0, f1, f2, f3)):
        items, toks, _ = f.shape
        for j in range(items):
            p = first_ref[lax.rem(group + k, 4) * items + j]
            f[j] = normed_ref[pl.ds(pl.multiple_of(p * toks, toks), toks), :]


def pick_kernel(table_ref, out_ref, ids_ref):
    step = pl.program_id(0)
    owners, height, _ = table_ref.shape
    rows, half = out_ref.shape
    blocks = half // 128
    images = (height - 8) // blocks
    lane = lax.broadcasted_iota(jnp.int32, (images, 128), 1)
    diagonal = lane == lax.broadcasted_iota(jnp.int32, (images, 128), 0)
    per_step = rows // images
    wanted = []
    for o in range(per_step):
        top = table_ref[step * per_step + o, blocks * images:, :].astype(F32)
        number = top[0:1, :] * float(images) + top[1:2, :]
        ids_ref[o] = number
        column = jnp.sum(jnp.where(diagonal, number, 0.0), axis=1, keepdims=True)
        wanted.append(jnp.broadcast_to(column, (images, 128)))
    wanted = jnp.concatenate(wanted, axis=0)
    lane = lax.broadcasted_iota(jnp.int32, (rows, 128), 1).astype(F32)
    hot = [jnp.where(wanted == lane + float(b * 128), 1.0, 0.0).astype(BF16) for b in range(owners * images // 128)]
    hot = jnp.concatenate(hot, axis=1)
    table = [table_ref[:, b * images:(b + 1) * images, :].reshape(owners * images, 128) for b in range(blocks)]
    out_ref[...] = jnp.dot(hot, jnp.concatenate(table, axis=1), preferred_element_type=F32).astype(BF16)


def sum_kernel(ids_ref, rows_ref, out_ref):
    step = pl.program_id(0)
    images = out_ref.shape[0]
    image = lax.broadcasted_iota(jnp.int32, (images, ids_ref.shape[1]), 0) + step * images
    hot = jnp.where(ids_ref[...] == image, 1.0, 0.0).astype(BF16)
    out_ref[...] = jnp.dot(hot, rows_ref[...], preferred_element_type=F32).astype(BF16)


def first_kernel(f0, f1, f2, f3, wq_ref, wkv_ref, q_ref, kv_ref):
    for k, f in enumerate((f0, f1, f2, f3)):
        items, toks, width = f.shape
        x = f[...].reshape(items * toks, width)
        q = jnp.dot(x, wq_ref[...], preferred_element_type=F32).astype(BF16)
        q_ref[:, k * toks:(k + 1) * toks, :] = q.reshape(items, toks, -1)
        kv = jnp.dot(x, wkv_ref[...], preferred_element_type=F32).astype(BF16)
        kv_ref[:, k * toks:(k + 1) * toks, :] = kv.reshape(items, toks, -1)


def masks(rows):
    lane = lax.broadcasted_iota(jnp.int32, (rows, 128), 1)
    low = lane < HEAD
    one_low = jnp.where(low, 1.0, 0.0).astype(BF16)
    one_high = jnp.where(low, 0.0, 1.0).astype(BF16)
    return low, one_low, one_high


def attend(q, k, v, low, one_low, one_high):
    rows = k.shape[0]
    zero = jnp.zeros((rows, 128), BF16)
    kk = jnp.concatenate([jnp.where(low, k, zero), jnp.where(low, zero, k)], axis=0)
    top = jnp.concatenate([jnp.where(low, v, zero), one_low], axis=1)
    bottom = jnp.concatenate([jnp.where(low, zero, v), one_high], axis=1)
    vv = jnp.concatenate([top, bottom], axis=0)
    s = lax.dot_general(q, kk, (((1,), (1,)), ((), ())), preferred_element_type=F32)
    s = s * (1.0 / HEAD ** 0.5)
    parts = []
    for part in (s[:, :rows], s[:, rows:]):
        parts.append(jnp.exp(part - jnp.max(part, axis=-1, keepdims=True)).astype(BF16))
    o = jnp.dot(jnp.concatenate(parts, axis=1), vv, preferred_element_type=F32)
    return o[:, :128] / o[:, 128:]


def by_pair(x_ref, scratch, x_scr, items):
    per_half = scratch.shape[0] // 2
    toks = scratch.shape[1] // items
    for b in range(scratch.shape[0]):
        h, at = divmod(b, per_half)
        scratch[b] = x_ref[h, :, at * 128:(at + 1) * 128].astype(F32)
        for j in range(items):
            rows = scratch[b, pl.ds(j, toks, stride=items), :]
            x_scr[j * toks:(j + 1) * toks, b * 128:(b + 1) * 128] = rows.astype(BF16)


def second_kernel(x_ref, kv_ref, wq_ref, back_ref, scratch, o_scr, x_scr, q_scr):
    step = pl.program_id(0)
    lane_blocks = scratch.shape[0]
    per_half = lane_blocks // 2
    rows = scratch.shape[1]
    toks = kv_ref.shape[1]
    width = lane_blocks * 128
    items = rows // toks

    @pl.when(step == 0)
    def _():
        by_pair(x_ref, scratch, x_scr, items)

        for i in range(rows // 256):
            at = slice(i * 256, (i + 1) * 256)
            q_scr[at, :] = jnp.dot(x_scr[at, :], wq_ref[...], preferred_element_type=F32).astype(BF16)

    mine = pl.ds(pl.multiple_of(step * toks, toks), toks)
    masked = masks(toks)
    for h in range(lane_blocks):
        at = slice(h * 128, (h + 1) * 128)
        k = kv_ref[0, :, at]
        v = kv_ref[0, :, width + h * 128:width + (h + 1) * 128]
        o_scr[h, mine, :] = attend(q_scr[mine, at], k, v, *masked)

    @pl.when(step == pl.num_programs(0) - 1)
    def _():
        for b in range(lane_blocks):
            h, at = divmod(b, per_half)
            for j in range(items):
                scratch[b, pl.ds(j, toks, stride=items), :] = o_scr[b, j * toks:(j + 1) * toks, :]
            back_ref[h, :, at * 128:(at + 1) * 128] = scratch[b].astype(BF16)


def near_kernel(x_ref, q_ref, wkv_ref, g0, g1, g2, g3, scratch, x_scr, kv_scr):
    step = pl.program_id(0)
    lane_blocks = scratch.shape[0]
    rows = scratch.shape[1]
    toks = q_ref.shape[1]
    width = lane_blocks * 128

    @pl.when(step == 0)
    def _():
        by_pair(x_ref, scratch, x_scr, rows // toks)

        @pl.loop(0, rows // 256)
        def _(i):
            at = pl.ds(pl.multiple_of(i * 256, 256), 256)
            kv_scr[at, :] = jnp.dot(x_scr[at, :], wkv_ref[...], preferred_element_type=F32).astype(BF16)

    mine = pl.ds(pl.multiple_of(step * toks, toks), toks)
    masked = masks(toks)
    part = toks // 4
    for h in range(lane_blocks):
        at = slice(h * 128, (h + 1) * 128)
        v = kv_scr[mine, width + h * 128:width + (h + 1) * 128]
        o = attend(q_ref[0, :, at], kv_scr[mine, at], v, *masked).astype(BF16)
        for k, g in enumerate((g0, g1, g2, g3)):
            g[0, :, at] = o[k * part:(k + 1) * part]


def base_kernel(first_ref, tok_ref, recip_ref, normed_ref, r0, r1, r2, r3, out_ref):
    images, toks, _ = out_ref.shape
    out_ref[...] = jnp.zeros_like(out_ref)
    group = tok_ref[0]
    for k, r in enumerate((r0, r1, r2, r3)):
        items = r.shape[0]

        @pl.loop(0, items)
        def _(j, r=r, k=k, items=items):
            p = first_ref[lax.rem(group + k, 4) * items + j]
            out_ref[p] = out_ref[p] + r[j].astype(F32)

    @pl.loop(0, images)
    def _(i):
        at = pl.ds(pl.multiple_of(i * toks, toks), toks)
        out_ref[i] = out_ref[i] * recip_ref[i] + normed_ref[at, :].astype(F32)


def join_kernel(recip_ref, far_ref, base_ref, out_ref, scratch):
    images, toks, width = base_ref.shape
    half = width // 2
    lane_blocks = width // 128
    first = pl.program_id(0) * images
    for b in range(lane_blocks):
        h, at = divmod(b * 128, half)
        for r in range(toks):
            scratch[b, pl.ds(r, images, stride=toks), :] = far_ref[h * toks + r, :, at:at + 128].astype(F32)
    for i in range(images):
        recip = recip_ref[first + i]
        for b in range(lane_blocks):
            lanes = slice(b * 128, (b + 1) * 128)
            far = scratch[b, i * toks:(i + 1) * toks, :]
            out_ref[i, :, lanes] = (far * recip + base_ref[i, :, lanes]).astype(BF16)


def body(tokens, embed, norm_gain, pairs, wq_first, wkv_first, wq_second, wkv_second):
    images, toks, enc = tokens.shape
    width = embed.shape[1]
    half = width // 2
    owners = lax.axis_size("img")
    groups = lax.axis_size("tok")
    count = pairs.shape[0]
    items = count // groups
    total = owners * count
    all_images = owners * images
    rows = images * toks
    img = lax.axis_index("img")
    tok = lax.axis_index("tok").astype(jnp.int32).reshape(1)
    smem = pl.BlockSpec(memory_space=pltpu.SMEM)
    vmem = pl.BlockSpec(memory_space=pltpu.VMEM)

    first_local = pairs[:, 0] - img * images
    part = jax.ShapeDtypeStruct((items, toks, width), BF16)
    second_owner = pairs[:, 1] // images
    numbers = jnp.stack([second_owner, pairs[:, 1] - second_owner * images]).astype(BF16)
    numbers = jnp.pad(numbers, ((0, 6), (0, 128 - count)))
    block = 256
    height = images * half // 128 + 8
    normed, pieces = call(
        embed_kernel,
        [
            pltpu.HBM((rows, width), BF16),
            pltpu.HBM((owners, height, 128), BF16),
        ],
        2 * rows * enc * width,
        2 * rows * (enc + 2 * width) + 2 * enc * width,
        28,
        grid=(rows // block,),
        in_specs=[
            pl.BlockSpec((block, enc), lambda i: (i, 0)),
            whole(enc, width),
            whole(1, width),
            whole(8, 128),
        ],
        out_specs=[
            pl.BlockSpec((block, width), lambda i: (i, 0)),
            whole(owners, height, 128),
        ],
        scratch_shapes=[pltpu.VMEM((width // 128, rows, 128), F32)],
        name="embed",
    )(hbm(tokens.reshape(rows, enc)), hbm(embed), norm_gain.reshape(1, width), numbers)

    table = lax.all_to_all(pieces, "img", split_axis=0, concat_axis=0, tiled=True)

    firsts = list(call(
        gather_kernel,
        [part] * 4,
        rows * width,
        4 * rows * width,
        8,
        in_specs=[smem, smem, vmem],
        out_specs=[vmem] * 4,
        name="gather",
    )(first_local, tok, normed))
    for k in range(1, groups):
        perm = [(t, (t + k) % groups) for t in range(groups)]
        firsts[k] = lax.ppermute(firsts[k], "tok", perm)
    table, *firsts = lax.optimization_barrier((table, *firsts))

    step_rows = 512
    asked, ids = call(
        pick_kernel,
        [
            pltpu.HBM((total, half), BF16),
            jax.ShapeDtypeStruct((owners, 1, 128), F32),
        ],
        2 * total * all_images * half,
        2 * (total + all_images) * half,
        16,
        grid=(total // step_rows,),
        in_specs=[whole(owners, height, 128)],
        out_specs=[
            pl.BlockSpec((step_rows, half), lambda i: (i, 0)),
            pl.BlockSpec((step_rows // count, 1, 128), lambda i: (i, 0, 0)),
        ],
        name="pick",
    )(table)
    ids = ids[:, 0, :count].astype(jnp.int32).reshape(total)
    seconds = lax.all_to_all(
        asked.reshape(owners * groups, items, half), ("img", "tok"), split_axis=0, concat_axis=0, tiled=True
    )

    whole_toks = toks * groups
    pair_rows = items * whole_toks
    q_first, kv_second = call(
        first_kernel,
        [
            jax.ShapeDtypeStruct((items, whole_toks, width), BF16),
            jax.ShapeDtypeStruct((items, whole_toks, 2 * width), BF16),
        ],
        2 * pair_rows * width * 3 * width,
        2 * pair_rows * width * 4 + 6 * width * width,
        20,
        in_specs=[vmem] * 6,
        out_specs=[vmem] * 2,
        name="first",
    )(*firsts, wq_first, wkv_second)
    own_ids = img * images + jnp.arange(images)
    seen = jnp.sum((ids[None, :] == own_ids[:, None]).astype(F32), axis=1)
    seen = seen + jnp.sum((pairs[:, 0][None, :] == own_ids[:, None]).astype(F32), axis=1)
    recip = 1.0 / jnp.maximum(seen, 1.0)

    seconds = seconds.reshape(2, pair_rows, half)
    back = call(
        second_kernel,
        pltpu.HBM((2, pair_rows, half), BF16),
        2 * pair_rows * width * width + 8 * pair_rows * whole_toks * width,
        2 * pair_rows * width * 4 + 2 * width * width,
        28,
        grid=(items,),
        in_specs=[
            whole(2, pair_rows, half),
            pl.BlockSpec((1, whole_toks, 2 * width), lambda j: (j, 0, 0)),
            whole(width, width),
        ],
        out_specs=whole(2, pair_rows, half),
        scratch_shapes=[
            pltpu.VMEM((width // 128, pair_rows, 128), F32),
            pltpu.VMEM((width // 128, pair_rows, 128), F32),
            pltpu.VMEM((pair_rows, width), BF16),
            pltpu.VMEM((pair_rows, width), BF16),
        ],
        name="second",
    )(seconds, kv_second, wq_second)
    returned = lax.all_to_all(
        back.reshape(owners * groups, items, half), ("img", "tok"), split_axis=0, concat_axis=0, tiled=True
    )

    seconds, _ = lax.optimization_barrier((seconds, back))
    near = list(call(
        near_kernel,
        [part] * 4,
        4 * pair_rows * width * width + 8 * pair_rows * whole_toks * width,
        2 * pair_rows * width * 3 + 4 * width * width,
        28,
        grid=(items,),
        in_specs=[
            whole(2, pair_rows, half),
            pl.BlockSpec((1, whole_toks, width), lambda j: (j, 0, 0)),
            whole(width, 2 * width),
        ],
        out_specs=[pl.BlockSpec((1, toks, width), lambda j: (j, 0, 0))] * 4,
        scratch_shapes=[
            pltpu.VMEM((width // 128, pair_rows, 128), F32),
            pltpu.VMEM((pair_rows, width), BF16),
            pltpu.VMEM((pair_rows, 2 * width), BF16),
        ],
        name="near",
    )(seconds, q_first, wkv_first))
    returned, *near = lax.optimization_barrier((returned, *near))
    for k in range(1, groups):
        perm = [(t, (t - k) % groups) for t in range(groups)]
        near[k] = lax.ppermute(near[k], "tok", perm)

    sums = call(
        sum_kernel,
        pltpu.HBM((all_images, half), BF16),
        2 * total * all_images * half,
        2 * (total + all_images) * half,
        16,
        grid=(all_images // step_rows,),
        in_specs=[whole(1, total), whole(total, half)],
        out_specs=pl.BlockSpec((step_rows, half), lambda i: (i, 0)),
        name="sum",
    )(ids.reshape(1, total), returned.reshape(total, half))
    far = lax.all_to_all(
        sums.reshape(owners, images, half), "img", split_axis=0, concat_axis=0, tiled=True
    )
    base = call(
        base_kernel,
        jax.ShapeDtypeStruct((images, toks, width), F32),
        rows * width,
        8 * rows * width,
        12,
        in_specs=[smem, smem, smem] + [vmem] * 5,
        out_specs=vmem,
        name="base",
    )(first_local, tok, recip, normed, *near)
    block = images // 2
    return call(
        join_kernel,
        jax.ShapeDtypeStruct((images, toks, width), BF16),
        rows * width * 4,
        rows * width * 8,
        16,
        grid=(images // block,),
        in_specs=[
            smem,
            pl.BlockSpec((owners, block, half), lambda i: (0, i, 0)),
            pl.BlockSpec((block, toks, width), lambda i: (i, 0, 0)),
        ],
        out_specs=pl.BlockSpec((block, toks, width), lambda i: (i, 0, 0)),
        scratch_shapes=[pltpu.VMEM((width // 128, block * toks, 128), F32)],
        name="join",
    )(recip, far, base)


def solution(mesh):
    in_specs = (P("img", "tok", None), P(), P(), P("img", None), P(), P(), P(), P())
    out_specs = P("img", "tok", None)
    return jax.shard_map(body, mesh=mesh, in_specs=in_specs, out_specs=out_specs, check_vma=False)
```

time: 305 us -> 239 us (0.78)
  blocking collectives: 129 us -> 0 us
  waiting for transfers between devices: 59.2 us -> 118 us
  Pallas kernels: 69 us -> 49.6 us
  local copies, waits for them, and re-layouts: 7.75 us -> 26.5 us
  starting transfers between devices: 36.9 us -> 42.2 us
    all_gather x1 -> x0, blocking collectives: 72.4 us -> none  [body(): all_pairs = lax.all_gather(pairs, 'img', axis=0, tiled=True)]
    all_to_all x1 -> x0, blocking collectives: 56.8 us -> none  [body(): lax.all_to_all(back.reshape(owners * groups, items, half), ('img', 'tok')...]
    all_to_all x1, waiting for transfers between devices: 0.07 us -> 29.4 us  [body(): lax.all_to_all(asked.reshape(owners * groups, items, half), ('img', 'tok'...]
    all_to_all x0 -> x1, waiting for transfers between devices: none -> 28 us  [body(): lax.all_to_all(back.reshape(owners * groups, items, half), ('img', 'tok')...]
    unnamed x25 -> x68, local copies, waits for them, and re-layouts: 3.41 us -> 25.7 us
    all_to_all x1, waiting for transfers between devices: 0.01 us -> 17.8 us  [body(): lax.all_to_all(pieces, 'img', split_axis=0, concat_axis=0, tiled=True)]
    ppermute x6, waiting for transfers between devices: 46.7 us -> 33.5 us  [the longest x3 18.2 us: body(): near[k] = lax.ppermute(near[k], 'tok', perm)]
    pallas_call x5 -> x7, Pallas kernels: 53 us -> 40.6 us  [the longest x1 9.25 us: body(): call(embed_kernel, [pltpu.HBM((rows, width), BF16), pltpu.HBM((owners, he...]
  transfers between devices with their start and end apart: 9 -> 10, of which waited for: 7 -> 9; matrix products, arithmetic and copies ran while one was open for 1% -> 0% of each run, Pallas kernels for 4% -> 6%
where the time goes in v2:
time: 239 us; the launch traced here: 238 us
  waiting for transfers between devices  118 us (49%)
  Pallas kernels  49.6 us (21%)
  starting transfers between devices  42.2 us (18%)
  local copies, waits for them, and re-layouts  26.5 us (11%)
    all_to_all x1, waiting for transfers between devices, body(): lax.all_to_all(asked.reshape(owners * groups, items, half), ('img', 'tok'...  29.4 us
    all_to_all x1, waiting for transfers between devices, body(): lax.all_to_all(back.reshape(owners * groups, items, half), ('img', 'tok')...  28 us
    unnamed x68, local copies, waits for them, and re-layouts  25.7 us
    ppermute x3, waiting for transfers between devices, body(): near[k] = lax.ppermute(near[k], 'tok', perm)  18.2 us
    all_to_all x1, waiting for transfers between devices, body(): lax.all_to_all(pieces, 'img', split_axis=0, concat_axis=0, tiled=True)  17.8 us
    ppermute x3, waiting for transfers between devices, body(): firsts[k] = lax.ppermute(firsts[k], 'tok', perm)  15.3 us
    all_to_all x1, starting transfers between devices, body(): lax.all_to_all(pieces, 'img', split_axis=0, concat_axis=0, tiled=True)  13.3 us
    pallas_call x1, Pallas kernels, body(): call(embed_kernel, [pltpu.HBM((rows, width), BF16), pltpu.HBM((owners, he...  9.25 us
  transfers between devices with their start and end apart: 10, of which 9 were waited for; matrix products, arithmetic and copies ran while one was open for 0% of the time, Pallas kernels for 6%

profile of v2, /device:TPU:1, one launch (start us, length us, event | category | flops | bytes accessed | tf_op | source)
XLA Modules:
  0.0 238.3 jit_solution(983773651046199782)
XLA Ops:
  2.1 9.3 %embed.1 = (bf16[1024,768]{1,0:T(8,128)(2,1)}, bf16[64,104,128]{2,1,0:T(8,128)(2,1)}) custom-call(bf16[1024,1024]{1,0:T(8,128)(2,1)} %bitcast.31, bf16[1024,768]{1,0:T(8,128)(2,1)} %w_ref.1, f32[1,768]{1,0:T(1,128)S(1)} %reshape.138.gain_ref, bf16[8,128]{1,0:T(8,128)(2,1)S(1)} %fusion.5.ids_ref), custom_call_target="tpu_custom_call" | custom-call | flops 1610612736 | bytes 6815744 | tf_op jit(solution)/shard_map/embed/pallas_call | solution.py:264
  11.3 13.3 %all-to-all-start = ((bf16[64,104,128]{2,1,0:T(8,128)(2,1)}), bf16[64,104,128]{2,1,0:T(8,128)(2,1)S(1)}, u32[]{:S(2)}, u32[]{:S(2)}) async-start(bf16[64,104,128]{2,1,0:T(8,128)(2,1)} %get-tuple-element.30), calls=%async_computation | async-start | bytes 3407872 | tf_op jit(solution)/shard_map/all_to_all | solution.py:288
  26.1 1.2 collective-permute-start
  27.3 2.4 %collective-permute-start.1 = (bf16[8,32,768]{2,1,0:T(8,128)(2,1)S(1)}, bf16[8,32,768]{2,1,0:T(8,128)(2,1)S(1)}, u32[]{:S(2)}, u32[]{:S(2)}) collective-permute-start(bf16[8,32,768]{2,1,0:T(8,128)(2,1)S(1)} %get-tuple-element.34), channel_id=1, source_target_pairs={{0,2},{1,3},{2,0},{3,1},{4,6},{5,7},{6,4},{7,5},{8,10},{9,11},{10,... | collective-permute-start | bytes 1179656 | tf_op jit(solution)/shard_map/ppermute | solution.py:302
  30.9 6.6 %collective-permute-done.f1 = bf16[8,32,768]{2,1,0:T(8,128)(2,1)S(1)} collective-permute-done((bf16[8,32,768]{2,1,0:T(8,128)(2,1)S(1)}, bf16[8,32,768]{2,1,0:T(8,128)(2,1)S(1)}, u32[]{:S(2)}, u32[]{:S(2)}) %collective-permute-start) | collective-permute-done | bytes 393248 | tf_op jit(solution)/shard_map/ppermute | solution.py:302
  38.3 8.6 %collective-permute-done.1.f2 = bf16[8,32,768]{2,1,0:T(8,128)(2,1)S(1)} collective-permute-done((bf16[8,32,768]{2,1,0:T(8,128)(2,1)S(1)}, bf16[8,32,768]{2,1,0:T(8,128)(2,1)S(1)}, u32[]{:S(2)}, u32[]{:S(2)}) %collective-permute-start.1) | collective-permute-done | bytes 393248 | tf_op jit(solution)/shard_map/ppermute | solution.py:302
  48.4 17.8 %all-to-all-done.table_ref = bf16[64,104,128]{2,1,0:T(8,128)(2,1)S(1)} async-done(((bf16[64,104,128]{2,1,0:T(8,128)(2,1)}), bf16[64,104,128]{2,1,0:T(8,128)(2,1)S(1)}, u32[]{:S(2)}, u32[]{:S(2)}) %all-to-all-start) | async-done | bytes 1703968 | tf_op jit(solution)/shard_map/all_to_all | solution.py:288
  66.3 6.0 %pick.1 = (bf16[2048,384]{1,0:T(8,128)(2,1)}, f32[64,1,128]{2,1,0:T(1,128)S(1)}) custom-call(bf16[64,104,128]{2,1,0:T(8,128)(2,1)S(1)} %all-to-all-done.table_ref), custom_call_target="tpu_custom_call" | custom-call | flops 3221225472 | bytes 3145728 | tf_op jit(solution)/shard_map/pick/pallas_call | solution.py:306
  72.3 9.2 %all-to-all-start.1 = ((bf16[256,8,384]{2,1,0:T(8,128)(2,1)}), bf16[256,8,384]{2,1,0:T(8,128)(2,1)S(1)}, u32[]{:S(2)}, u32[]{:S(2)}) async-start(bf16[256,8,384]{2,1,0:T(8,128)(2,1)} %bitcast.29), calls=%async_computation.1 | async-start | bytes 3145728 | tf_op jit(solution)/shard_map/all_to_all | solution.py:324
  81.5 1.7 copy-done.13
  83.1 1.3 copy-done.15
  87.4 3.8 %first.1 = (bf16[8,128,768]{2,1,0:T(8,128)(2,1)S(1)}, bf16[8,128,1536]{2,1,0:T(8,128)(2,1)S(1)}) custom-call(bf16[8,32,768]{2,1,0:T(8,128)(2,1)S(1)} %copy-done.23, bf16[8,32,768]{2,1,0:T(8,128)(2,1)S(1)} %copy-done.25, bf16[8,32,768]{2,1,0:T(8,128)(2,1)S(1)} %copy-done.27, bf16[8,32,768]{2,1,0:T(8,128)(2,1)S(1)} %copy-done.29, ...), custom_call_target="tpu_custom_call" | custom-call | flops 3623878656 | bytes 9830400 | tf_op jit(solution)/shard_map/first/pallas_call | solution.py:330
  91.2 1.6 copy-done.2
  92.9 1.2 copy-done.30
  94.1 29.4 %all-to-all-done.1 = bf16[256,8,384]{2,1,0:T(8,128)(2,1)S(1)} async-done(((bf16[256,8,384]{2,1,0:T(8,128)(2,1)}), bf16[256,8,384]{2,1,0:T(8,128)(2,1)S(1)}, u32[]{:S(2)}, u32[]{:S(2)}) %all-to-all-start.1) | async-done | bytes 1572896 | tf_op jit(solution)/shard_map/all_to_all | solution.py:324
  123.5 1.9 copy-done.3
  125.4 8.6 %second.1 = bf16[2,1024,384]{2,1,0:T(8,128)(2,1)} custom-call(bf16[2,1024,384]{2,1,0:T(8,128)(2,1)S(1)} %bitcast.24, bf16[8,128,1536]{2,1,0:T(8,128)(2,1)S(1)} %copy-done.3, bf16[768,768]{1,0:T(8,128)(2,1)S(1)} %copy-done.4), custom_call_target="tpu_custom_call" | custom-call | flops 2013265920 | bytes 7471104 | tf_op jit(solution)/shard_map/second/pallas_call | solution.py:349
  134.0 6.7 %all-to-all-start.2 = ((bf16[256,8,384]{2,1,0:T(8,128)(2,1)}), bf16[256,8,384]{2,1,0:T(8,128)(2,1)S(1)}, u32[]{:S(2)}, u32[]{:S(2)}) async-start(bf16[256,8,384]{2,1,0:T(8,128)(2,1)} %bitcast.27), calls=%async_computation.2 | async-start | bytes 3145728 | tf_op jit(solution)/shard_map/all_to_all | solution.py:370
  140.8 1.7 copy-done.14
  142.5 1.4 copy-done.31
  143.9 8.6 %near.1 = (bf16[8,32,768]{2,1,0:T(8,128)(2,1)S(1)}, bf16[8,32,768]{2,1,0:T(8,128)(2,1)S(1)}, bf16[8,32,768]{2,1,0:T(8,128)(2,1)S(1)}, bf16[8,32,768]{2,1,0:T(8,128)(2,1)S(1)}) custom-call(bf16[2,1024,384]{2,1,0:T(8,128)(2,1)S(1)} %bitcast.25, bf16[8,128,768]{2,1,0:T(8,128)(2,1)S(1)} %copy-done.31, bf16[768,1536]{1,0:T(8,128)(2,1)S(1)} %copy-done.14), custom_call_target="tpu_custom_call" | custom-call | flops 3221225472 | bytes 7077888 | tf_op jit(solution)/shard_map/near/pallas_call | solution.py:375
  154.7 28.0 %all-to-all-done.2 = bf16[256,8,384]{2,1,0:T(8,128)(2,1)S(1)} async-done(((bf16[256,8,384]{2,1,0:T(8,128)(2,1)}), bf16[256,8,384]{2,1,0:T(8,128)(2,1)S(1)}, u32[]{:S(2)}, u32[]{:S(2)}) %all-to-all-start.2) | async-done | bytes 1572896 | tf_op jit(solution)/shard_map/all_to_all | solution.py:370
  182.7 5.8 %sum.1 = bf16[2048,384]{1,0:T(8,128)(2,1)} custom-call(s32[1,2048]{1,0:T(1,128)S(1)} %convert_element_type.30.ids_ref, bf16[2048,384]{1,0:T(8,128)(2,1)S(1)} %bitcast.26), custom_call_target="tpu_custom_call" | custom-call | flops 3221225472 | bytes 3145728 | tf_op jit(solution)/shard_map/sum/pallas_call | solution.py:400
  188.5 5.8 %all-to-all-start.3 = ((bf16[64,32,384]{2,1,0:T(8,128)(2,1)}), bf16[64,32,384]{2,1,0:T(8,128)(2,1)}, u32[]{:S(2)}, u32[]{:S(2)}) async-start(bf16[64,32,384]{2,1,0:T(8,128)(2,1)} %bitcast.28), calls=%async_computation.3 | async-start | bytes 3145728 | tf_op jit(solution)/shard_map/all_to_all | solution.py:411
  194.5 1.5 collective-permute-start.3
  197.4 7.4 %collective-permute-done.3.r1 = bf16[8,32,768]{2,1,0:T(8,128)(2,1)S(1)} collective-permute-done((bf16[8,32,768]{2,1,0:T(8,128)(2,1)S(1)}, bf16[8,32,768]{2,1,0:T(8,128)(2,1)S(1)}, u32[]{:S(2)}, u32[]{:S(2)}) %collective-permute-start.3) | collective-permute-done | bytes 393248 | tf_op jit(solution)/shard_map/ppermute | solution.py:398
  205.6 1.9 collective-permute-done.4.r2
  208.3 8.8 %collective-permute-done.5.r3 = bf16[8,32,768]{2,1,0:T(8,128)(2,1)S(1)} collective-permute-done((bf16[8,32,768]{2,1,0:T(8,128)(2,1)S(1)}, bf16[8,32,768]{2,1,0:T(8,128)(2,1)S(1)}, u32[]{:S(2)}, u32[]{:S(2)}) %collective-permute-start.5) | collective-permute-done | bytes 393248 | tf_op jit(solution)/shard_map/ppermute | solution.py:398
  217.8 1.4 copy-done.1
  222.2 1.8 base.1.base_ref
  224.0 9.2 %all-to-all-done.3.far_ref = bf16[64,32,384]{2,1,0:T(8,128)(2,1)} async-done(((bf16[64,32,384]{2,1,0:T(8,128)(2,1)}), bf16[64,32,384]{2,1,0:T(8,128)(2,1)}, u32[]{:S(2)}, u32[]{:S(2)}) %all-to-all-start.3) | async-done | bytes 1572896 | tf_op jit(solution)/shard_map/all_to_all | solution.py:411
  233.2 5.1 %join.1 = bf16[32,32,768]{2,1,0:T(8,128)(2,1)} custom-call(f32[32]{0:T(128)S(1)} %maximum_divide_fusion.recip_ref, bf16[64,32,384]{2,1,0:T(8,128)(2,1)} %all-to-all-done.3.far_ref, f32[32,32,768]{2,1,0:T(8,128)S(1)} %base.1.base_ref), custom_call_target="tpu_custom_call" | custom-call | flops 3145728 | bytes 6291456 | tf_op jit(solution)/shard_map/join/pallas_call | solution.py:425
  (78 shorter events, 19.1 us)
Async XLA Ops:
  11.3 13.3 %copy-start.32 = (s32[32,2]{0,1:T(2,128)S(1)}, s32[32,2]{0,1:T(2,128)}, u32[]{:S(2)}) copy-start(s32[32,2]{0,1:T(2,128)} %param.11) | copy-start | bytes 772
  11.3 13.3 %copy-start = (bf16[1024,768]{1,0:T(8,128)(2,1)S(1)}, bf16[1024,768]{1,0:T(8,128)(2,1)}, u32[]{:S(2)}) copy-start(bf16[1024,768]{1,0:T(8,128)(2,1)} %get-tuple-element.31.normed_ref) | copy-start | bytes 4718596
  11.3 54.9 %all-to-all-start = ((bf16[64,104,128]{2,1,0:T(8,128)(2,1)}), bf16[64,104,128]{2,1,0:T(8,128)(2,1)S(1)}, u32[]{:S(2)}, u32[]{:S(2)}) async-start(bf16[64,104,128]{2,1,0:T(8,128)(2,1)} %get-tuple-element.30), calls=%async_computation | async-start | bytes 3407872 | tf_op jit(solution)/shard_map/all_to_all | solution.py:288
  26.1 11.4 %collective-permute-start = (bf16[8,32,768]{2,1,0:T(8,128)(2,1)S(1)}, bf16[8,32,768]{2,1,0:T(8,128)(2,1)S(1)}, u32[]{:S(2)}, u32[]{:S(2)}) collective-permute-start(bf16[8,32,768]{2,1,0:T(8,128)(2,1)S(1)} %get-tuple-element.33), channel_id=1, source_target_pairs={{0,1},{1,2},{2,3},{3,0},{4,5},{5,6},{6,7},{7,4},{8,9},{9,10},{10,1... | collective-permute-start | bytes 1179656 | tf_op jit(solution)/shard_map/ppermute | solution.py:302
  27.3 19.6 %collective-permute-start.1 = (bf16[8,32,768]{2,1,0:T(8,128)(2,1)S(1)}, bf16[8,32,768]{2,1,0:T(8,128)(2,1)S(1)}, u32[]{:S(2)}, u32[]{:S(2)}) collective-permute-start(bf16[8,32,768]{2,1,0:T(8,128)(2,1)S(1)} %get-tuple-element.34), channel_id=1, source_target_pairs={{0,2},{1,3},{2,0},{3,1},{4,6},{5,7},{6,4},{7,5},{8,10},{9,11},{10,... | collective-permute-start | bytes 1179656 | tf_op jit(solution)/shard_map/ppermute | solution.py:302
  29.8 17.9 %collective-permute-start.2 = (bf16[8,32,768]{2,1,0:T(8,128)(2,1)S(1)}, bf16[8,32,768]{2,1,0:T(8,128)(2,1)S(1)}, u32[]{:S(2)}, u32[]{:S(2)}) collective-permute-start(bf16[8,32,768]{2,1,0:T(8,128)(2,1)S(1)} %get-tuple-element.35), channel_id=1, source_target_pairs={{0,3},{1,0},{2,1},{3,2},{4,7},{5,4},{6,5},{7,6},{8,11},{9,8},{10,9... | collective-permute-start | bytes 1179656 | tf_op jit(solution)/shard_map/ppermute | solution.py:302
  72.3 68.4 %copy-start.11 = (f32[64,1,128]{2,1,0:T(1,128)}, f32[64,1,128]{2,1,0:T(1,128)S(1)}, u32[]{:S(2)}) copy-start(f32[64,1,128]{2,1,0:T(1,128)S(1)} %get-tuple-element.37) | copy-start | bytes 98308
  72.3 9.2 %copy-start.23 = (bf16[8,32,768]{2,1,0:T(8,128)(2,1)S(1)}, bf16[8,32,768]{2,1,0:T(8,128)(2,1)}, u32[]{:S(2)}) copy-start(bf16[8,32,768]{2,1,0:T(8,128)(2,1)} %copy-done.22) | copy-start | bytes 1179652
  72.3 51.2 %all-to-all-start.1 = ((bf16[256,8,384]{2,1,0:T(8,128)(2,1)}), bf16[256,8,384]{2,1,0:T(8,128)(2,1)S(1)}, u32[]{:S(2)}, u32[]{:S(2)}) async-start(bf16[256,8,384]{2,1,0:T(8,128)(2,1)} %bitcast.29), calls=%async_computation.1 | async-start | bytes 3145728 | tf_op jit(solution)/shard_map/all_to_all | solution.py:324
  81.4 1.7 copy-start.13
  83.1 1.3 copy-start.15
  84.4 1.0 copy-start.25
  85.4 1.0 copy-start.27
  86.4 1.0 copy-start.29
  87.4 36.1 %copy-start.4 = (bf16[768,768]{1,0:T(8,128)(2,1)S(1)}, bf16[768,768]{1,0:T(8,128)(2,1)}, u32[]{:S(2)}) copy-start(bf16[768,768]{1,0:T(8,128)(2,1)} %wq_ref.3) | copy-start | bytes 3538948
  91.2 1.6 copy-start.2
  92.9 1.2 copy-start.30
  123.5 1.9 copy-start.3
  134.0 48.7 %all-to-all-start.2 = ((bf16[256,8,384]{2,1,0:T(8,128)(2,1)}), bf16[256,8,384]{2,1,0:T(8,128)(2,1)S(1)}, u32[]{:S(2)}, u32[]{:S(2)}) async-start(bf16[256,8,384]{2,1,0:T(8,128)(2,1)} %bitcast.27), calls=%async_computation.2 | async-start | bytes 3145728 | tf_op jit(solution)/shard_map/all_to_all | solution.py:370
  140.8 1.7 copy-start.14
  142.5 1.4 copy-start.31
  188.5 5.8 %copy-start.33 = (s32[32,2]{0,1:T(2,128)S(1)}, s32[32,2]{0,1:T(2,128)}, u32[]{:S(2)}) copy-start(s32[32,2]{0,1:T(2,128)} %param.11) | copy-start | bytes 772
  188.5 6.0 %copy-start.21 = (bf16[8,32,768]{2,1,0:T(8,128)(2,1)S(1)}, bf16[8,32,768]{2,1,0:T(8,128)(2,1)}, u32[]{:S(2)}) copy-start(bf16[8,32,768]{2,1,0:T(8,128)(2,1)} %copy-done.20) | copy-start | bytes 1179652
  188.5 7.5 %copy-start.19 = (bf16[8,32,768]{2,1,0:T(8,128)(2,1)S(1)}, bf16[8,32,768]{2,1,0:T(8,128)(2,1)}, u32[]{:S(2)}) copy-start(bf16[8,32,768]{2,1,0:T(8,128)(2,1)} %copy-done.18) | copy-start | bytes 1179652
  188.5 8.2 %copy-start.17 = (bf16[8,32,768]{2,1,0:T(8,128)(2,1)S(1)}, bf16[8,32,768]{2,1,0:T(8,128)(2,1)}, u32[]{:S(2)}) copy-start(bf16[8,32,768]{2,1,0:T(8,128)(2,1)} %copy-done.16) | copy-start | bytes 1179652
  188.5 8.5 %copy-start.12 = (f32[64,1,128]{2,1,0:T(1,128)S(1)}, f32[64,1,128]{2,1,0:T(1,128)}, u32[]{:S(2)}) copy-start(f32[64,1,128]{2,1,0:T(1,128)} %copy-done.11) | copy-start | bytes 98308
  188.5 44.7 %all-to-all-start.3 = ((bf16[64,32,384]{2,1,0:T(8,128)(2,1)}), bf16[64,32,384]{2,1,0:T(8,128)(2,1)}, u32[]{:S(2)}, u32[]{:S(2)}) async-start(bf16[64,32,384]{2,1,0:T(8,128)(2,1)} %bitcast.28), calls=%async_computation.3 | async-start | bytes 3145728 | tf_op jit(solution)/shard_map/all_to_all | solution.py:411
  194.5 10.3 %collective-permute-start.3 = (bf16[8,32,768]{2,1,0:T(8,128)(2,1)S(1)}, bf16[8,32,768]{2,1,0:T(8,128)(2,1)S(1)}, u32[]{:S(2)}, u32[]{:S(2)}) collective-permute-start(bf16[8,32,768]{2,1,0:T(8,128)(2,1)S(1)} %copy-done.21), channel_id=1, source_target_pairs={{0,3},{1,0},{2,1},{3,2},{4,7},{5,4},{6,5},{7,6},{8,11},{9,8},{10,9... | collective-permute-start | bytes 1179656 | tf_op jit(solution)/shard_map/ppermute | solution.py:398
  196.0 11.5 %collective-permute-start.4 = (bf16[8,32,768]{2,1,0:T(8,128)(2,1)S(1)}, bf16[8,32,768]{2,1,0:T(8,128)(2,1)S(1)}, u32[]{:S(2)}, u32[]{:S(2)}) collective-permute-start(bf16[8,32,768]{2,1,0:T(8,128)(2,1)S(1)} %copy-done.19), channel_id=1, source_target_pairs={{0,2},{1,3},{2,0},{3,1},{4,6},{5,7},{6,4},{7,5},{8,10},{9,11},{10,... | collective-permute-start | bytes 1179656 | tf_op jit(solution)/shard_map/ppermute | solution.py:398
  196.6 20.4 %collective-permute-start.5 = (bf16[8,32,768]{2,1,0:T(8,128)(2,1)S(1)}, bf16[8,32,768]{2,1,0:T(8,128)(2,1)S(1)}, u32[]{:S(2)}, u32[]{:S(2)}) collective-permute-start(bf16[8,32,768]{2,1,0:T(8,128)(2,1)S(1)} %copy-done.17), channel_id=1, source_target_pairs={{0,1},{1,2},{2,3},{3,0},{4,5},{5,6},{6,7},{7,4},{8,9},{9,10},{10,1... | collective-permute-start | bytes 1179656 | tf_op jit(solution)/shard_map/ppermute | solution.py:398
  217.8 1.4 copy-start.1
  221.2 1.0 copy-start.10
  (12 other events, 9.6 us)

commit v3 on v2

--- a/solution.py
+++ b/solution.py
@@ -29,31 +29,65 @@
     return pl.BlockSpec(shape, lambda *_: (0,) * len(shape))
 
 
-def embed_kernel(x_ref, w_ref, gain_ref, ids_ref, normed_ref, pieces_ref, scratch):
-    step = pl.program_id(0)
-    rows = x_ref.shape[0]
-    width = w_ref.shape[1]
-    e = jnp.dot(x_ref[...], w_ref[...], preferred_element_type=F32)
-    c = e - jnp.mean(e, axis=-1, keepdims=True)
-    spread = jnp.mean(c * c, axis=-1, keepdims=True)
-    n = c * lax.rsqrt(spread + 1e-06) * gain_ref[...]
-    normed_ref[...] = n.astype(BF16)
-    start = pl.multiple_of(step * rows, rows)
-    for b in range(width // 128):
-        scratch[b, pl.ds(start, rows), :] = n[:, b * 128:(b + 1) * 128]
-
-    @pl.when(step == pl.num_programs(0) - 1)
-    def _():
-        per_half = width // 256
-        toks = pieces_ref.shape[0] // 2
-        images = scratch.shape[1] // toks
+def embed_kernel(
+    x_hbm, w_hbm, gain_hbm, pairs_hbm, normed_hbm, pieces_hbm,
+    x_scr, w_scr, gain_scr, pairs_scr, normed_scr, pieces_scr, scratch, in_sems, normed_sems, piece_sems,
+):
+    chunks, rows, _ = x_scr.shape
+    width = w_scr.shape[1]
+    per_half = width // 256
+    toks = pieces_scr.shape[0] // 2
+    pitch = toks + 8
+    images = scratch.shape[1] // pitch
+    small = [
+        pltpu.make_async_copy(pairs_hbm, pairs_scr, in_sems.at[chunks + 1]),
+        pltpu.make_async_copy(gain_hbm, gain_scr, in_sems.at[chunks + 2]),
+    ]
+    loads = [pltpu.make_async_copy(w_hbm, w_scr, in_sems.at[chunks])]
+    for i in range(chunks):
+        loads.append(pltpu.make_async_copy(x_hbm.at[pl.ds(i * rows, rows)], x_scr.at[i], in_sems.at[i]))
+    for load in loads + small:
+        load.start()
+    for load in small:
+        load.wait()
+    gain = gain_scr[...].reshape(1, width)
+    second = pairs_scr[1:2, :]
+    owner = lax.div(second, images)
+    numbers = jnp.concatenate([owner, second - owner * images], axis=0).astype(F32)
+    numbers = jnp.concatenate([numbers, jnp.zeros((6, numbers.shape[1]), F32)], axis=0)
+    numbers = jnp.concatenate([numbers, jnp.zeros((8, 128 - numbers.shape[1]), F32)], axis=1).astype(BF16)
+    for m in range(2 * toks):
+        pieces_scr[m, per_half * images:, :] = numbers
+    loads[0].wait()
+    stores = []
+    for i in range(chunks):
+        loads[i + 1].wait()
+        at = pl.ds(i * rows, rows)
+        e = jnp.dot(x_scr[i], w_scr[...], preferred_element_type=F32)
+        c = e - jnp.mean(e, axis=-1, keepdims=True)
+        spread = jnp.mean(c * c, axis=-1, keepdims=True)
+        n = c * lax.rsqrt(spread + 1e-06) * gain
+        normed_scr[at, :] = n.astype(BF16)
+        stores.append(pltpu.make_async_copy(normed_scr.at[at], normed_hbm.at[at], normed_sems.at[i]))
+        stores[-1].start()
+        for u in range(rows // toks):
+            to = pl.ds((i * (rows // toks) + u) * pitch, toks)
+            for b in range(width // 128):
+                scratch[b, to, :] = n[u * toks:(u + 1) * toks, b * 128:(b + 1) * 128]
+    group = 8
+    for h in range(2):
         for r in range(toks):
-            for b in range(width // 128):
-                h, at = divmod(b, per_half)
-                v = scratch[b, pl.ds(r, images, stride=toks), :]
-                pieces_ref[h * toks + r, at * images:(at + 1) * images, :] = v.astype(BF16)
-        for m in range(2 * toks):
-            pieces_ref[m, per_half * images:, :] = ids_ref[...]
+            for b in range(per_half):
+                v = scratch[h * per_half + b, pl.ds(r, images, stride=pitch), :]
+                pieces_scr[h * toks + r, b * images:(b + 1) * images, :] = v.astype(BF16)
+            if r % group == group - 1:
+                first = h * toks + r - group + 1
+                at = pl.ds(first, group)
+                sem = piece_sems.at[first // group]
+                stores.append(pltpu.make_async_copy(pieces_scr.at[at], pieces_hbm.at[at], sem))
+                stores[-1].start()
+    for store in stores:
+        store.wait()
 
 
 def gather_kernel(first_ref, tok_ref, normed_ref, f0, f1, f2, f3):
@@ -142,38 +176,37 @@
             x_scr[j * toks:(j + 1) * toks, b * 128:(b + 1) * 128] = rows.astype(BF16)
 
 
-def second_kernel(x_ref, kv_ref, wq_ref, back_ref, scratch, o_scr, x_scr, q_scr):
+def second_kernel(x_ref, kv_ref, wq_ref, back_ref, q_scr, o_scr):
     step = pl.program_id(0)
-    lane_blocks = scratch.shape[0]
+    steps = pl.num_programs(0)
+    lane_blocks, rows, _ = q_scr.shape
     per_half = lane_blocks // 2
-    rows = scratch.shape[1]
-    toks = kv_ref.shape[1]
+    per_step, toks, _ = kv_ref.shape
     width = lane_blocks * 128
     items = rows // toks
 
     @pl.when(step == 0)
     def _():
-        by_pair(x_ref, scratch, x_scr, items)
-
         for i in range(rows // 256):
             at = slice(i * 256, (i + 1) * 256)
-            q_scr[at, :] = jnp.dot(x_scr[at, :], wq_ref[...], preferred_element_type=F32).astype(BF16)
-
-    mine = pl.ds(pl.multiple_of(step * toks, toks), toks)
+            x = jnp.concatenate([x_ref[0, at, :], x_ref[1, at, :]], axis=1)
+            q = jnp.dot(x, wq_ref[...], preferred_element_type=F32)
+            for b in range(lane_blocks):
+                q_scr[b, at, :] = q[:, b * 128:(b + 1) * 128]
+
     masked = masks(toks)
-    for h in range(lane_blocks):
-        at = slice(h * 128, (h + 1) * 128)
-        k = kv_ref[0, :, at]
-        v = kv_ref[0, :, width + h * 128:width + (h + 1) * 128]
-        o_scr[h, mine, :] = attend(q_scr[mine, at], k, v, *masked)
-
-    @pl.when(step == pl.num_programs(0) - 1)
+    for p in range(per_step):
+        mine = pl.ds(step * per_step + p, toks, stride=items)
+        for h in range(lane_blocks):
+            k = kv_ref[p, :, h * 128:(h + 1) * 128]
+            v = kv_ref[p, :, width + h * 128:width + (h + 1) * 128]
+            o_scr[h, mine, :] = attend(q_scr[h, mine, :].astype(BF16), k, v, *masked)
+
+    @pl.when(step == steps - 1)
     def _():
         for b in range(lane_blocks):
             h, at = divmod(b, per_half)
-            for j in range(items):
-                scratch[b, pl.ds(j, toks, stride=items), :] = o_scr[b, j * toks:(j + 1) * toks, :]
-            back_ref[h, :, at * 128:(at + 1) * 128] = scratch[b].astype(BF16)
+            back_ref[h, :, at * 128:(at + 1) * 128] = o_scr[b].astype(BF16)
 
 
 def near_kernel(x_ref, q_ref, wkv_ref, g0, g1, g2, g3, scratch, x_scr, kv_scr):
@@ -221,21 +254,32 @@
         out_ref[i] = out_ref[i] * recip_ref[i] + normed_ref[at, :].astype(F32)
 
 
-def join_kernel(recip_ref, far_ref, base_ref, out_ref, scratch):
+def join_kernel(recip_ref, far_ref, base_ref, out_hbm, out_scr, scratch, sems):
     images, toks, width = base_ref.shape
     half = width // 2
     lane_blocks = width // 128
-    first = pl.program_id(0) * images
-    for b in range(lane_blocks):
-        h, at = divmod(b * 128, half)
-        for r in range(toks):
-            scratch[b, pl.ds(r, images, stride=toks), :] = far_ref[h * toks + r, :, at:at + 128].astype(F32)
-    for i in range(images):
-        recip = recip_ref[first + i]
+    pitch = toks + 8
+    group = scratch.shape[1] // pitch
+    stores = []
+    for g in range(images // group):
         for b in range(lane_blocks):
-            lanes = slice(b * 128, (b + 1) * 128)
-            far = scratch[b, i * toks:(i + 1) * toks, :]
-            out_ref[i, :, lanes] = (far * recip + base_ref[i, :, lanes]).astype(BF16)
+            h, at = divmod(b * 128, half)
+            for r in range(toks):
+                far = far_ref[h * toks + r, g * group:(g + 1) * group, at:at + 128]
+                scratch[b, pl.ds(r, group, stride=pitch), :] = far.astype(F32)
+        for u in range(group):
+            i = g * group + u
+            recip = recip_ref[i]
+            for b in range(lane_blocks):
+                lanes = slice(b * 128, (b + 1) * 128)
+                far = scratch[b, u * pitch:u * pitch + toks, :]
+                out_scr[i, :, lanes] = (far * recip + base_ref[i, :, lanes]).astype(BF16)
+            if u % 8 == 7:
+                at = pl.ds(i - 7, 8)
+                stores.append(pltpu.make_async_copy(out_scr.at[at], out_hbm.at[at], sems.at[i // 8]))
+                stores[-1].start()
+    for store in stores:
+        store.wait()
 
 
 def body(tokens, embed, norm_gain, pairs, wq_first, wkv_first, wq_second, wkv_second):
@@ -256,11 +300,9 @@
 
     first_local = pairs[:, 0] - img * images
     part = jax.ShapeDtypeStruct((items, toks, width), BF16)
-    second_owner = pairs[:, 1] // images
-    numbers = jnp.stack([second_owner, pairs[:, 1] - second_owner * images]).astype(BF16)
-    numbers = jnp.pad(numbers, ((0, 6), (0, 128 - count)))
     block = 256
     height = images * half // 128 + 8
+    anywhere = pl.BlockSpec(memory_space=pl.ANY)
     normed, pieces = call(
         embed_kernel,
         [
@@ -270,20 +312,22 @@
         2 * rows * enc * width,
         2 * rows * (enc + 2 * width) + 2 * enc * width,
         28,
-        grid=(rows // block,),
-        in_specs=[
-            pl.BlockSpec((block, enc), lambda i: (i, 0)),
-            whole(enc, width),
-            whole(1, width),
-            whole(8, 128),
-        ],
-        out_specs=[
-            pl.BlockSpec((block, width), lambda i: (i, 0)),
-            whole(owners, height, 128),
-        ],
-        scratch_shapes=[pltpu.VMEM((width // 128, rows, 128), F32)],
+        in_specs=[anywhere] * 4,
+        out_specs=[anywhere, anywhere],
+        scratch_shapes=[
+            pltpu.VMEM((rows // block, block, enc), BF16),
+            pltpu.VMEM((enc, width), BF16),
+            pltpu.VMEM((width,), F32),
+            pltpu.VMEM((2, count), jnp.int32),
+            pltpu.VMEM((rows, width), BF16),
+            pltpu.VMEM((owners, height, 128), BF16),
+            pltpu.VMEM((width // 128, images * (toks + 8), 128), F32),
+            pltpu.SemaphoreType.DMA((rows // block + 3,)),
+            pltpu.SemaphoreType.DMA((rows // block,)),
+            pltpu.SemaphoreType.DMA((owners // 8,)),
+        ],
         name="embed",
-    )(hbm(tokens.reshape(rows, enc)), hbm(embed), norm_gain.reshape(1, width), numbers)
+    )(hbm(tokens.reshape(rows, enc)), hbm(embed), hbm(norm_gain), hbm(pairs.T))
 
     table = lax.all_to_all(pieces, "img", split_axis=0, concat_axis=0, tiled=True)
 
@@ -313,7 +357,7 @@
         2 * (total + all_images) * half,
         16,
         grid=(total // step_rows,),
-        in_specs=[whole(owners, height, 128)],
+        in_specs=[vmem],
         out_specs=[
             pl.BlockSpec((step_rows, half), lambda i: (i, 0)),
             pl.BlockSpec((step_rows // count, 1, 128), lambda i: (i, 0, 0)),
@@ -352,21 +396,19 @@
         2 * pair_rows * width * width + 8 * pair_rows * whole_toks * width,
         2 * pair_rows * width * 4 + 2 * width * width,
         28,
-        grid=(items,),
+        grid=(items // 2,),
         in_specs=[
-            whole(2, pair_rows, half),
-            pl.BlockSpec((1, whole_toks, 2 * width), lambda j: (j, 0, 0)),
-            whole(width, width),
+            vmem,
+            pl.BlockSpec((2, whole_toks, 2 * width), lambda j: (j, 0, 0)),
+            vmem,
         ],
         out_specs=whole(2, pair_rows, half),
         scratch_shapes=[
             pltpu.VMEM((width // 128, pair_rows, 128), F32),
             pltpu.VMEM((width // 128, pair_rows, 128), F32),
-            pltpu.VMEM((pair_rows, width), BF16),
-            pltpu.VMEM((pair_rows, width), BF16),
         ],
         name="second",
-    )(seconds, kv_second, wq_second)
+    )(seconds, hbm(kv_second), wq_second)
     returned = lax.all_to_all(
         back.reshape(owners * groups, items, half), ("img", "tok"), split_axis=0, concat_axis=0, tiled=True
     )
@@ -380,9 +422,9 @@
         28,
         grid=(items,),
         in_specs=[
-            whole(2, pair_rows, half),
+            vmem,
             pl.BlockSpec((1, whole_toks, width), lambda j: (j, 0, 0)),
-            whole(width, 2 * width),
+            vmem,
         ],
         out_specs=[pl.BlockSpec((1, toks, width), lambda j: (j, 0, 0))] * 4,
         scratch_shapes=[
@@ -404,7 +446,7 @@
         2 * (total + all_images) * half,
         16,
         grid=(all_images // step_rows,),
-        in_specs=[whole(1, total), whole(total, half)],
+        in_specs=[vmem, vmem],
         out_specs=pl.BlockSpec((step_rows, half), lambda i: (i, 0)),
         name="sum",
     )(ids.reshape(1, total), returned.reshape(total, half))
@@ -421,21 +463,19 @@
         out_specs=vmem,
         name="base",
     )(first_local, tok, recip, normed, *near)
-    block = images // 2
     return call(
         join_kernel,
-        jax.ShapeDtypeStruct((images, toks, width), BF16),
+        pltpu.HBM((images, toks, width), BF16),
         rows * width * 4,
         rows * width * 8,
-        16,
-        grid=(images // block,),
-        in_specs=[
-            smem,
-            pl.BlockSpec((owners, block, half), lambda i: (0, i, 0)),
-            pl.BlockSpec((block, toks, width), lambda i: (i, 0, 0)),
-        ],
-        out_specs=pl.BlockSpec((block, toks, width), lambda i: (i, 0, 0)),
-        scratch_shapes=[pltpu.VMEM((width // 128, block * toks, 128), F32)],
+        24,
+        in_specs=[smem, vmem, vmem],
+        out_specs=anywhere,
+        scratch_shapes=[
+            pltpu.VMEM((images, toks, width), BF16),
+            pltpu.VMEM((width // 128, images // 2 * (toks + 8), 128), F32),
+            pltpu.SemaphoreType.DMA((images // 8,)),
+        ],
         name="join",
     )(recip, far, base)
 

time: 239 us -> 230 us (0.962)
  Pallas kernels: 49.6 us -> 44.3 us
  local copies, waits for them, and re-layouts: 26.5 us -> 24 us
    unnamed x68 -> x64, local copies, waits for them, and re-layouts: 25.7 us -> 23.8 us
where the time goes in v3:
time: 230 us; the launch traced here: 229 us
  waiting for transfers between devices  118 us (51%)
  Pallas kernels  44.3 us (19%)
  starting transfers between devices  42.2 us (18%)
  local copies, waits for them, and re-layouts  24 us (10%)
    all_to_all x1, waiting for transfers between devices, body(): lax.all_to_all(asked.reshape(owners * groups, items, half), ('img', 'tok'...  29.4 us
    all_to_all x1, waiting for transfers between devices, body(): lax.all_to_all(back.reshape(owners * groups, items, half), ('img', 'tok')...  27.9 us
    unnamed x64, local copies, waits for them, and re-layouts  23.8 us
    ppermute x3, waiting for transfers between devices, body(): near[k] = lax.ppermute(near[k], 'tok', perm)  18.2 us
    all_to_all x1, waiting for transfers between devices, body(): lax.all_to_all(pieces, 'img', split_axis=0, concat_axis=0, tiled=True)  17.8 us
    ppermute x3, waiting for transfers between devices, body(): firsts[k] = lax.ppermute(firsts[k], 'tok', perm)  15.3 us
    all_to_all x1, starting transfers between devices, body(): lax.all_to_all(pieces, 'img', split_axis=0, concat_axis=0, tiled=True)  13.3 us
    all_to_all x1, waiting for transfers between devices, body(): lax.all_to_all(sums.reshape(owners, images, half), 'img', split_axis=0, c...  9.22 us
  transfers between devices with their start and end apart: 10, of which 9 were waited for; matrix products, arithmetic and copies ran while one was open for 0% of the time, Pallas kernels for 6%

profile of v3, /device:TPU:1, one launch (start us, length us, event | category | flops | bytes accessed | tf_op | source)
XLA Modules:
  0.0 229.3 jit_solution(9083848734595690121)
XLA Ops:
  0.0 7.0 %embed.1 = (bf16[1024,768]{1,0:T(8,128)(2,1)}, bf16[64,104,128]{2,1,0:T(8,128)(2,1)}) custom-call(bf16[1024,1024]{1,0:T(8,128)(2,1)} %bitcast.20, bf16[1024,768]{1,0:T(8,128)(2,1)} %w_hbm.1, f32[768]{0:T(1024)} %gain_hbm.1, s32[2,32]{1,0:T(2,128)} %bitcast.21), custom_call_target="tpu_custom_call" | custom-call | flops 1610612736 | bytes 6815744 | tf_op jit(solution)/shard_map/embed/pallas_call | solution.py:306
  7.0 13.3 %all-to-all-start = ((bf16[64,104,128]{2,1,0:T(8,128)(2,1)}), bf16[64,104,128]{2,1,0:T(8,128)(2,1)S(1)}, u32[]{:S(2)}, u32[]{:S(2)}) async-start(bf16[64,104,128]{2,1,0:T(8,128)(2,1)} %get-tuple-element.30), calls=%async_computation | async-start | bytes 3407872 | tf_op jit(solution)/shard_map/all_to_all | solution.py:332
  21.8 1.2 collective-permute-start
  23.0 2.5 %collective-permute-start.1 = (bf16[8,32,768]{2,1,0:T(8,128)(2,1)S(1)}, bf16[8,32,768]{2,1,0:T(8,128)(2,1)S(1)}, u32[]{:S(2)}, u32[]{:S(2)}) collective-permute-start(bf16[8,32,768]{2,1,0:T(8,128)(2,1)S(1)} %get-tuple-element.34), channel_id=1, source_target_pairs={{0,2},{1,3},{2,0},{3,1},{4,6},{5,7},{6,4},{7,5},{8,10},{9,11},{10,... | collective-permute-start | bytes 1179656 | tf_op jit(solution)/shard_map/ppermute | solution.py:346
  25.5 1.2 collective-permute-start.2
  26.6 6.6 %collective-permute-done.f1 = bf16[8,32,768]{2,1,0:T(8,128)(2,1)S(1)} collective-permute-done((bf16[8,32,768]{2,1,0:T(8,128)(2,1)S(1)}, bf16[8,32,768]{2,1,0:T(8,128)(2,1)S(1)}, u32[]{:S(2)}, u32[]{:S(2)}) %collective-permute-start) | collective-permute-done | bytes 393248 | tf_op jit(solution)/shard_map/ppermute | solution.py:346
  34.0 8.7 %collective-permute-done.1.f2 = bf16[8,32,768]{2,1,0:T(8,128)(2,1)S(1)} collective-permute-done((bf16[8,32,768]{2,1,0:T(8,128)(2,1)S(1)}, bf16[8,32,768]{2,1,0:T(8,128)(2,1)S(1)}, u32[]{:S(2)}, u32[]{:S(2)}) %collective-permute-start.1) | collective-permute-done | bytes 393248 | tf_op jit(solution)/shard_map/ppermute | solution.py:346
  44.2 17.8 %all-to-all-done.table_ref = bf16[64,104,128]{2,1,0:T(8,128)(2,1)S(1)} async-done(((bf16[64,104,128]{2,1,0:T(8,128)(2,1)}), bf16[64,104,128]{2,1,0:T(8,128)(2,1)S(1)}, u32[]{:S(2)}, u32[]{:S(2)}) %all-to-all-start) | async-done | bytes 1703968 | tf_op jit(solution)/shard_map/all_to_all | solution.py:332
  61.9 6.0 %pick.1 = (bf16[2048,384]{1,0:T(8,128)(2,1)}, f32[64,1,128]{2,1,0:T(1,128)S(1)}) custom-call(bf16[64,104,128]{2,1,0:T(8,128)(2,1)S(1)} %all-to-all-done.table_ref), custom_call_target="tpu_custom_call" | custom-call | flops 3221225472 | bytes 3145728 | tf_op jit(solution)/shard_map/pick/pallas_call | solution.py:350
  67.9 9.2 %all-to-all-start.1 = ((bf16[256,8,384]{2,1,0:T(8,128)(2,1)}), bf16[256,8,384]{2,1,0:T(8,128)(2,1)S(1)}, u32[]{:S(2)}, u32[]{:S(2)}) async-start(bf16[256,8,384]{2,1,0:T(8,128)(2,1)} %bitcast.18), calls=%async_computation.1 | async-start | bytes 3145728 | tf_op jit(solution)/shard_map/all_to_all | solution.py:368
  77.2 1.7 copy-done.12
  78.8 1.3 copy-done.14
  83.1 3.8 %first.1 = (bf16[8,128,768]{2,1,0:T(8,128)(2,1)S(1)}, bf16[8,128,1536]{2,1,0:T(8,128)(2,1)S(1)}) custom-call(bf16[8,32,768]{2,1,0:T(8,128)(2,1)S(1)} %copy-done.22, bf16[8,32,768]{2,1,0:T(8,128)(2,1)S(1)} %copy-done.24, bf16[8,32,768]{2,1,0:T(8,128)(2,1)S(1)} %copy-done.26, bf16[8,32,768]{2,1,0:T(8,128)(2,1)S(1)} %copy-done.28, ...), custom_call_target="tpu_custom_call" | custom-call | flops 3623878656 | bytes 9830400 | tf_op jit(solution)/shard_map/first/pallas_call | solution.py:374
  86.9 1.6 copy-done.2
  88.6 1.2 copy-done.29
  89.8 29.4 %all-to-all-done.1 = bf16[256,8,384]{2,1,0:T(8,128)(2,1)S(1)} async-done(((bf16[256,8,384]{2,1,0:T(8,128)(2,1)}), bf16[256,8,384]{2,1,0:T(8,128)(2,1)S(1)}, u32[]{:S(2)}, u32[]{:S(2)}) %all-to-all-start.1) | async-done | bytes 1572896 | tf_op jit(solution)/shard_map/all_to_all | solution.py:368
  119.2 7.7 %second.1 = bf16[2,1024,384]{2,1,0:T(8,128)(2,1)} custom-call(bf16[2,1024,384]{2,1,0:T(8,128)(2,1)S(1)} %bitcast.13, bf16[8,128,1536]{2,1,0:T(8,128)(2,1)} %copy-done.2, bf16[768,768]{1,0:T(8,128)(2,1)S(1)} %copy-done.3), custom_call_target="tpu_custom_call" | custom-call | flops 2013265920 | bytes 7471104 | tf_op jit(solution)/shard_map/second/pallas_call | solution.py:393
  126.8 6.7 %all-to-all-start.2 = ((bf16[256,8,384]{2,1,0:T(8,128)(2,1)}), bf16[256,8,384]{2,1,0:T(8,128)(2,1)S(1)}, u32[]{:S(2)}, u32[]{:S(2)}) async-start(bf16[256,8,384]{2,1,0:T(8,128)(2,1)} %bitcast.16), calls=%async_computation.2 | async-start | bytes 3145728 | tf_op jit(solution)/shard_map/all_to_all | solution.py:412
  133.6 1.7 copy-done.13
  135.3 1.4 copy-done.30
  136.7 8.6 %near.1 = (bf16[8,32,768]{2,1,0:T(8,128)(2,1)S(1)}, bf16[8,32,768]{2,1,0:T(8,128)(2,1)S(1)}, bf16[8,32,768]{2,1,0:T(8,128)(2,1)S(1)}, bf16[8,32,768]{2,1,0:T(8,128)(2,1)S(1)}) custom-call(bf16[2,1024,384]{2,1,0:T(8,128)(2,1)S(1)} %bitcast.14, bf16[8,128,768]{2,1,0:T(8,128)(2,1)S(1)} %copy-done.30, bf16[768,1536]{1,0:T(8,128)(2,1)S(1)} %copy-done.13), custom_call_target="tpu_custom_call" | custom-call | flops 3221225472 | bytes 7077888 | tf_op jit(solution)/shard_map/near/pallas_call | solution.py:417
  147.6 27.9 %all-to-all-done.2 = bf16[256,8,384]{2,1,0:T(8,128)(2,1)S(1)} async-done(((bf16[256,8,384]{2,1,0:T(8,128)(2,1)}), bf16[256,8,384]{2,1,0:T(8,128)(2,1)S(1)}, u32[]{:S(2)}, u32[]{:S(2)}) %all-to-all-start.2) | async-done | bytes 1572896 | tf_op jit(solution)/shard_map/all_to_all | solution.py:412
  175.5 5.8 %sum.1 = bf16[2048,384]{1,0:T(8,128)(2,1)} custom-call(s32[1,2048]{1,0:T(1,128)S(1)} %convert_element_type.27.ids_ref, bf16[2048,384]{1,0:T(8,128)(2,1)S(1)} %bitcast.15), custom_call_target="tpu_custom_call" | custom-call | flops 3221225472 | bytes 3145728 | tf_op jit(solution)/shard_map/sum/pallas_call | solution.py:442
  181.3 5.8 %all-to-all-start.3 = ((bf16[64,32,384]{2,1,0:T(8,128)(2,1)}), bf16[64,32,384]{2,1,0:T(8,128)(2,1)}, u32[]{:S(2)}, u32[]{:S(2)}) async-start(bf16[64,32,384]{2,1,0:T(8,128)(2,1)} %bitcast.17), calls=%async_computation.3 | async-start | bytes 3145728 | tf_op jit(solution)/shard_map/all_to_all | solution.py:453
  187.3 1.5 collective-permute-start.3
  190.2 7.4 %collective-permute-done.3.r1 = bf16[8,32,768]{2,1,0:T(8,128)(2,1)S(1)} collective-permute-done((bf16[8,32,768]{2,1,0:T(8,128)(2,1)S(1)}, bf16[8,32,768]{2,1,0:T(8,128)(2,1)S(1)}, u32[]{:S(2)}, u32[]{:S(2)}) %collective-permute-start.3) | collective-permute-done | bytes 393248 | tf_op jit(solution)/shard_map/ppermute | solution.py:440
  198.4 1.9 collective-permute-done.4.r2
  201.1 8.8 %collective-permute-done.5.r3 = bf16[8,32,768]{2,1,0:T(8,128)(2,1)S(1)} collective-permute-done((bf16[8,32,768]{2,1,0:T(8,128)(2,1)S(1)}, bf16[8,32,768]{2,1,0:T(8,128)(2,1)S(1)}, u32[]{:S(2)}, u32[]{:S(2)}) %collective-permute-start.5) | collective-permute-done | bytes 393248 | tf_op jit(solution)/shard_map/ppermute | solution.py:440
  210.7 1.4 copy-done.1
  215.1 1.8 base.1.base_ref
  216.8 9.2 %all-to-all-done.3.far_ref = bf16[64,32,384]{2,1,0:T(8,128)(2,1)} async-done(((bf16[64,32,384]{2,1,0:T(8,128)(2,1)}), bf16[64,32,384]{2,1,0:T(8,128)(2,1)}, u32[]{:S(2)}, u32[]{:S(2)}) %all-to-all-start.3) | async-done | bytes 1572896 | tf_op jit(solution)/shard_map/all_to_all | solution.py:453
  226.0 3.1 %join.1 = bf16[32,32,768]{2,1,0:T(8,128)(2,1)} custom-call(f32[32]{0:T(128)S(1)} %maximum_divide_fusion.recip_ref, bf16[64,32,384]{2,1,0:T(8,128)(2,1)} %all-to-all-done.3.far_ref, f32[32,32,768]{2,1,0:T(8,128)S(1)} %base.1.base_ref), custom_call_target="tpu_custom_call" | custom-call | flops 3145728 | bytes 6291456 | tf_op jit(solution)/shard_map/join/pallas_call | solution.py:466
  (71 shorter events, 15.9 us)
Async XLA Ops:
  7.0 13.3 %copy-start.31 = (s32[32,2]{0,1:T(2,128)S(1)}, s32[32,2]{0,1:T(2,128)}, u32[]{:S(2)}) copy-start(s32[32,2]{0,1:T(2,128)} %param.11) | copy-start | bytes 772
  7.0 13.3 %copy-start = (bf16[1024,768]{1,0:T(8,128)(2,1)S(1)}, bf16[1024,768]{1,0:T(8,128)(2,1)}, u32[]{:S(2)}) copy-start(bf16[1024,768]{1,0:T(8,128)(2,1)} %get-tuple-element.31.normed_ref) | copy-start | bytes 4718596
  7.0 54.9 %all-to-all-start = ((bf16[64,104,128]{2,1,0:T(8,128)(2,1)}), bf16[64,104,128]{2,1,0:T(8,128)(2,1)S(1)}, u32[]{:S(2)}, u32[]{:S(2)}) async-start(bf16[64,104,128]{2,1,0:T(8,128)(2,1)} %get-tuple-element.30), calls=%async_computation | async-start | bytes 3407872 | tf_op jit(solution)/shard_map/all_to_all | solution.py:332
  21.8 11.4 %collective-permute-start = (bf16[8,32,768]{2,1,0:T(8,128)(2,1)S(1)}, bf16[8,32,768]{2,1,0:T(8,128)(2,1)S(1)}, u32[]{:S(2)}, u32[]{:S(2)}) collective-permute-start(bf16[8,32,768]{2,1,0:T(8,128)(2,1)S(1)} %get-tuple-element.33), channel_id=1, source_target_pairs={{0,1},{1,2},{2,3},{3,0},{4,5},{5,6},{6,7},{7,4},{8,9},{9,10},{10,1... | collective-permute-start | bytes 1179656 | tf_op jit(solution)/shard_map/ppermute | solution.py:346
  23.0 19.6 %collective-permute-start.1 = (bf16[8,32,768]{2,1,0:T(8,128)(2,1)S(1)}, bf16[8,32,768]{2,1,0:T(8,128)(2,1)S(1)}, u32[]{:S(2)}, u32[]{:S(2)}) collective-permute-start(bf16[8,32,768]{2,1,0:T(8,128)(2,1)S(1)} %get-tuple-element.34), channel_id=1, source_target_pairs={{0,2},{1,3},{2,0},{3,1},{4,6},{5,7},{6,4},{7,5},{8,10},{9,11},{10,... | collective-permute-start | bytes 1179656 | tf_op jit(solution)/shard_map/ppermute | solution.py:346
  25.5 17.9 %collective-permute-start.2 = (bf16[8,32,768]{2,1,0:T(8,128)(2,1)S(1)}, bf16[8,32,768]{2,1,0:T(8,128)(2,1)S(1)}, u32[]{:S(2)}, u32[]{:S(2)}) collective-permute-start(bf16[8,32,768]{2,1,0:T(8,128)(2,1)S(1)} %get-tuple-element.35), channel_id=1, source_target_pairs={{0,3},{1,0},{2,1},{3,2},{4,7},{5,4},{6,5},{7,6},{8,11},{9,8},{10,9... | collective-permute-start | bytes 1179656 | tf_op jit(solution)/shard_map/ppermute | solution.py:346
  67.9 65.6 %copy-start.10 = (f32[64,1,128]{2,1,0:T(1,128)}, f32[64,1,128]{2,1,0:T(1,128)S(1)}, u32[]{:S(2)}) copy-start(f32[64,1,128]{2,1,0:T(1,128)S(1)} %get-tuple-element.37) | copy-start | bytes 98308
  67.9 9.2 %copy-start.22 = (bf16[8,32,768]{2,1,0:T(8,128)(2,1)S(1)}, bf16[8,32,768]{2,1,0:T(8,128)(2,1)}, u32[]{:S(2)}) copy-start(bf16[8,32,768]{2,1,0:T(8,128)(2,1)} %copy-done.21) | copy-start | bytes 1179652
  67.9 51.2 %all-to-all-start.1 = ((bf16[256,8,384]{2,1,0:T(8,128)(2,1)}), bf16[256,8,384]{2,1,0:T(8,128)(2,1)S(1)}, u32[]{:S(2)}, u32[]{:S(2)}) async-start(bf16[256,8,384]{2,1,0:T(8,128)(2,1)} %bitcast.18), calls=%async_computation.1 | async-start | bytes 3145728 | tf_op jit(solution)/shard_map/all_to_all | solution.py:368
  77.1 1.7 copy-start.12
  78.8 1.3 copy-start.14
  80.1 1.0 copy-start.24
  81.1 1.0 copy-start.26
  82.1 1.0 copy-start.28
  83.1 36.1 %copy-start.3 = (bf16[768,768]{1,0:T(8,128)(2,1)S(1)}, bf16[768,768]{1,0:T(8,128)(2,1)}, u32[]{:S(2)}) copy-start(bf16[768,768]{1,0:T(8,128)(2,1)} %wq_ref.3) | copy-start | bytes 3538948
  86.9 1.6 copy-start.2
  88.6 1.2 copy-start.29
  126.8 48.7 %all-to-all-start.2 = ((bf16[256,8,384]{2,1,0:T(8,128)(2,1)}), bf16[256,8,384]{2,1,0:T(8,128)(2,1)S(1)}, u32[]{:S(2)}, u32[]{:S(2)}) async-start(bf16[256,8,384]{2,1,0:T(8,128)(2,1)} %bitcast.16), calls=%async_computation.2 | async-start | bytes 3145728 | tf_op jit(solution)/shard_map/all_to_all | solution.py:412
  133.6 1.7 copy-start.13
  135.3 1.4 copy-start.30
  181.3 6.0 %copy-start.20 = (bf16[8,32,768]{2,1,0:T(8,128)(2,1)S(1)}, bf16[8,32,768]{2,1,0:T(8,128)(2,1)}, u32[]{:S(2)}) copy-start(bf16[8,32,768]{2,1,0:T(8,128)(2,1)} %copy-done.19) | copy-start | bytes 1179652
  181.3 7.5 %copy-start.18 = (bf16[8,32,768]{2,1,0:T(8,128)(2,1)S(1)}, bf16[8,32,768]{2,1,0:T(8,128)(2,1)}, u32[]{:S(2)}) copy-start(bf16[8,32,768]{2,1,0:T(8,128)(2,1)} %copy-done.17) | copy-start | bytes 1179652
  181.3 8.2 %copy-start.16 = (bf16[8,32,768]{2,1,0:T(8,128)(2,1)S(1)}, bf16[8,32,768]{2,1,0:T(8,128)(2,1)}, u32[]{:S(2)}) copy-start(bf16[8,32,768]{2,1,0:T(8,128)(2,1)} %copy-done.15) | copy-start | bytes 1179652
  181.3 8.5 %copy-start.11 = (f32[64,1,128]{2,1,0:T(1,128)S(1)}, f32[64,1,128]{2,1,0:T(1,128)}, u32[]{:S(2)}) copy-start(f32[64,1,128]{2,1,0:T(1,128)} %copy-done.10) | copy-start | bytes 98308
  181.3 44.7 %all-to-all-start.3 = ((bf16[64,32,384]{2,1,0:T(8,128)(2,1)}), bf16[64,32,384]{2,1,0:T(8,128)(2,1)}, u32[]{:S(2)}, u32[]{:S(2)}) async-start(bf16[64,32,384]{2,1,0:T(8,128)(2,1)} %bitcast.17), calls=%async_computation.3 | async-start | bytes 3145728 | tf_op jit(solution)/shard_map/all_to_all | solution.py:453
  187.3 10.3 %collective-permute-start.3 = (bf16[8,32,768]{2,1,0:T(8,128)(2,1)S(1)}, bf16[8,32,768]{2,1,0:T(8,128)(2,1)S(1)}, u32[]{:S(2)}, u32[]{:S(2)}) collective-permute-start(bf16[8,32,768]{2,1,0:T(8,128)(2,1)S(1)} %copy-done.20), channel_id=1, source_target_pairs={{0,3},{1,0},{2,1},{3,2},{4,7},{5,4},{6,5},{7,6},{8,11},{9,8},{10,9... | collective-permute-start | bytes 1179656 | tf_op jit(solution)/shard_map/ppermute | solution.py:440
  188.8 11.5 %collective-permute-start.4 = (bf16[8,32,768]{2,1,0:T(8,128)(2,1)S(1)}, bf16[8,32,768]{2,1,0:T(8,128)(2,1)S(1)}, u32[]{:S(2)}, u32[]{:S(2)}) collective-permute-start(bf16[8,32,768]{2,1,0:T(8,128)(2,1)S(1)} %copy-done.18), channel_id=1, source_target_pairs={{0,2},{1,3},{2,0},{3,1},{4,6},{5,7},{6,4},{7,5},{8,10},{9,11},{10,... | collective-permute-start | bytes 1179656 | tf_op jit(solution)/shard_map/ppermute | solution.py:440
  189.5 20.4 %collective-permute-start.5 = (bf16[8,32,768]{2,1,0:T(8,128)(2,1)S(1)}, bf16[8,32,768]{2,1,0:T(8,128)(2,1)S(1)}, u32[]{:S(2)}, u32[]{:S(2)}) collective-permute-start(bf16[8,32,768]{2,1,0:T(8,128)(2,1)S(1)} %copy-done.16), channel_id=1, source_target_pairs={{0,1},{1,2},{2,3},{3,0},{4,5},{5,6},{6,7},{7,4},{8,9},{9,10},{10,1... | collective-permute-start | bytes 1179656 | tf_op jit(solution)/shard_map/ppermute | solution.py:440
  210.7 1.4 copy-start.1
  212.1 1.0 copy-start.5
  213.1 1.0 copy-start.7
  214.1 1.0 copy-start.9
  (10 other events, 7.6 us)

commit v4 on v3

--- a/solution.py
+++ b/solution.py
@@ -30,7 +30,7 @@
 
 
 def embed_kernel(
-    x_hbm, w_hbm, gain_hbm, pairs_hbm, normed_hbm, pieces_hbm,
+    img_ref, x_hbm, w_hbm, gain_hbm, pairs_hbm, normed_hbm, pieces_hbm,
     x_scr, w_scr, gain_scr, pairs_scr, normed_scr, pieces_scr, scratch, in_sems, normed_sems, piece_sems,
 ):
     chunks, rows, _ = x_scr.shape
@@ -54,40 +54,59 @@
     second = pairs_scr[1:2, :]
     owner = lax.div(second, images)
     numbers = jnp.concatenate([owner, second - owner * images], axis=0).astype(F32)
-    numbers = jnp.concatenate([numbers, jnp.zeros((6, numbers.shape[1]), F32)], axis=0)
-    numbers = jnp.concatenate([numbers, jnp.zeros((8, 128 - numbers.shape[1]), F32)], axis=1).astype(BF16)
+    count = numbers.shape[1]
+    numbers = jnp.concatenate([numbers, jnp.zeros((6, count), F32)], axis=0)
+    numbers = jnp.concatenate([numbers] * (128 // count), axis=1)
+    place = lax.div(lax.broadcasted_iota(jnp.int32, numbers.shape, 1), count)
+    numbers = jnp.where(place == lax.rem(img_ref[0], 128 // count), numbers, 0.0).astype(BF16)
     for m in range(2 * toks):
         pieces_scr[m, per_half * images:, :] = numbers
     loads[0].wait()
-    stores = []
-    for i in range(chunks):
-        loads[i + 1].wait()
-        at = pl.ds(i * rows, rows)
+
+    def normed_out(i):
+        at = pl.ds(pl.multiple_of(i * rows, rows), rows)
+        return pltpu.make_async_copy(normed_scr.at[at], normed_hbm.at[at], normed_sems.at[i])
+
+    @pl.loop(0, chunks)
+    def _(i):
+        at = pl.ds(pl.multiple_of(i * rows, rows), rows)
+        pltpu.make_async_copy(x_hbm.at[at], x_scr.at[i], in_sems.at[i]).wait()
         e = jnp.dot(x_scr[i], w_scr[...], preferred_element_type=F32)
         c = e - jnp.mean(e, axis=-1, keepdims=True)
         spread = jnp.mean(c * c, axis=-1, keepdims=True)
         n = c * lax.rsqrt(spread + 1e-06) * gain
         normed_scr[at, :] = n.astype(BF16)
-        stores.append(pltpu.make_async_copy(normed_scr.at[at], normed_hbm.at[at], normed_sems.at[i]))
-        stores[-1].start()
+        normed_out(i).start()
         for u in range(rows // toks):
-            to = pl.ds((i * (rows // toks) + u) * pitch, toks)
+            to = pl.ds(pl.multiple_of((i * (rows // toks) + u) * pitch, 8), toks)
             for b in range(width // 128):
                 scratch[b, to, :] = n[u * toks:(u + 1) * toks, b * 128:(b + 1) * 128]
+
     group = 8
-    for h in range(2):
-        for r in range(toks):
-            for b in range(per_half):
-                v = scratch[h * per_half + b, pl.ds(r, images, stride=pitch), :]
-                pieces_scr[h * toks + r, b * images:(b + 1) * images, :] = v.astype(BF16)
-            if r % group == group - 1:
-                first = h * toks + r - group + 1
-                at = pl.ds(first, group)
-                sem = piece_sems.at[first // group]
-                stores.append(pltpu.make_async_copy(pieces_scr.at[at], pieces_hbm.at[at], sem))
-                stores[-1].start()
-    for store in stores:
-        store.wait()
+
+    def outgoing(h, g):
+        at = pl.ds(pl.multiple_of(h * toks + g * group, group), group)
+        sem = piece_sems.at[h * (toks // group) + g]
+        return pltpu.make_async_copy(pieces_scr.at[at], pieces_hbm.at[at], sem)
+
+    @pl.loop(0, toks // group)
+    def _(g):
+        for h in range(2):
+            for u in range(group):
+                r = g * group + u
+                for b in range(per_half):
+                    v = scratch[h * per_half + b, pl.ds(r, images, stride=pitch), :]
+                    pieces_scr[h * toks + r, b * images:(b + 1) * images, :] = v.astype(BF16)
+            outgoing(h, g).start()
+
+    @pl.loop(0, toks // group)
+    def _(g):
+        for h in range(2):
+            outgoing(h, g).wait()
+
+    @pl.loop(0, chunks)
+    def _(i):
+        normed_out(i).wait()
 
 
 def gather_kernel(first_ref, tok_ref, normed_ref, f0, f1, f2, f3):
@@ -105,30 +124,33 @@
     rows, half = out_ref.shape
     blocks = half // 128
     images = (height - 8) // blocks
-    lane = lax.broadcasted_iota(jnp.int32, (images, 128), 1)
-    diagonal = lane == lax.broadcasted_iota(jnp.int32, (images, 128), 0)
-    per_step = rows // images
-    wanted = []
-    for o in range(per_step):
-        top = table_ref[step * per_step + o, blocks * images:, :].astype(F32)
-        number = top[0:1, :] * float(images) + top[1:2, :]
-        ids_ref[o] = number
-        column = jnp.sum(jnp.where(diagonal, number, 0.0), axis=1, keepdims=True)
-        wanted.append(jnp.broadcast_to(column, (images, 128)))
-    wanted = jnp.concatenate(wanted, axis=0)
-    lane = lax.broadcasted_iota(jnp.int32, (rows, 128), 1).astype(F32)
-    hot = [jnp.where(wanted == lane + float(b * 128), 1.0, 0.0).astype(BF16) for b in range(owners * images // 128)]
+
+    table = [table_ref[:, b * images:(b + 1) * images, :].reshape(owners * images, 128) for b in range(blocks)]
+    table = jnp.concatenate(table, axis=1)
+    image = lax.broadcasted_iota(jnp.int32, (owners * images, 128), 0).astype(F32)
+    hot = []
+    for q in range(rows // 128):
+        wanted = jnp.zeros((1, 128), F32)
+        for o in range(128 // images):
+            top = table_ref[step * (rows // images) + q * (128 // images) + o, blocks * images:, :].astype(F32)
+            wanted = wanted + top[0:1, :] * float(images) + top[1:2, :]
+        ids_ref[q] = wanted
+        hot.append(jnp.where(wanted == image, 1.0, 0.0).astype(BF16))
     hot = jnp.concatenate(hot, axis=1)
-    table = [table_ref[:, b * images:(b + 1) * images, :].reshape(owners * images, 128) for b in range(blocks)]
-    out_ref[...] = jnp.dot(hot, jnp.concatenate(table, axis=1), preferred_element_type=F32).astype(BF16)
+    picked = lax.dot_general(table, hot, (((0,), (0,)), ((), ())), preferred_element_type=F32)
+    out_ref[...] = picked.T.astype(BF16)
 
 
 def sum_kernel(ids_ref, rows_ref, out_ref):
     step = pl.program_id(0)
-    images = out_ref.shape[0]
-    image = lax.broadcasted_iota(jnp.int32, (images, ids_ref.shape[1]), 0) + step * images
-    hot = jnp.where(ids_ref[...] == image, 1.0, 0.0).astype(BF16)
-    out_ref[...] = jnp.dot(hot, rows_ref[...], preferred_element_type=F32).astype(BF16)
+    images, half = out_ref.shape
+
+    ids = ids_ref[...]
+    lane = lax.broadcasted_iota(jnp.int32, ids.shape, 1) + step * images
+    hot = [jnp.where(ids == lane + b * 128, 1.0, 0.0).astype(BF16) for b in range(images // 128)]
+    hot = jnp.concatenate(hot, axis=1)
+    total = lax.dot_general(rows_ref[...], hot, (((0,), (0,)), ((), ())), preferred_element_type=F32)
+    out_ref[...] = total.T.astype(BF16)
 
 
 def first_kernel(f0, f1, f2, f3, wq_ref, wkv_ref, q_ref, kv_ref):
@@ -312,7 +334,7 @@
         2 * rows * enc * width,
         2 * rows * (enc + 2 * width) + 2 * enc * width,
         28,
-        in_specs=[anywhere] * 4,
+        in_specs=[smem] + [anywhere] * 4,
         out_specs=[anywhere, anywhere],
         scratch_shapes=[
             pltpu.VMEM((rows // block, block, enc), BF16),
@@ -327,7 +349,7 @@
             pltpu.SemaphoreType.DMA((owners // 8,)),
         ],
         name="embed",
-    )(hbm(tokens.reshape(rows, enc)), hbm(embed), hbm(norm_gain), hbm(pairs.T))
+    )(img.astype(jnp.int32).reshape(1), hbm(tokens.reshape(rows, enc)), hbm(embed), hbm(norm_gain), hbm(pairs.T))
 
     table = lax.all_to_all(pieces, "img", split_axis=0, concat_axis=0, tiled=True)
 
@@ -346,25 +368,25 @@
         firsts[k] = lax.ppermute(firsts[k], "tok", perm)
     table, *firsts = lax.optimization_barrier((table, *firsts))
 
-    step_rows = 512
+    step_rows = 1024
     asked, ids = call(
         pick_kernel,
         [
             pltpu.HBM((total, half), BF16),
-            jax.ShapeDtypeStruct((owners, 1, 128), F32),
+            jax.ShapeDtypeStruct((total // 128, 1, 128), F32),
         ],
         2 * total * all_images * half,
         2 * (total + all_images) * half,
-        16,
+        24,
         grid=(total // step_rows,),
         in_specs=[vmem],
         out_specs=[
             pl.BlockSpec((step_rows, half), lambda i: (i, 0)),
-            pl.BlockSpec((step_rows // count, 1, 128), lambda i: (i, 0, 0)),
+            pl.BlockSpec((step_rows // 128, 1, 128), lambda i: (i, 0, 0)),
         ],
         name="pick",
     )(table)
-    ids = ids[:, 0, :count].astype(jnp.int32).reshape(total)
+    ids = ids.astype(jnp.int32).reshape(total)
     seconds = lax.all_to_all(
         asked.reshape(owners * groups, items, half), ("img", "tok"), split_axis=0, concat_axis=0, tiled=True
     )
@@ -444,12 +466,12 @@
         pltpu.HBM((all_images, half), BF16),
         2 * total * all_images * half,
         2 * (total + all_images) * half,
-        16,
+        20,
         grid=(all_images // step_rows,),
         in_specs=[vmem, vmem],
         out_specs=pl.BlockSpec((step_rows, half), lambda i: (i, 0)),
         name="sum",
-    )(ids.reshape(1, total), returned.reshape(total, half))
+    )(jnp.broadcast_to(ids[:, None], (total, 128)), returned.reshape(total, half))
     far = lax.all_to_all(
         sums.reshape(owners, images, half), "img", split_axis=0, concat_axis=0, tiled=True
     )

time: 230 us -> 228 us (level)
  local copies, waits for them, and re-layouts: 24 us -> 18.8 us
  waiting for transfers between devices: 118 us -> 123 us
  Pallas kernels: 44.3 us -> 41.6 us
    unnamed x64 -> x50, local copies, waits for them, and re-layouts: 23.8 us -> 18.5 us
    all_to_all x1, waiting for transfers between devices: 9.22 us -> 13.1 us  [body(): lax.all_to_all(sums.reshape(owners, images, half), 'img', split_axis=0, c...]
  transfers between devices with their start and end apart: 10 -> 10, of which waited for: 9 -> 9; matrix products, arithmetic and copies ran while one was open for 0% -> 0% of each run, Pallas kernels for 6% -> 7%
where the time goes in v4:
time: 228 us; the launch traced here: 227 us
  waiting for transfers between devices  123 us (54%)
  starting transfers between devices  42.2 us (19%)
  Pallas kernels  41.6 us (18%)
  local copies, waits for them, and re-layouts  18.8 us (8%)
    all_to_all x1, waiting for transfers between devices, body(): lax.all_to_all(asked.reshape(owners * groups, items, half), ('img', 'tok'...  29.4 us
    all_to_all x1, waiting for transfers between devices, body(): lax.all_to_all(back.reshape(owners * groups, items, half), ('img', 'tok')...  28.1 us
    ppermute x3, waiting for transfers between devices, body(): near[k] = lax.ppermute(near[k], 'tok', perm)  19.7 us
    unnamed x50, local copies, waits for them, and re-layouts  18.5 us
    all_to_all x1, waiting for transfers between devices, body(): lax.all_to_all(pieces, 'img', split_axis=0, concat_axis=0, tiled=True)  17.8 us
    ppermute x3, waiting for transfers between devices, body(): firsts[k] = lax.ppermute(firsts[k], 'tok', perm)  15.3 us
    all_to_all x1, starting transfers between devices, body(): lax.all_to_all(pieces, 'img', split_axis=0, concat_axis=0, tiled=True)  13.3 us
    all_to_all x1, waiting for transfers between devices, body(): lax.all_to_all(sums.reshape(owners, images, half), 'img', split_axis=0, c...  13.1 us
  transfers between devices with their start and end apart: 10, of which 9 were waited for; matrix products, arithmetic and copies ran while one was open for 0% of the time, Pallas kernels for 7%

profile of v4, /device:TPU:1, one launch (start us, length us, event | category | flops | bytes accessed | tf_op | source)
XLA Modules:
  0.0 226.9 jit_solution(1542990475960195067)
XLA Ops:
  0.0 6.5 %embed.1 = (bf16[1024,768]{1,0:T(8,128)(2,1)}, bf16[64,104,128]{2,1,0:T(8,128)(2,1)}) custom-call(s32[1]{0:T(128)} %bitcast.img_ref, bf16[1024,1024]{1,0:T(8,128)(2,1)} %bitcast.23, bf16[1024,768]{1,0:T(8,128)(2,1)} %w_hbm.1, f32[768]{0:T(1024)} %gain_hbm.1, s32[2,32]{1,0:T(2,128)} %bitcast.22), custom_call_target="tpu_custom_call" | custom-call | flops 1610612736 | bytes 6815744 | tf_op jit(solution)/shard_map/embed/pallas_call | solution.py:328
  6.6 13.3 %all-to-all-start = ((bf16[64,104,128]{2,1,0:T(8,128)(2,1)}), bf16[64,104,128]{2,1,0:T(8,128)(2,1)S(1)}, u32[]{:S(2)}, u32[]{:S(2)}) async-start(bf16[64,104,128]{2,1,0:T(8,128)(2,1)} %get-tuple-element.30), calls=%async_computation | async-start | bytes 3407872 | tf_op jit(solution)/shard_map/all_to_all | solution.py:354
  21.3 1.2 collective-permute-start
  22.5 2.4 %collective-permute-start.1 = (bf16[8,32,768]{2,1,0:T(8,128)(2,1)S(1)}, bf16[8,32,768]{2,1,0:T(8,128)(2,1)S(1)}, u32[]{:S(2)}, u32[]{:S(2)}) collective-permute-start(bf16[8,32,768]{2,1,0:T(8,128)(2,1)S(1)} %get-tuple-element.34), channel_id=1, source_target_pairs={{0,2},{1,3},{2,0},{3,1},{4,6},{5,7},{6,4},{7,5},{8,10},{9,11},{10,... | collective-permute-start | bytes 1179656 | tf_op jit(solution)/shard_map/ppermute | solution.py:368
  25.0 1.2 collective-permute-start.2
  26.1 6.6 %collective-permute-done.f1 = bf16[8,32,768]{2,1,0:T(8,128)(2,1)S(1)} collective-permute-done((bf16[8,32,768]{2,1,0:T(8,128)(2,1)S(1)}, bf16[8,32,768]{2,1,0:T(8,128)(2,1)S(1)}, u32[]{:S(2)}, u32[]{:S(2)}) %collective-permute-start) | collective-permute-done | bytes 393248 | tf_op jit(solution)/shard_map/ppermute | solution.py:368
  33.5 8.7 %collective-permute-done.1.f2 = bf16[8,32,768]{2,1,0:T(8,128)(2,1)S(1)} collective-permute-done((bf16[8,32,768]{2,1,0:T(8,128)(2,1)S(1)}, bf16[8,32,768]{2,1,0:T(8,128)(2,1)S(1)}, u32[]{:S(2)}, u32[]{:S(2)}) %collective-permute-start.1) | collective-permute-done | bytes 393248 | tf_op jit(solution)/shard_map/ppermute | solution.py:368
  43.7 17.8 %all-to-all-done.table_ref = bf16[64,104,128]{2,1,0:T(8,128)(2,1)S(1)} async-done(((bf16[64,104,128]{2,1,0:T(8,128)(2,1)}), bf16[64,104,128]{2,1,0:T(8,128)(2,1)S(1)}, u32[]{:S(2)}, u32[]{:S(2)}) %all-to-all-start) | async-done | bytes 1703968 | tf_op jit(solution)/shard_map/all_to_all | solution.py:354
  61.5 4.7 %pick.1 = (bf16[2048,384]{1,0:T(8,128)(2,1)}, f32[16,1,128]{2,1,0:T(1,128)S(1)}) custom-call(bf16[64,104,128]{2,1,0:T(8,128)(2,1)S(1)} %all-to-all-done.table_ref), custom_call_target="tpu_custom_call" | custom-call | flops 3221225472 | bytes 3145728 | tf_op jit(solution)/shard_map/pick/pallas_call | solution.py:372
  66.1 9.2 %all-to-all-start.1 = ((bf16[256,8,384]{2,1,0:T(8,128)(2,1)}), bf16[256,8,384]{2,1,0:T(8,128)(2,1)S(1)}, u32[]{:S(2)}, u32[]{:S(2)}) async-start(bf16[256,8,384]{2,1,0:T(8,128)(2,1)} %bitcast.19), calls=%async_computation.1 | async-start | bytes 3145728 | tf_op jit(solution)/shard_map/all_to_all | solution.py:390
  75.3 1.7 copy-done.4
  77.0 1.3 copy-done.6
  81.2 3.8 %first.1 = (bf16[8,128,768]{2,1,0:T(8,128)(2,1)S(1)}, bf16[8,128,1536]{2,1,0:T(8,128)(2,1)S(1)}) custom-call(bf16[8,32,768]{2,1,0:T(8,128)(2,1)S(1)} %copy-done.12, bf16[8,32,768]{2,1,0:T(8,128)(2,1)S(1)} %copy-done.16, bf16[8,32,768]{2,1,0:T(8,128)(2,1)S(1)} %copy-done.18, bf16[8,32,768]{2,1,0:T(8,128)(2,1)S(1)} %copy-done.20, ...), custom_call_target="tpu_custom_call" | custom-call | flops 3623878656 | bytes 9830400 | tf_op jit(solution)/shard_map/first/pallas_call | solution.py:396
  85.1 1.6 copy-done.2
  86.7 1.2 copy-done.21
  87.9 29.4 %all-to-all-done.1 = bf16[256,8,384]{2,1,0:T(8,128)(2,1)S(1)} async-done(((bf16[256,8,384]{2,1,0:T(8,128)(2,1)}), bf16[256,8,384]{2,1,0:T(8,128)(2,1)S(1)}, u32[]{:S(2)}, u32[]{:S(2)}) %all-to-all-start.1) | async-done | bytes 1572896 | tf_op jit(solution)/shard_map/all_to_all | solution.py:390
  117.3 7.7 %second.1 = bf16[2,1024,384]{2,1,0:T(8,128)(2,1)} custom-call(bf16[2,1024,384]{2,1,0:T(8,128)(2,1)S(1)} %bitcast.14, bf16[8,128,1536]{2,1,0:T(8,128)(2,1)} %copy-done.2, bf16[768,768]{1,0:T(8,128)(2,1)S(1)} %copy-done.3), custom_call_target="tpu_custom_call" | custom-call | flops 2013265920 | bytes 7471104 | tf_op jit(solution)/shard_map/second/pallas_call | solution.py:415
  125.0 6.7 %all-to-all-start.2 = ((bf16[256,8,384]{2,1,0:T(8,128)(2,1)}), bf16[256,8,384]{2,1,0:T(8,128)(2,1)S(1)}, u32[]{:S(2)}, u32[]{:S(2)}) async-start(bf16[256,8,384]{2,1,0:T(8,128)(2,1)} %bitcast.17), calls=%async_computation.2 | async-start | bytes 3145728 | tf_op jit(solution)/shard_map/all_to_all | solution.py:434
  131.7 1.7 copy-done.5
  133.4 1.4 copy-done.22
  134.8 8.6 %near.1 = (bf16[8,32,768]{2,1,0:T(8,128)(2,1)S(1)}, bf16[8,32,768]{2,1,0:T(8,128)(2,1)S(1)}, bf16[8,32,768]{2,1,0:T(8,128)(2,1)S(1)}, bf16[8,32,768]{2,1,0:T(8,128)(2,1)S(1)}) custom-call(bf16[2,1024,384]{2,1,0:T(8,128)(2,1)S(1)} %bitcast.15, bf16[8,128,768]{2,1,0:T(8,128)(2,1)S(1)} %copy-done.22, bf16[768,1536]{1,0:T(8,128)(2,1)S(1)} %copy-done.5), custom_call_target="tpu_custom_call" | custom-call | flops 3221225472 | bytes 7077888 | tf_op jit(solution)/shard_map/near/pallas_call | solution.py:439
  145.6 28.1 %all-to-all-done.2 = bf16[256,8,384]{2,1,0:T(8,128)(2,1)S(1)} async-done(((bf16[256,8,384]{2,1,0:T(8,128)(2,1)}), bf16[256,8,384]{2,1,0:T(8,128)(2,1)S(1)}, u32[]{:S(2)}, u32[]{:S(2)}) %all-to-all-start.2) | async-done | bytes 1572896 | tf_op jit(solution)/shard_map/all_to_all | solution.py:434
  174.0 4.9 %sum.1 = bf16[2048,384]{1,0:T(8,128)(2,1)} custom-call(s32[2048,128]{1,0:T(8,128)S(1)} %broadcast_in_dim.2.ids_ref, bf16[2048,384]{1,0:T(8,128)(2,1)S(1)} %bitcast.16), custom_call_target="tpu_custom_call" | custom-call | flops 3221225472 | bytes 3145728 | tf_op jit(solution)/shard_map/sum/pallas_call | solution.py:464
  179.0 5.8 %all-to-all-start.3 = ((bf16[64,32,384]{2,1,0:T(8,128)(2,1)}), bf16[64,32,384]{2,1,0:T(8,128)(2,1)}, u32[]{:S(2)}, u32[]{:S(2)}) async-start(bf16[64,32,384]{2,1,0:T(8,128)(2,1)} %bitcast.18), calls=%async_computation.3 | async-start | bytes 3145728 | tf_op jit(solution)/shard_map/all_to_all | solution.py:475
  184.8 1.5 collective-permute-start.3
  187.7 7.5 %collective-permute-done.3.r1 = bf16[8,32,768]{2,1,0:T(8,128)(2,1)S(1)} collective-permute-done((bf16[8,32,768]{2,1,0:T(8,128)(2,1)S(1)}, bf16[8,32,768]{2,1,0:T(8,128)(2,1)S(1)}, u32[]{:S(2)}, u32[]{:S(2)}) %collective-permute-start.3) | collective-permute-done | bytes 393248 | tf_op jit(solution)/shard_map/ppermute | solution.py:462
  195.1 2.7 %collective-permute-done.4.r2 = bf16[8,32,768]{2,1,0:T(8,128)(2,1)S(1)} collective-permute-done((bf16[8,32,768]{2,1,0:T(8,128)(2,1)S(1)}, bf16[8,32,768]{2,1,0:T(8,128)(2,1)S(1)}, u32[]{:S(2)}, u32[]{:S(2)}) %collective-permute-start.4) | collective-permute-done | bytes 393248 | tf_op jit(solution)/shard_map/ppermute | solution.py:462
  197.8 9.6 %collective-permute-done.5.r3 = bf16[8,32,768]{2,1,0:T(8,128)(2,1)S(1)} collective-permute-done((bf16[8,32,768]{2,1,0:T(8,128)(2,1)S(1)}, bf16[8,32,768]{2,1,0:T(8,128)(2,1)S(1)}, u32[]{:S(2)}, u32[]{:S(2)}) %collective-permute-start.5) | collective-permute-done | bytes 393248 | tf_op jit(solution)/shard_map/ppermute | solution.py:462
  207.4 1.4 copy-done.1
  208.8 1.8 base.1.base_ref
  210.5 13.1 %all-to-all-done.3.far_ref = bf16[64,32,384]{2,1,0:T(8,128)(2,1)} async-done(((bf16[64,32,384]{2,1,0:T(8,128)(2,1)}), bf16[64,32,384]{2,1,0:T(8,128)(2,1)}, u32[]{:S(2)}, u32[]{:S(2)}) %all-to-all-start.3) | async-done | bytes 1572896 | tf_op jit(solution)/shard_map/all_to_all | solution.py:475
  223.7 3.1 %join.1 = bf16[32,32,768]{2,1,0:T(8,128)(2,1)} custom-call(f32[32]{0:T(128)S(1)} %maximum_divide_fusion.recip_ref, bf16[64,32,384]{2,1,0:T(8,128)(2,1)} %all-to-all-done.3.far_ref, f32[32,32,768]{2,1,0:T(8,128)S(1)} %base.1.base_ref), custom_call_target="tpu_custom_call" | custom-call | flops 3145728 | bytes 6291456 | tf_op jit(solution)/shard_map/join/pallas_call | solution.py:488
  (54 shorter events, 10.6 us)
Async XLA Ops:
  6.5 13.3 %copy-start.23 = (s32[32,2]{0,1:T(2,128)S(1)}, s32[32,2]{0,1:T(2,128)}, u32[]{:S(2)}) copy-start(s32[32,2]{0,1:T(2,128)} %param.11) | copy-start | bytes 772
  6.5 13.3 %copy-start = (bf16[1024,768]{1,0:T(8,128)(2,1)S(1)}, bf16[1024,768]{1,0:T(8,128)(2,1)}, u32[]{:S(2)}) copy-start(bf16[1024,768]{1,0:T(8,128)(2,1)} %get-tuple-element.31.normed_ref) | copy-start | bytes 4718596
  6.6 54.9 %all-to-all-start = ((bf16[64,104,128]{2,1,0:T(8,128)(2,1)}), bf16[64,104,128]{2,1,0:T(8,128)(2,1)S(1)}, u32[]{:S(2)}, u32[]{:S(2)}) async-start(bf16[64,104,128]{2,1,0:T(8,128)(2,1)} %get-tuple-element.30), calls=%async_computation | async-start | bytes 3407872 | tf_op jit(solution)/shard_map/all_to_all | solution.py:354
  21.3 11.4 %collective-permute-start = (bf16[8,32,768]{2,1,0:T(8,128)(2,1)S(1)}, bf16[8,32,768]{2,1,0:T(8,128)(2,1)S(1)}, u32[]{:S(2)}, u32[]{:S(2)}) collective-permute-start(bf16[8,32,768]{2,1,0:T(8,128)(2,1)S(1)} %get-tuple-element.33), channel_id=1, source_target_pairs={{0,1},{1,2},{2,3},{3,0},{4,5},{5,6},{6,7},{7,4},{8,9},{9,10},{10,1... | collective-permute-start | bytes 1179656 | tf_op jit(solution)/shard_map/ppermute | solution.py:368
  22.5 19.6 %collective-permute-start.1 = (bf16[8,32,768]{2,1,0:T(8,128)(2,1)S(1)}, bf16[8,32,768]{2,1,0:T(8,128)(2,1)S(1)}, u32[]{:S(2)}, u32[]{:S(2)}) collective-permute-start(bf16[8,32,768]{2,1,0:T(8,128)(2,1)S(1)} %get-tuple-element.34), channel_id=1, source_target_pairs={{0,2},{1,3},{2,0},{3,1},{4,6},{5,7},{6,4},{7,5},{8,10},{9,11},{10,... | collective-permute-start | bytes 1179656 | tf_op jit(solution)/shard_map/ppermute | solution.py:368
  25.0 17.9 %collective-permute-start.2 = (bf16[8,32,768]{2,1,0:T(8,128)(2,1)S(1)}, bf16[8,32,768]{2,1,0:T(8,128)(2,1)S(1)}, u32[]{:S(2)}, u32[]{:S(2)}) collective-permute-start(bf16[8,32,768]{2,1,0:T(8,128)(2,1)S(1)} %get-tuple-element.35), channel_id=1, source_target_pairs={{0,3},{1,0},{2,1},{3,2},{4,7},{5,4},{6,5},{7,6},{8,11},{9,8},{10,9... | collective-permute-start | bytes 1179656 | tf_op jit(solution)/shard_map/ppermute | solution.py:368
  32.8 0.8 copy-start.15
  42.9 0.8 copy-start.19
  66.1 9.2 %copy-start.12 = (bf16[8,32,768]{2,1,0:T(8,128)(2,1)S(1)}, bf16[8,32,768]{2,1,0:T(8,128)(2,1)}, u32[]{:S(2)}) copy-start(bf16[8,32,768]{2,1,0:T(8,128)(2,1)} %copy-done.11) | copy-start | bytes 1179652
  66.1 51.2 %all-to-all-start.1 = ((bf16[256,8,384]{2,1,0:T(8,128)(2,1)}), bf16[256,8,384]{2,1,0:T(8,128)(2,1)S(1)}, u32[]{:S(2)}, u32[]{:S(2)}) async-start(bf16[256,8,384]{2,1,0:T(8,128)(2,1)} %bitcast.19), calls=%async_computation.1 | async-start | bytes 3145728 | tf_op jit(solution)/shard_map/all_to_all | solution.py:390
  75.3 1.7 copy-start.4
  77.0 1.3 copy-start.6
  78.3 1.0 copy-start.16
  79.3 1.0 copy-start.18
  80.3 1.0 copy-start.20
  81.2 36.1 %copy-start.3 = (bf16[768,768]{1,0:T(8,128)(2,1)S(1)}, bf16[768,768]{1,0:T(8,128)(2,1)}, u32[]{:S(2)}) copy-start(bf16[768,768]{1,0:T(8,128)(2,1)} %wq_ref.3) | copy-start | bytes 3538948
  85.1 1.6 copy-start.2
  86.7 1.2 copy-start.21
  125.0 48.7 %all-to-all-start.2 = ((bf16[256,8,384]{2,1,0:T(8,128)(2,1)}), bf16[256,8,384]{2,1,0:T(8,128)(2,1)S(1)}, u32[]{:S(2)}, u32[]{:S(2)}) async-start(bf16[256,8,384]{2,1,0:T(8,128)(2,1)} %bitcast.17), calls=%async_computation.2 | async-start | bytes 3145728 | tf_op jit(solution)/shard_map/all_to_all | solution.py:434
  131.7 1.7 copy-start.5
  133.4 1.4 copy-start.22
  143.3 0.8 copy-start.7
  144.9 0.7 copy-start.13
  179.0 5.8 %copy-start.24 = (s32[32,2]{0,1:T(2,128)S(1)}, s32[32,2]{0,1:T(2,128)}, u32[]{:S(2)}) copy-start(s32[32,2]{0,1:T(2,128)} %param.11) | copy-start | bytes 772
  179.0 5.8 %copy-start.14 = (bf16[8,32,768]{2,1,0:T(8,128)(2,1)S(1)}, bf16[8,32,768]{2,1,0:T(8,128)(2,1)}, u32[]{:S(2)}) copy-start(bf16[8,32,768]{2,1,0:T(8,128)(2,1)} %copy-done.13) | copy-start | bytes 1179652
  179.0 7.3 %copy-start.10 = (bf16[8,32,768]{2,1,0:T(8,128)(2,1)S(1)}, bf16[8,32,768]{2,1,0:T(8,128)(2,1)}, u32[]{:S(2)}) copy-start(bf16[8,32,768]{2,1,0:T(8,128)(2,1)} %copy-done.9) | copy-start | bytes 1179652
  179.0 8.0 %copy-start.8 = (bf16[8,32,768]{2,1,0:T(8,128)(2,1)S(1)}, bf16[8,32,768]{2,1,0:T(8,128)(2,1)}, u32[]{:S(2)}) copy-start(bf16[8,32,768]{2,1,0:T(8,128)(2,1)} %copy-done.7) | copy-start | bytes 1179652
  179.0 44.7 %all-to-all-start.3 = ((bf16[64,32,384]{2,1,0:T(8,128)(2,1)}), bf16[64,32,384]{2,1,0:T(8,128)(2,1)}, u32[]{:S(2)}, u32[]{:S(2)}) async-start(bf16[64,32,384]{2,1,0:T(8,128)(2,1)} %bitcast.18), calls=%async_computation.3 | async-start | bytes 3145728 | tf_op jit(solution)/shard_map/all_to_all | solution.py:475
  184.8 10.3 %collective-permute-start.3 = (bf16[8,32,768]{2,1,0:T(8,128)(2,1)S(1)}, bf16[8,32,768]{2,1,0:T(8,128)(2,1)S(1)}, u32[]{:S(2)}, u32[]{:S(2)}) collective-permute-start(bf16[8,32,768]{2,1,0:T(8,128)(2,1)S(1)} %copy-done.14), channel_id=1, source_target_pairs={{0,3},{1,0},{2,1},{3,2},{4,7},{5,4},{6,5},{7,6},{8,11},{9,8},{10,9... | collective-permute-start | bytes 1179656 | tf_op jit(solution)/shard_map/ppermute | solution.py:462
  186.3 11.5 %collective-permute-start.4 = (bf16[8,32,768]{2,1,0:T(8,128)(2,1)S(1)}, bf16[8,32,768]{2,1,0:T(8,128)(2,1)S(1)}, u32[]{:S(2)}, u32[]{:S(2)}) collective-permute-start(bf16[8,32,768]{2,1,0:T(8,128)(2,1)S(1)} %copy-done.10), channel_id=1, source_target_pairs={{0,2},{1,3},{2,0},{3,1},{4,6},{5,7},{6,4},{7,5},{8,10},{9,11},{10,... | collective-permute-start | bytes 1179656 | tf_op jit(solution)/shard_map/ppermute | solution.py:462
  186.9 20.4 %collective-permute-start.5 = (bf16[8,32,768]{2,1,0:T(8,128)(2,1)S(1)}, bf16[8,32,768]{2,1,0:T(8,128)(2,1)S(1)}, u32[]{:S(2)}, u32[]{:S(2)}) collective-permute-start(bf16[8,32,768]{2,1,0:T(8,128)(2,1)S(1)} %copy-done.8), channel_id=1, source_target_pairs={{0,1},{1,2},{2,3},{3,0},{4,5},{5,6},{6,7},{7,4},{8,9},{9,10},{10,1... | collective-permute-start | bytes 1179656 | tf_op jit(solution)/shard_map/ppermute | solution.py:462
  207.4 1.4 copy-start.1
  (3 other events, 2.2 us)

commit v5 on v4

--- a/solution.py
+++ b/solution.py
@@ -198,7 +198,7 @@
             x_scr[j * toks:(j + 1) * toks, b * 128:(b + 1) * 128] = rows.astype(BF16)
 
 
-def second_kernel(x_ref, kv_ref, wq_ref, back_ref, q_scr, o_scr):
+def second_kernel(x_ref, kv_ref, wq_ref, back_hbm, q_scr, o_scr, back_scr, sems):
     step = pl.program_id(0)
     steps = pl.num_programs(0)
     lane_blocks, rows, _ = q_scr.shape
@@ -226,9 +226,18 @@
 
     @pl.when(step == steps - 1)
     def _():
-        for b in range(lane_blocks):
-            h, at = divmod(b, per_half)
-            back_ref[h, :, at * 128:(at + 1) * 128] = o_scr[b].astype(BF16)
+        stores = []
+        for h in range(2):
+            for q in range(2):
+                rows_at = pl.ds(q * (rows // 2), rows // 2)
+                for at in range(per_half):
+                    piece = o_scr[h * per_half + at, rows_at, :].astype(BF16)
+                    back_scr[h, rows_at, at * 128:(at + 1) * 128] = piece
+                sem = sems.at[h * 2 + q]
+                stores.append(pltpu.make_async_copy(back_scr.at[h, rows_at], back_hbm.at[h, rows_at], sem))
+                stores[-1].start()
+        for store in stores:
+            store.wait()
 
 
 def near_kernel(x_ref, q_ref, wkv_ref, g0, g1, g2, g3, scratch, x_scr, kv_scr):
@@ -418,16 +427,18 @@
         2 * pair_rows * width * width + 8 * pair_rows * whole_toks * width,
         2 * pair_rows * width * 4 + 2 * width * width,
         28,
-        grid=(items // 2,),
+        grid=(items // 4,),
         in_specs=[
             vmem,
-            pl.BlockSpec((2, whole_toks, 2 * width), lambda j: (j, 0, 0)),
+            pl.BlockSpec((4, whole_toks, 2 * width), lambda j: (j, 0, 0)),
             vmem,
         ],
-        out_specs=whole(2, pair_rows, half),
+        out_specs=anywhere,
         scratch_shapes=[
             pltpu.VMEM((width // 128, pair_rows, 128), F32),
             pltpu.VMEM((width // 128, pair_rows, 128), F32),
+            pltpu.VMEM((2, pair_rows, half), BF16),
+            pltpu.SemaphoreType.DMA((4,)),
         ],
         name="second",
     )(seconds, hbm(kv_second), wq_second)

time: 228 us -> 227 us (level)
  no operation moved by 1% of the time
where the time goes in v5:
time: 227 us; the launch traced here: 226 us
  waiting for transfers between devices  123 us (54%)
  starting transfers between devices  42.4 us (19%)
  Pallas kernels  41.1 us (18%)
  local copies, waits for them, and re-layouts  18.8 us (8%)
    all_to_all x1, waiting for transfers between devices, body(): lax.all_to_all(asked.reshape(owners * groups, items, half), ('img', 'tok'...  29.4 us
    all_to_all x1, waiting for transfers between devices, body(): lax.all_to_all(back.reshape(owners * groups, items, half), ('img', 'tok')...  28.1 us
    ppermute x3, waiting for transfers between devices, body(): near[k] = lax.ppermute(near[k], 'tok', perm)  19.7 us
    unnamed x50, local copies, waits for them, and re-layouts  18.5 us
    all_to_all x1, waiting for transfers between devices, body(): lax.all_to_all(pieces, 'img', split_axis=0, concat_axis=0, tiled=True)  17.8 us
    ppermute x3, waiting for transfers between devices, body(): firsts[k] = lax.ppermute(firsts[k], 'tok', perm)  15.3 us
    all_to_all x1, starting transfers between devices, body(): lax.all_to_all(pieces, 'img', split_axis=0, concat_axis=0, tiled=True)  13.3 us
    all_to_all x1, waiting for transfers between devices, body(): lax.all_to_all(sums.reshape(owners, images, half), 'img', split_axis=0, c...  12.9 us
  transfers between devices with their start and end apart: 10, of which 9 were waited for; matrix products, arithmetic and copies ran while one was open for 0% of the time, Pallas kernels for 7%

profile of v5, /device:TPU:1, one launch (start us, length us, event | category | flops | bytes accessed | tf_op | source)
XLA Modules:
  0.0 226.4 jit_solution(17533540442042590160)
XLA Ops:
  0.0 6.5 %embed.1 = (bf16[1024,768]{1,0:T(8,128)(2,1)}, bf16[64,104,128]{2,1,0:T(8,128)(2,1)}) custom-call(s32[1]{0:T(128)} %bitcast.img_ref, bf16[1024,1024]{1,0:T(8,128)(2,1)} %bitcast.23, bf16[1024,768]{1,0:T(8,128)(2,1)} %w_hbm.1, f32[768]{0:T(1024)} %gain_hbm.1, s32[2,32]{1,0:T(2,128)} %bitcast.22), custom_call_target="tpu_custom_call" | custom-call | flops 1610612736 | bytes 6815744 | tf_op jit(solution)/shard_map/embed/pallas_call | solution.py:337
  6.6 13.3 %all-to-all-start = ((bf16[64,104,128]{2,1,0:T(8,128)(2,1)}), bf16[64,104,128]{2,1,0:T(8,128)(2,1)S(1)}, u32[]{:S(2)}, u32[]{:S(2)}) async-start(bf16[64,104,128]{2,1,0:T(8,128)(2,1)} %get-tuple-element.30), calls=%async_computation | async-start | bytes 3407872 | tf_op jit(solution)/shard_map/all_to_all | solution.py:363
  21.3 1.2 collective-permute-start
  22.5 2.4 %collective-permute-start.1 = (bf16[8,32,768]{2,1,0:T(8,128)(2,1)S(1)}, bf16[8,32,768]{2,1,0:T(8,128)(2,1)S(1)}, u32[]{:S(2)}, u32[]{:S(2)}) collective-permute-start(bf16[8,32,768]{2,1,0:T(8,128)(2,1)S(1)} %get-tuple-element.34), channel_id=1, source_target_pairs={{0,2},{1,3},{2,0},{3,1},{4,6},{5,7},{6,4},{7,5},{8,10},{9,11},{10,... | collective-permute-start | bytes 1179656 | tf_op jit(solution)/shard_map/ppermute | solution.py:377
  25.0 1.2 collective-permute-start.2
  26.1 6.6 %collective-permute-done.f1 = bf16[8,32,768]{2,1,0:T(8,128)(2,1)S(1)} collective-permute-done((bf16[8,32,768]{2,1,0:T(8,128)(2,1)S(1)}, bf16[8,32,768]{2,1,0:T(8,128)(2,1)S(1)}, u32[]{:S(2)}, u32[]{:S(2)}) %collective-permute-start) | collective-permute-done | bytes 393248 | tf_op jit(solution)/shard_map/ppermute | solution.py:377
  33.5 8.7 %collective-permute-done.1.f2 = bf16[8,32,768]{2,1,0:T(8,128)(2,1)S(1)} collective-permute-done((bf16[8,32,768]{2,1,0:T(8,128)(2,1)S(1)}, bf16[8,32,768]{2,1,0:T(8,128)(2,1)S(1)}, u32[]{:S(2)}, u32[]{:S(2)}) %collective-permute-start.1) | collective-permute-done | bytes 393248 | tf_op jit(solution)/shard_map/ppermute | solution.py:377
  43.7 17.8 %all-to-all-done.table_ref = bf16[64,104,128]{2,1,0:T(8,128)(2,1)S(1)} async-done(((bf16[64,104,128]{2,1,0:T(8,128)(2,1)}), bf16[64,104,128]{2,1,0:T(8,128)(2,1)S(1)}, u32[]{:S(2)}, u32[]{:S(2)}) %all-to-all-start) | async-done | bytes 1703968 | tf_op jit(solution)/shard_map/all_to_all | solution.py:363
  61.5 4.7 %pick.1 = (bf16[2048,384]{1,0:T(8,128)(2,1)}, f32[16,1,128]{2,1,0:T(1,128)S(1)}) custom-call(bf16[64,104,128]{2,1,0:T(8,128)(2,1)S(1)} %all-to-all-done.table_ref), custom_call_target="tpu_custom_call" | custom-call | flops 3221225472 | bytes 3145728 | tf_op jit(solution)/shard_map/pick/pallas_call | solution.py:381
  66.1 9.2 %all-to-all-start.1 = ((bf16[256,8,384]{2,1,0:T(8,128)(2,1)}), bf16[256,8,384]{2,1,0:T(8,128)(2,1)S(1)}, u32[]{:S(2)}, u32[]{:S(2)}) async-start(bf16[256,8,384]{2,1,0:T(8,128)(2,1)} %bitcast.19), calls=%async_computation.1 | async-start | bytes 3145728 | tf_op jit(solution)/shard_map/all_to_all | solution.py:399
  75.3 1.7 copy-done.4
  77.0 1.3 copy-done.6
  81.2 3.8 %first.1 = (bf16[8,128,768]{2,1,0:T(8,128)(2,1)S(1)}, bf16[8,128,1536]{2,1,0:T(8,128)(2,1)S(1)}) custom-call(bf16[8,32,768]{2,1,0:T(8,128)(2,1)S(1)} %copy-done.12, bf16[8,32,768]{2,1,0:T(8,128)(2,1)S(1)} %copy-done.16, bf16[8,32,768]{2,1,0:T(8,128)(2,1)S(1)} %copy-done.18, bf16[8,32,768]{2,1,0:T(8,128)(2,1)S(1)} %copy-done.20, ...), custom_call_target="tpu_custom_call" | custom-call | flops 3623878656 | bytes 9830400 | tf_op jit(solution)/shard_map/first/pallas_call | solution.py:405
  85.1 1.6 copy-done.2
  86.7 1.2 copy-done.21
  87.9 29.4 %all-to-all-done.1 = bf16[256,8,384]{2,1,0:T(8,128)(2,1)S(1)} async-done(((bf16[256,8,384]{2,1,0:T(8,128)(2,1)}), bf16[256,8,384]{2,1,0:T(8,128)(2,1)S(1)}, u32[]{:S(2)}, u32[]{:S(2)}) %all-to-all-start.1) | async-done | bytes 1572896 | tf_op jit(solution)/shard_map/all_to_all | solution.py:399
  117.3 7.1 %second.1 = bf16[2,1024,384]{2,1,0:T(8,128)(2,1)} custom-call(bf16[2,1024,384]{2,1,0:T(8,128)(2,1)S(1)} %bitcast.14, bf16[8,128,1536]{2,1,0:T(8,128)(2,1)} %copy-done.2, bf16[768,768]{1,0:T(8,128)(2,1)S(1)} %copy-done.3), custom_call_target="tpu_custom_call" | custom-call | flops 2013265920 | bytes 7471104 | tf_op jit(solution)/shard_map/second/pallas_call | solution.py:424
  124.5 6.7 %all-to-all-start.2 = ((bf16[256,8,384]{2,1,0:T(8,128)(2,1)}), bf16[256,8,384]{2,1,0:T(8,128)(2,1)S(1)}, u32[]{:S(2)}, u32[]{:S(2)}) async-start(bf16[256,8,384]{2,1,0:T(8,128)(2,1)} %bitcast.17), calls=%async_computation.2 | async-start | bytes 3145728 | tf_op jit(solution)/shard_map/all_to_all | solution.py:445
  131.2 1.7 copy-done.5
  132.9 1.4 copy-done.22
  134.3 8.6 %near.1 = (bf16[8,32,768]{2,1,0:T(8,128)(2,1)S(1)}, bf16[8,32,768]{2,1,0:T(8,128)(2,1)S(1)}, bf16[8,32,768]{2,1,0:T(8,128)(2,1)S(1)}, bf16[8,32,768]{2,1,0:T(8,128)(2,1)S(1)}) custom-call(bf16[2,1024,384]{2,1,0:T(8,128)(2,1)S(1)} %bitcast.15, bf16[8,128,768]{2,1,0:T(8,128)(2,1)S(1)} %copy-done.22, bf16[768,1536]{1,0:T(8,128)(2,1)S(1)} %copy-done.5), custom_call_target="tpu_custom_call" | custom-call | flops 3221225472 | bytes 7077888 | tf_op jit(solution)/shard_map/near/pallas_call | solution.py:450
  145.1 28.1 %all-to-all-done.2 = bf16[256,8,384]{2,1,0:T(8,128)(2,1)S(1)} async-done(((bf16[256,8,384]{2,1,0:T(8,128)(2,1)}), bf16[256,8,384]{2,1,0:T(8,128)(2,1)S(1)}, u32[]{:S(2)}, u32[]{:S(2)}) %all-to-all-start.2) | async-done | bytes 1572896 | tf_op jit(solution)/shard_map/all_to_all | solution.py:445
  173.5 4.9 %sum.1 = bf16[2048,384]{1,0:T(8,128)(2,1)} custom-call(s32[2048,128]{1,0:T(8,128)S(1)} %broadcast_in_dim.2.ids_ref, bf16[2048,384]{1,0:T(8,128)(2,1)S(1)} %bitcast.16), custom_call_target="tpu_custom_call" | custom-call | flops 3221225472 | bytes 3145728 | tf_op jit(solution)/shard_map/sum/pallas_call | solution.py:475
  178.5 5.8 %all-to-all-start.3 = ((bf16[64,32,384]{2,1,0:T(8,128)(2,1)}), bf16[64,32,384]{2,1,0:T(8,128)(2,1)}, u32[]{:S(2)}, u32[]{:S(2)}) async-start(bf16[64,32,384]{2,1,0:T(8,128)(2,1)} %bitcast.18), calls=%async_computation.3 | async-start | bytes 3145728 | tf_op jit(solution)/shard_map/all_to_all | solution.py:486
  184.3 1.7 collective-permute-start.3
  187.4 7.5 %collective-permute-done.3.r1 = bf16[8,32,768]{2,1,0:T(8,128)(2,1)S(1)} collective-permute-done((bf16[8,32,768]{2,1,0:T(8,128)(2,1)S(1)}, bf16[8,32,768]{2,1,0:T(8,128)(2,1)S(1)}, u32[]{:S(2)}, u32[]{:S(2)}) %collective-permute-start.3) | collective-permute-done | bytes 393248 | tf_op jit(solution)/shard_map/ppermute | solution.py:473
  194.8 2.7 %collective-permute-done.4.r2 = bf16[8,32,768]{2,1,0:T(8,128)(2,1)S(1)} collective-permute-done((bf16[8,32,768]{2,1,0:T(8,128)(2,1)S(1)}, bf16[8,32,768]{2,1,0:T(8,128)(2,1)S(1)}, u32[]{:S(2)}, u32[]{:S(2)}) %collective-permute-start.4) | collective-permute-done | bytes 393248 | tf_op jit(solution)/shard_map/ppermute | solution.py:473
  197.5 9.6 %collective-permute-done.5.r3 = bf16[8,32,768]{2,1,0:T(8,128)(2,1)S(1)} collective-permute-done((bf16[8,32,768]{2,1,0:T(8,128)(2,1)S(1)}, bf16[8,32,768]{2,1,0:T(8,128)(2,1)S(1)}, u32[]{:S(2)}, u32[]{:S(2)}) %collective-permute-start.5) | collective-permute-done | bytes 393248 | tf_op jit(solution)/shard_map/ppermute | solution.py:473
  207.1 1.4 copy-done.1
  208.5 1.8 base.1.base_ref
  210.3 12.9 %all-to-all-done.3.far_ref = bf16[64,32,384]{2,1,0:T(8,128)(2,1)} async-done(((bf16[64,32,384]{2,1,0:T(8,128)(2,1)}), bf16[64,32,384]{2,1,0:T(8,128)(2,1)}, u32[]{:S(2)}, u32[]{:S(2)}) %all-to-all-start.3) | async-done | bytes 1572896 | tf_op jit(solution)/shard_map/all_to_all | solution.py:486
  223.2 3.1 %join.1 = bf16[32,32,768]{2,1,0:T(8,128)(2,1)} custom-call(f32[32]{0:T(128)S(1)} %maximum_divide_fusion.recip_ref, bf16[64,32,384]{2,1,0:T(8,128)(2,1)} %all-to-all-done.3.far_ref, f32[32,32,768]{2,1,0:T(8,128)S(1)} %base.1.base_ref), custom_call_target="tpu_custom_call" | custom-call | flops 3145728 | bytes 6291456 | tf_op jit(solution)/shard_map/join/pallas_call | solution.py:499
  (54 shorter events, 10.6 us)
Async XLA Ops:
  6.5 13.3 %copy-start.23 = (s32[32,2]{0,1:T(2,128)S(1)}, s32[32,2]{0,1:T(2,128)}, u32[]{:S(2)}) copy-start(s32[32,2]{0,1:T(2,128)} %param.11) | copy-start | bytes 772
  6.5 13.3 %copy-start = (bf16[1024,768]{1,0:T(8,128)(2,1)S(1)}, bf16[1024,768]{1,0:T(8,128)(2,1)}, u32[]{:S(2)}) copy-start(bf16[1024,768]{1,0:T(8,128)(2,1)} %get-tuple-element.31.normed_ref) | copy-start | bytes 4718596
  6.6 54.9 %all-to-all-start = ((bf16[64,104,128]{2,1,0:T(8,128)(2,1)}), bf16[64,104,128]{2,1,0:T(8,128)(2,1)S(1)}, u32[]{:S(2)}, u32[]{:S(2)}) async-start(bf16[64,104,128]{2,1,0:T(8,128)(2,1)} %get-tuple-element.30), calls=%async_computation | async-start | bytes 3407872 | tf_op jit(solution)/shard_map/all_to_all | solution.py:363
  21.3 11.4 %collective-permute-start = (bf16[8,32,768]{2,1,0:T(8,128)(2,1)S(1)}, bf16[8,32,768]{2,1,0:T(8,128)(2,1)S(1)}, u32[]{:S(2)}, u32[]{:S(2)}) collective-permute-start(bf16[8,32,768]{2,1,0:T(8,128)(2,1)S(1)} %get-tuple-element.33), channel_id=1, source_target_pairs={{0,1},{1,2},{2,3},{3,0},{4,5},{5,6},{6,7},{7,4},{8,9},{9,10},{10,1... | collective-permute-start | bytes 1179656 | tf_op jit(solution)/shard_map/ppermute | solution.py:377
  22.5 19.6 %collective-permute-start.1 = (bf16[8,32,768]{2,1,0:T(8,128)(2,1)S(1)}, bf16[8,32,768]{2,1,0:T(8,128)(2,1)S(1)}, u32[]{:S(2)}, u32[]{:S(2)}) collective-permute-start(bf16[8,32,768]{2,1,0:T(8,128)(2,1)S(1)} %get-tuple-element.34), channel_id=1, source_target_pairs={{0,2},{1,3},{2,0},{3,1},{4,6},{5,7},{6,4},{7,5},{8,10},{9,11},{10,... | collective-permute-start | bytes 1179656 | tf_op jit(solution)/shard_map/ppermute | solution.py:377
  25.0 17.9 %collective-permute-start.2 = (bf16[8,32,768]{2,1,0:T(8,128)(2,1)S(1)}, bf16[8,32,768]{2,1,0:T(8,128)(2,1)S(1)}, u32[]{:S(2)}, u32[]{:S(2)}) collective-permute-start(bf16[8,32,768]{2,1,0:T(8,128)(2,1)S(1)} %get-tuple-element.35), channel_id=1, source_target_pairs={{0,3},{1,0},{2,1},{3,2},{4,7},{5,4},{6,5},{7,6},{8,11},{9,8},{10,9... | collective-permute-start | bytes 1179656 | tf_op jit(solution)/shard_map/ppermute | solution.py:377
  32.8 0.8 copy-start.15
  42.9 0.8 copy-start.19
  66.1 9.2 %copy-start.12 = (bf16[8,32,768]{2,1,0:T(8,128)(2,1)S(1)}, bf16[8,32,768]{2,1,0:T(8,128)(2,1)}, u32[]{:S(2)}) copy-start(bf16[8,32,768]{2,1,0:T(8,128)(2,1)} %copy-done.11) | copy-start | bytes 1179652
  66.1 51.2 %all-to-all-start.1 = ((bf16[256,8,384]{2,1,0:T(8,128)(2,1)}), bf16[256,8,384]{2,1,0:T(8,128)(2,1)S(1)}, u32[]{:S(2)}, u32[]{:S(2)}) async-start(bf16[256,8,384]{2,1,0:T(8,128)(2,1)} %bitcast.19), calls=%async_computation.1 | async-start | bytes 3145728 | tf_op jit(solution)/shard_map/all_to_all | solution.py:399
  75.3 1.7 copy-start.4
  77.0 1.3 copy-start.6
  78.3 1.0 copy-start.16
  79.3 1.0 copy-start.18
  80.3 1.0 copy-start.20
  81.2 36.1 %copy-start.3 = (bf16[768,768]{1,0:T(8,128)(2,1)S(1)}, bf16[768,768]{1,0:T(8,128)(2,1)}, u32[]{:S(2)}) copy-start(bf16[768,768]{1,0:T(8,128)(2,1)} %wq_ref.3) | copy-start | bytes 3538948
  85.1 1.6 copy-start.2
  86.7 1.2 copy-start.21
  124.5 48.7 %all-to-all-start.2 = ((bf16[256,8,384]{2,1,0:T(8,128)(2,1)}), bf16[256,8,384]{2,1,0:T(8,128)(2,1)S(1)}, u32[]{:S(2)}, u32[]{:S(2)}) async-start(bf16[256,8,384]{2,1,0:T(8,128)(2,1)} %bitcast.17), calls=%async_computation.2 | async-start | bytes 3145728 | tf_op jit(solution)/shard_map/all_to_all | solution.py:445
  131.2 1.7 copy-start.5
  132.9 1.4 copy-start.22
  142.8 0.8 copy-start.7
  144.4 0.7 copy-start.13
  178.4 5.8 %copy-start.24 = (s32[32,2]{0,1:T(2,128)S(1)}, s32[32,2]{0,1:T(2,128)}, u32[]{:S(2)}) copy-start(s32[32,2]{0,1:T(2,128)} %param.11) | copy-start | bytes 772
  178.4 5.8 %copy-start.14 = (bf16[8,32,768]{2,1,0:T(8,128)(2,1)S(1)}, bf16[8,32,768]{2,1,0:T(8,128)(2,1)}, u32[]{:S(2)}) copy-start(bf16[8,32,768]{2,1,0:T(8,128)(2,1)} %copy-done.13) | copy-start | bytes 1179652
  178.4 7.6 %copy-start.10 = (bf16[8,32,768]{2,1,0:T(8,128)(2,1)S(1)}, bf16[8,32,768]{2,1,0:T(8,128)(2,1)}, u32[]{:S(2)}) copy-start(bf16[8,32,768]{2,1,0:T(8,128)(2,1)} %copy-done.9) | copy-start | bytes 1179652
  178.4 8.2 %copy-start.8 = (bf16[8,32,768]{2,1,0:T(8,128)(2,1)S(1)}, bf16[8,32,768]{2,1,0:T(8,128)(2,1)}, u32[]{:S(2)}) copy-start(bf16[8,32,768]{2,1,0:T(8,128)(2,1)} %copy-done.7) | copy-start | bytes 1179652
  178.5 44.7 %all-to-all-start.3 = ((bf16[64,32,384]{2,1,0:T(8,128)(2,1)}), bf16[64,32,384]{2,1,0:T(8,128)(2,1)}, u32[]{:S(2)}, u32[]{:S(2)}) async-start(bf16[64,32,384]{2,1,0:T(8,128)(2,1)} %bitcast.18), calls=%async_computation.3 | async-start | bytes 3145728 | tf_op jit(solution)/shard_map/all_to_all | solution.py:486
  184.3 10.6 %collective-permute-start.3 = (bf16[8,32,768]{2,1,0:T(8,128)(2,1)S(1)}, bf16[8,32,768]{2,1,0:T(8,128)(2,1)S(1)}, u32[]{:S(2)}, u32[]{:S(2)}) collective-permute-start(bf16[8,32,768]{2,1,0:T(8,128)(2,1)S(1)} %copy-done.14), channel_id=1, source_target_pairs={{0,3},{1,0},{2,1},{3,2},{4,7},{5,4},{6,5},{7,6},{8,11},{9,8},{10,9... | collective-permute-start | bytes 1179656 | tf_op jit(solution)/shard_map/ppermute | solution.py:473
  186.0 11.5 %collective-permute-start.4 = (bf16[8,32,768]{2,1,0:T(8,128)(2,1)S(1)}, bf16[8,32,768]{2,1,0:T(8,128)(2,1)S(1)}, u32[]{:S(2)}, u32[]{:S(2)}) collective-permute-start(bf16[8,32,768]{2,1,0:T(8,128)(2,1)S(1)} %copy-done.10), channel_id=1, source_target_pairs={{0,2},{1,3},{2,0},{3,1},{4,6},{5,7},{6,4},{7,5},{8,10},{9,11},{10,... | collective-permute-start | bytes 1179656 | tf_op jit(solution)/shard_map/ppermute | solution.py:473
  186.7 20.4 %collective-permute-start.5 = (bf16[8,32,768]{2,1,0:T(8,128)(2,1)S(1)}, bf16[8,32,768]{2,1,0:T(8,128)(2,1)S(1)}, u32[]{:S(2)}, u32[]{:S(2)}) collective-permute-start(bf16[8,32,768]{2,1,0:T(8,128)(2,1)S(1)} %copy-done.8), channel_id=1, source_target_pairs={{0,1},{1,2},{2,3},{3,0},{4,5},{5,6},{6,7},{7,4},{8,9},{9,10},{10,1... | collective-permute-start | bytes 1179656 | tf_op jit(solution)/shard_map/ppermute | solution.py:473
  207.1 1.4 copy-start.1
  (3 other events, 2.2 us)

commit v6 on v5

--- a/solution.py
+++ b/solution.py
@@ -331,7 +331,7 @@
 
     first_local = pairs[:, 0] - img * images
     part = jax.ShapeDtypeStruct((items, toks, width), BF16)
-    block = 256
+    block = 512
     height = images * half // 128 + 8
     anywhere = pl.BlockSpec(memory_space=pl.ANY)
     normed, pieces = call(

time: 227 us -> 227 us (level)
  no operation moved by 1% of the time
where the time goes in v6:
time: 227 us; the launch traced here: 226 us
  waiting for transfers between devices  123 us (54%)
  starting transfers between devices  42.4 us (19%)
  Pallas kernels  40.7 us (18%)
  local copies, waits for them, and re-layouts  18.8 us (8%)
    all_to_all x1, waiting for transfers between devices, body(): lax.all_to_all(asked.reshape(owners * groups, items, half), ('img', 'tok'...  29.4 us
    all_to_all x1, waiting for transfers between devices, body(): lax.all_to_all(back.reshape(owners * groups, items, half), ('img', 'tok')...  28.1 us
    ppermute x3, waiting for transfers between devices, body(): near[k] = lax.ppermute(near[k], 'tok', perm)  19.7 us
    unnamed x50, local copies, waits for them, and re-layouts  18.5 us
    all_to_all x1, waiting for transfers between devices, body(): lax.all_to_all(pieces, 'img', split_axis=0, concat_axis=0, tiled=True)  17.8 us
    ppermute x3, waiting for transfers between devices, body(): firsts[k] = lax.ppermute(firsts[k], 'tok', perm)  15.3 us
    all_to_all x1, starting transfers between devices, body(): lax.all_to_all(pieces, 'img', split_axis=0, concat_axis=0, tiled=True)  13.3 us
    all_to_all x1, waiting for transfers between devices, body(): lax.all_to_all(sums.reshape(owners, images, half), 'img', split_axis=0, c...  12.9 us
  transfers between devices with their start and end apart: 10, of which 9 were waited for; matrix products, arithmetic and copies ran while one was open for 0% of the time, Pallas kernels for 7%

profile of v6, /device:TPU:1, one launch (start us, length us, event | category | flops | bytes accessed | tf_op | source)
XLA Modules:
  0.0 226.0 jit_solution(2699745876164828778)
XLA Ops:
  0.0 6.2 %embed.1 = (bf16[1024,768]{1,0:T(8,128)(2,1)}, bf16[64,104,128]{2,1,0:T(8,128)(2,1)}) custom-call(s32[1]{0:T(128)} %bitcast.img_ref, bf16[1024,1024]{1,0:T(8,128)(2,1)} %bitcast.23, bf16[1024,768]{1,0:T(8,128)(2,1)} %w_hbm.1, f32[768]{0:T(1024)} %gain_hbm.1, s32[2,32]{1,0:T(2,128)} %bitcast.22), custom_call_target="tpu_custom_call" | custom-call | flops 1610612736 | bytes 6815744 | tf_op jit(solution)/shard_map/embed/pallas_call | solution.py:337
  6.2 13.3 %all-to-all-start = ((bf16[64,104,128]{2,1,0:T(8,128)(2,1)}), bf16[64,104,128]{2,1,0:T(8,128)(2,1)S(1)}, u32[]{:S(2)}, u32[]{:S(2)}) async-start(bf16[64,104,128]{2,1,0:T(8,128)(2,1)} %get-tuple-element.30), calls=%async_computation | async-start | bytes 3407872 | tf_op jit(solution)/shard_map/all_to_all | solution.py:363
  20.9 1.2 collective-permute-start
  22.2 2.5 %collective-permute-start.1 = (bf16[8,32,768]{2,1,0:T(8,128)(2,1)S(1)}, bf16[8,32,768]{2,1,0:T(8,128)(2,1)S(1)}, u32[]{:S(2)}, u32[]{:S(2)}) collective-permute-start(bf16[8,32,768]{2,1,0:T(8,128)(2,1)S(1)} %get-tuple-element.34), channel_id=1, source_target_pairs={{0,2},{1,3},{2,0},{3,1},{4,6},{5,7},{6,4},{7,5},{8,10},{9,11},{10,... | collective-permute-start | bytes 1179656 | tf_op jit(solution)/shard_map/ppermute | solution.py:377
  24.6 1.2 collective-permute-start.2
  25.8 6.6 %collective-permute-done.f1 = bf16[8,32,768]{2,1,0:T(8,128)(2,1)S(1)} collective-permute-done((bf16[8,32,768]{2,1,0:T(8,128)(2,1)S(1)}, bf16[8,32,768]{2,1,0:T(8,128)(2,1)S(1)}, u32[]{:S(2)}, u32[]{:S(2)}) %collective-permute-start) | collective-permute-done | bytes 393248 | tf_op jit(solution)/shard_map/ppermute | solution.py:377
  33.1 8.7 %collective-permute-done.1.f2 = bf16[8,32,768]{2,1,0:T(8,128)(2,1)S(1)} collective-permute-done((bf16[8,32,768]{2,1,0:T(8,128)(2,1)S(1)}, bf16[8,32,768]{2,1,0:T(8,128)(2,1)S(1)}, u32[]{:S(2)}, u32[]{:S(2)}) %collective-permute-start.1) | collective-permute-done | bytes 393248 | tf_op jit(solution)/shard_map/ppermute | solution.py:377
  43.3 17.8 %all-to-all-done.table_ref = bf16[64,104,128]{2,1,0:T(8,128)(2,1)S(1)} async-done(((bf16[64,104,128]{2,1,0:T(8,128)(2,1)}), bf16[64,104,128]{2,1,0:T(8,128)(2,1)S(1)}, u32[]{:S(2)}, u32[]{:S(2)}) %all-to-all-start) | async-done | bytes 1703968 | tf_op jit(solution)/shard_map/all_to_all | solution.py:363
  61.1 4.7 %pick.1 = (bf16[2048,384]{1,0:T(8,128)(2,1)}, f32[16,1,128]{2,1,0:T(1,128)S(1)}) custom-call(bf16[64,104,128]{2,1,0:T(8,128)(2,1)S(1)} %all-to-all-done.table_ref), custom_call_target="tpu_custom_call" | custom-call | flops 3221225472 | bytes 3145728 | tf_op jit(solution)/shard_map/pick/pallas_call | solution.py:381
  65.8 9.2 %all-to-all-start.1 = ((bf16[256,8,384]{2,1,0:T(8,128)(2,1)}), bf16[256,8,384]{2,1,0:T(8,128)(2,1)S(1)}, u32[]{:S(2)}, u32[]{:S(2)}) async-start(bf16[256,8,384]{2,1,0:T(8,128)(2,1)} %bitcast.19), calls=%async_computation.1 | async-start | bytes 3145728 | tf_op jit(solution)/shard_map/all_to_all | solution.py:399
  75.0 1.7 copy-done.4
  76.6 1.3 copy-done.6
  80.9 3.8 %first.1 = (bf16[8,128,768]{2,1,0:T(8,128)(2,1)S(1)}, bf16[8,128,1536]{2,1,0:T(8,128)(2,1)S(1)}) custom-call(bf16[8,32,768]{2,1,0:T(8,128)(2,1)S(1)} %copy-done.12, bf16[8,32,768]{2,1,0:T(8,128)(2,1)S(1)} %copy-done.16, bf16[8,32,768]{2,1,0:T(8,128)(2,1)S(1)} %copy-done.18, bf16[8,32,768]{2,1,0:T(8,128)(2,1)S(1)} %copy-done.20, ...), custom_call_target="tpu_custom_call" | custom-call | flops 3623878656 | bytes 9830400 | tf_op jit(solution)/shard_map/first/pallas_call | solution.py:405
  84.7 1.6 copy-done.2
  86.4 1.2 copy-done.21
  87.6 29.4 %all-to-all-done.1 = bf16[256,8,384]{2,1,0:T(8,128)(2,1)S(1)} async-done(((bf16[256,8,384]{2,1,0:T(8,128)(2,1)}), bf16[256,8,384]{2,1,0:T(8,128)(2,1)S(1)}, u32[]{:S(2)}, u32[]{:S(2)}) %all-to-all-start.1) | async-done | bytes 1572896 | tf_op jit(solution)/shard_map/all_to_all | solution.py:399
  117.0 7.1 %second.1 = bf16[2,1024,384]{2,1,0:T(8,128)(2,1)} custom-call(bf16[2,1024,384]{2,1,0:T(8,128)(2,1)S(1)} %bitcast.14, bf16[8,128,1536]{2,1,0:T(8,128)(2,1)} %copy-done.2, bf16[768,768]{1,0:T(8,128)(2,1)S(1)} %copy-done.3), custom_call_target="tpu_custom_call" | custom-call | flops 2013265920 | bytes 7471104 | tf_op jit(solution)/shard_map/second/pallas_call | solution.py:424
  124.1 6.7 %all-to-all-start.2 = ((bf16[256,8,384]{2,1,0:T(8,128)(2,1)}), bf16[256,8,384]{2,1,0:T(8,128)(2,1)S(1)}, u32[]{:S(2)}, u32[]{:S(2)}) async-start(bf16[256,8,384]{2,1,0:T(8,128)(2,1)} %bitcast.17), calls=%async_computation.2 | async-start | bytes 3145728 | tf_op jit(solution)/shard_map/all_to_all | solution.py:445
  130.8 1.7 copy-done.5
  132.5 1.4 copy-done.22
  133.9 8.6 %near.1 = (bf16[8,32,768]{2,1,0:T(8,128)(2,1)S(1)}, bf16[8,32,768]{2,1,0:T(8,128)(2,1)S(1)}, bf16[8,32,768]{2,1,0:T(8,128)(2,1)S(1)}, bf16[8,32,768]{2,1,0:T(8,128)(2,1)S(1)}) custom-call(bf16[2,1024,384]{2,1,0:T(8,128)(2,1)S(1)} %bitcast.15, bf16[8,128,768]{2,1,0:T(8,128)(2,1)S(1)} %copy-done.22, bf16[768,1536]{1,0:T(8,128)(2,1)S(1)} %copy-done.5), custom_call_target="tpu_custom_call" | custom-call | flops 3221225472 | bytes 7077888 | tf_op jit(solution)/shard_map/near/pallas_call | solution.py:450
  144.7 28.1 %all-to-all-done.2 = bf16[256,8,384]{2,1,0:T(8,128)(2,1)S(1)} async-done(((bf16[256,8,384]{2,1,0:T(8,128)(2,1)}), bf16[256,8,384]{2,1,0:T(8,128)(2,1)S(1)}, u32[]{:S(2)}, u32[]{:S(2)}) %all-to-all-start.2) | async-done | bytes 1572896 | tf_op jit(solution)/shard_map/all_to_all | solution.py:445
  173.2 4.9 %sum.1 = bf16[2048,384]{1,0:T(8,128)(2,1)} custom-call(s32[2048,128]{1,0:T(8,128)S(1)} %broadcast_in_dim.2.ids_ref, bf16[2048,384]{1,0:T(8,128)(2,1)S(1)} %bitcast.16), custom_call_target="tpu_custom_call" | custom-call | flops 3221225472 | bytes 3145728 | tf_op jit(solution)/shard_map/sum/pallas_call | solution.py:475
  178.1 5.8 %all-to-all-start.3 = ((bf16[64,32,384]{2,1,0:T(8,128)(2,1)}), bf16[64,32,384]{2,1,0:T(8,128)(2,1)}, u32[]{:S(2)}, u32[]{:S(2)}) async-start(bf16[64,32,384]{2,1,0:T(8,128)(2,1)} %bitcast.18), calls=%async_computation.3 | async-start | bytes 3145728 | tf_op jit(solution)/shard_map/all_to_all | solution.py:486
  183.9 1.7 collective-permute-start.3
  187.0 7.4 %collective-permute-done.3.r1 = bf16[8,32,768]{2,1,0:T(8,128)(2,1)S(1)} collective-permute-done((bf16[8,32,768]{2,1,0:T(8,128)(2,1)S(1)}, bf16[8,32,768]{2,1,0:T(8,128)(2,1)S(1)}, u32[]{:S(2)}, u32[]{:S(2)}) %collective-permute-start.3) | collective-permute-done | bytes 393248 | tf_op jit(solution)/shard_map/ppermute | solution.py:473
  194.5 2.7 %collective-permute-done.4.r2 = bf16[8,32,768]{2,1,0:T(8,128)(2,1)S(1)} collective-permute-done((bf16[8,32,768]{2,1,0:T(8,128)(2,1)S(1)}, bf16[8,32,768]{2,1,0:T(8,128)(2,1)S(1)}, u32[]{:S(2)}, u32[]{:S(2)}) %collective-permute-start.4) | collective-permute-done | bytes 393248 | tf_op jit(solution)/shard_map/ppermute | solution.py:473
  197.1 9.6 %collective-permute-done.5.r3 = bf16[8,32,768]{2,1,0:T(8,128)(2,1)S(1)} collective-permute-done((bf16[8,32,768]{2,1,0:T(8,128)(2,1)S(1)}, bf16[8,32,768]{2,1,0:T(8,128)(2,1)S(1)}, u32[]{:S(2)}, u32[]{:S(2)}) %collective-permute-start.5) | collective-permute-done | bytes 393248 | tf_op jit(solution)/shard_map/ppermute | solution.py:473
  206.7 1.4 copy-done.1
  208.1 1.8 base.1.base_ref
  209.9 12.9 %all-to-all-done.3.far_ref = bf16[64,32,384]{2,1,0:T(8,128)(2,1)} async-done(((bf16[64,32,384]{2,1,0:T(8,128)(2,1)}), bf16[64,32,384]{2,1,0:T(8,128)(2,1)}, u32[]{:S(2)}, u32[]{:S(2)}) %all-to-all-start.3) | async-done | bytes 1572896 | tf_op jit(solution)/shard_map/all_to_all | solution.py:486
  222.8 3.1 %join.1 = bf16[32,32,768]{2,1,0:T(8,128)(2,1)} custom-call(f32[32]{0:T(128)S(1)} %maximum_divide_fusion.recip_ref, bf16[64,32,384]{2,1,0:T(8,128)(2,1)} %all-to-all-done.3.far_ref, f32[32,32,768]{2,1,0:T(8,128)S(1)} %base.1.base_ref), custom_call_target="tpu_custom_call" | custom-call | flops 3145728 | bytes 6291456 | tf_op jit(solution)/shard_map/join/pallas_call | solution.py:499
  (54 shorter events, 10.6 us)
Async XLA Ops:
  6.2 13.3 %copy-start.23 = (s32[32,2]{0,1:T(2,128)S(1)}, s32[32,2]{0,1:T(2,128)}, u32[]{:S(2)}) copy-start(s32[32,2]{0,1:T(2,128)} %param.11) | copy-start | bytes 772
  6.2 13.3 %copy-start = (bf16[1024,768]{1,0:T(8,128)(2,1)S(1)}, bf16[1024,768]{1,0:T(8,128)(2,1)}, u32[]{:S(2)}) copy-start(bf16[1024,768]{1,0:T(8,128)(2,1)} %get-tuple-element.31.normed_ref) | copy-start | bytes 4718596
  6.2 54.9 %all-to-all-start = ((bf16[64,104,128]{2,1,0:T(8,128)(2,1)}), bf16[64,104,128]{2,1,0:T(8,128)(2,1)S(1)}, u32[]{:S(2)}, u32[]{:S(2)}) async-start(bf16[64,104,128]{2,1,0:T(8,128)(2,1)} %get-tuple-element.30), calls=%async_computation | async-start | bytes 3407872 | tf_op jit(solution)/shard_map/all_to_all | solution.py:363
  20.9 11.4 %collective-permute-start = (bf16[8,32,768]{2,1,0:T(8,128)(2,1)S(1)}, bf16[8,32,768]{2,1,0:T(8,128)(2,1)S(1)}, u32[]{:S(2)}, u32[]{:S(2)}) collective-permute-start(bf16[8,32,768]{2,1,0:T(8,128)(2,1)S(1)} %get-tuple-element.33), channel_id=1, source_target_pairs={{0,1},{1,2},{2,3},{3,0},{4,5},{5,6},{6,7},{7,4},{8,9},{9,10},{10,1... | collective-permute-start | bytes 1179656 | tf_op jit(solution)/shard_map/ppermute | solution.py:377
  22.2 19.6 %collective-permute-start.1 = (bf16[8,32,768]{2,1,0:T(8,128)(2,1)S(1)}, bf16[8,32,768]{2,1,0:T(8,128)(2,1)S(1)}, u32[]{:S(2)}, u32[]{:S(2)}) collective-permute-start(bf16[8,32,768]{2,1,0:T(8,128)(2,1)S(1)} %get-tuple-element.34), channel_id=1, source_target_pairs={{0,2},{1,3},{2,0},{3,1},{4,6},{5,7},{6,4},{7,5},{8,10},{9,11},{10,... | collective-permute-start | bytes 1179656 | tf_op jit(solution)/shard_map/ppermute | solution.py:377
  24.6 17.9 %collective-permute-start.2 = (bf16[8,32,768]{2,1,0:T(8,128)(2,1)S(1)}, bf16[8,32,768]{2,1,0:T(8,128)(2,1)S(1)}, u32[]{:S(2)}, u32[]{:S(2)}) collective-permute-start(bf16[8,32,768]{2,1,0:T(8,128)(2,1)S(1)} %get-tuple-element.35), channel_id=1, source_target_pairs={{0,3},{1,0},{2,1},{3,2},{4,7},{5,4},{6,5},{7,6},{8,11},{9,8},{10,9... | collective-permute-start | bytes 1179656 | tf_op jit(solution)/shard_map/ppermute | solution.py:377
  32.4 0.8 copy-start.15
  42.6 0.8 copy-start.19
  65.8 9.2 %copy-start.12 = (bf16[8,32,768]{2,1,0:T(8,128)(2,1)S(1)}, bf16[8,32,768]{2,1,0:T(8,128)(2,1)}, u32[]{:S(2)}) copy-start(bf16[8,32,768]{2,1,0:T(8,128)(2,1)} %copy-done.11) | copy-start | bytes 1179652
  65.8 51.2 %all-to-all-start.1 = ((bf16[256,8,384]{2,1,0:T(8,128)(2,1)}), bf16[256,8,384]{2,1,0:T(8,128)(2,1)S(1)}, u32[]{:S(2)}, u32[]{:S(2)}) async-start(bf16[256,8,384]{2,1,0:T(8,128)(2,1)} %bitcast.19), calls=%async_computation.1 | async-start | bytes 3145728 | tf_op jit(solution)/shard_map/all_to_all | solution.py:399
  75.0 1.7 copy-start.4
  76.6 1.3 copy-start.6
  77.9 1.0 copy-start.16
  78.9 1.0 copy-start.18
  79.9 1.0 copy-start.20
  80.9 36.1 %copy-start.3 = (bf16[768,768]{1,0:T(8,128)(2,1)S(1)}, bf16[768,768]{1,0:T(8,128)(2,1)}, u32[]{:S(2)}) copy-start(bf16[768,768]{1,0:T(8,128)(2,1)} %wq_ref.3) | copy-start | bytes 3538948
  84.7 1.6 copy-start.2
  86.4 1.2 copy-start.21
  124.1 48.7 %all-to-all-start.2 = ((bf16[256,8,384]{2,1,0:T(8,128)(2,1)}), bf16[256,8,384]{2,1,0:T(8,128)(2,1)S(1)}, u32[]{:S(2)}, u32[]{:S(2)}) async-start(bf16[256,8,384]{2,1,0:T(8,128)(2,1)} %bitcast.17), calls=%async_computation.2 | async-start | bytes 3145728 | tf_op jit(solution)/shard_map/all_to_all | solution.py:445
  130.8 1.7 copy-start.5
  132.5 1.4 copy-start.22
  142.5 0.8 copy-start.7
  144.0 0.7 copy-start.13
  178.1 5.8 %copy-start.24 = (s32[32,2]{0,1:T(2,128)S(1)}, s32[32,2]{0,1:T(2,128)}, u32[]{:S(2)}) copy-start(s32[32,2]{0,1:T(2,128)} %param.11) | copy-start | bytes 772
  178.1 5.8 %copy-start.14 = (bf16[8,32,768]{2,1,0:T(8,128)(2,1)S(1)}, bf16[8,32,768]{2,1,0:T(8,128)(2,1)}, u32[]{:S(2)}) copy-start(bf16[8,32,768]{2,1,0:T(8,128)(2,1)} %copy-done.13) | copy-start | bytes 1179652
  178.1 7.6 %copy-start.10 = (bf16[8,32,768]{2,1,0:T(8,128)(2,1)S(1)}, bf16[8,32,768]{2,1,0:T(8,128)(2,1)}, u32[]{:S(2)}) copy-start(bf16[8,32,768]{2,1,0:T(8,128)(2,1)} %copy-done.9) | copy-start | bytes 1179652
  178.1 8.2 %copy-start.8 = (bf16[8,32,768]{2,1,0:T(8,128)(2,1)S(1)}, bf16[8,32,768]{2,1,0:T(8,128)(2,1)}, u32[]{:S(2)}) copy-start(bf16[8,32,768]{2,1,0:T(8,128)(2,1)} %copy-done.7) | copy-start | bytes 1179652
  178.1 44.7 %all-to-all-start.3 = ((bf16[64,32,384]{2,1,0:T(8,128)(2,1)}), bf16[64,32,384]{2,1,0:T(8,128)(2,1)}, u32[]{:S(2)}, u32[]{:S(2)}) async-start(bf16[64,32,384]{2,1,0:T(8,128)(2,1)} %bitcast.18), calls=%async_computation.3 | async-start | bytes 3145728 | tf_op jit(solution)/shard_map/all_to_all | solution.py:486
  183.9 10.6 %collective-permute-start.3 = (bf16[8,32,768]{2,1,0:T(8,128)(2,1)S(1)}, bf16[8,32,768]{2,1,0:T(8,128)(2,1)S(1)}, u32[]{:S(2)}, u32[]{:S(2)}) collective-permute-start(bf16[8,32,768]{2,1,0:T(8,128)(2,1)S(1)} %copy-done.14), channel_id=1, source_target_pairs={{0,3},{1,0},{2,1},{3,2},{4,7},{5,4},{6,5},{7,6},{8,11},{9,8},{10,9... | collective-permute-start | bytes 1179656 | tf_op jit(solution)/shard_map/ppermute | solution.py:473
  185.6 11.5 %collective-permute-start.4 = (bf16[8,32,768]{2,1,0:T(8,128)(2,1)S(1)}, bf16[8,32,768]{2,1,0:T(8,128)(2,1)S(1)}, u32[]{:S(2)}, u32[]{:S(2)}) collective-permute-start(bf16[8,32,768]{2,1,0:T(8,128)(2,1)S(1)} %copy-done.10), channel_id=1, source_target_pairs={{0,2},{1,3},{2,0},{3,1},{4,6},{5,7},{6,4},{7,5},{8,10},{9,11},{10,... | collective-permute-start | bytes 1179656 | tf_op jit(solution)/shard_map/ppermute | solution.py:473
  186.3 20.4 %collective-permute-start.5 = (bf16[8,32,768]{2,1,0:T(8,128)(2,1)S(1)}, bf16[8,32,768]{2,1,0:T(8,128)(2,1)S(1)}, u32[]{:S(2)}, u32[]{:S(2)}) collective-permute-start(bf16[8,32,768]{2,1,0:T(8,128)(2,1)S(1)} %copy-done.8), channel_id=1, source_target_pairs={{0,1},{1,2},{2,3},{3,0},{4,5},{5,6},{6,7},{7,4},{8,9},{9,10},{10,1... | collective-permute-start | bytes 1179656 | tf_op jit(solution)/shard_map/ppermute | solution.py:473
  206.7 1.4 copy-start.1
  (3 other events, 2.2 us)
